TPU v7x, 32 devices: a whole 2x2x4 slice. The times are simulated.
32 devices in a mesh: cam: 8 (over y, x, core), fsdp: 4 (over z).
Axes of the slice: x: 2, y: 2, z: 4, core: 2. Of those that a mesh axis runs over, the one named last changes fastest.
Arguments:
- queries: bfloat16 [4, 1280, 4096], P('fsdp', 'cam'), may hold values from -16 to 16
- keys: bfloat16 [4, 1280, 4096], P('fsdp', 'cam'), may hold values from -16 to 16
- values: bfloat16 [4, 1280, 4096], P('fsdp', 'cam'), may hold values from -6 to 6
- out_weight: bfloat16 [4096, 5120], P('fsdp'), may hold values from -0.09375 to 0.09375
- block_counts: int32 [4, 8], P('fsdp', 'cam'), may hold values from 1 to 5, as said below
- row_mask: int32 [4, 1280], P('fsdp', 'cam'), may hold values from 0 to 1, as said below
Outputs:
- projected: bfloat16 [4, 1280, 5120], P('fsdp', 'cam')
Inputs may be any that keep to these rules, and one draw needn't show every extreme that they name: `block_counts`: every view uses at least one block; in every clip one view uses all 5 blocks. `row_mask`: 0 or 1; the first two rows of every block are 1.
All inputs are finite; a program needn't handle non-finite values.
Results may differ from a plain program's by a relative error of at most 0.0057.
Values may be sent and summed in bfloat16 or wider, within the bound.
No kernel may reach another device: no remote copies, remote signals or barrier semaphores. Data moves between devices by JAX's collectives and lax.ppermute only.
A program may use at most 128 MiB of HBM per device.

v0:
```python
import math

import jax
import jax.numpy as jnp
from jax import lax
from jax.experimental import pallas as pl
from jax.experimental.pallas import tpu as pltpu
from jax.sharding import PartitionSpec as P

HEAD_DIM = 128
BLOCK = 32
SENTINEL = 32.0
LIMIT = 24.0
UNIT = 128


def params(mebibytes):
    return pltpu.CompilerParams(vmem_limit_bytes=mebibytes * 1024 * 1024)


def order(count):
    return sorted(range(1, count), key=lambda mask: (mask == 1, mask & 1, -bin(mask).count("1")))


def variants(total):
    return sorted({-(-total * tenths // (10 * UNIT)) * UNIT for tenths in (4, 5, 6, 8, 10)})


def full_spec(shape):
    return pl.BlockSpec(shape, lambda i, *_: (0,) * len(shape))


def column_of(row):
    n = row.shape[1]
    diagonal = lax.broadcasted_iota(jnp.int32, (n, n), 0) == lax.broadcasted_iota(
        jnp.int32, (n, n), 1
    )
    return jnp.sum(jnp.where(diagonal, row, 0.0), axis=1, keepdims=True)


def valid_column(mask_ref, blocks):
    rows = mask_ref.shape[1]
    inside = lax.broadcasted_iota(jnp.int32, (1, rows), 1) < blocks * BLOCK
    return column_of(jnp.where((mask_ref[...] == 1) & inside, 1.0, 0.0))


def xor_permute(array, mask, count):
    return lax.ppermute(array, "cam", [(place, place ^ mask) for place in range(count)])


def pack(place, block_counts, row_mask, queries, keys, values, out_weight, count):
    _, rows, features = queries.shape
    width = features // count
    depth = out_weight.shape[0]
    columns = out_weight.shape[1] // count
    slicing = columns % HEAD_DIM == 0
    chunks = 1 if slicing else 0
    staged = columns if slicing else HEAD_DIM

    def body(place_ref, blocks_ref, mask_ref, q_ref, k_ref, v_ref, w_ref, *refs):
        out_refs = refs[:count]
        weight_refs = refs[count : count + chunks]
        held, key_out, w_held, load_sems, sems, weight_sems = refs[count + chunks :]
        loads = []
        for slot, ref in enumerate((k_ref, q_ref, v_ref)):
            load = pltpu.make_async_copy(ref.at[0], held.at[slot], load_sems.at[slot])
            load.start()
            loads.append(load)
        if chunks:
            start = pl.multiple_of(place_ref[0] * columns, HEAD_DIM)
            load = pltpu.make_async_copy(
                w_ref.at[:, pl.ds(start, columns)], w_held, load_sems.at[3]
            )
            load.start()
            loads.append(load)
        starts = [pl.multiple_of((place_ref[0] ^ m) * width, HEAD_DIM) for m in range(count)]
        good = valid_column(mask_ref, blocks_ref[0, 0]) > 0.5
        copies = []

        def send(source, target, sem):
            copy = pltpu.make_async_copy(source, target, sem)
            copy.start()
            copies.append(copy)

        loads[0].wait()
        for mask in range(count):
            part = held[0, :, pl.ds(starts[mask], width)]
            key_out[mask] = jnp.where(good, part, jnp.bfloat16(SENTINEL))
            send(key_out.at[mask], out_refs[mask].at[1], sems.at[mask, 1])
        for slot, target in ((1, 0), (2, 2)):
            loads[slot].wait()
            for mask in range(count):
                source = held.at[slot, :, pl.ds(starts[mask], width)]
                send(source, out_refs[mask].at[target], sems.at[mask, target])
        if chunks:
            loads[3].wait()
            send(w_held, weight_refs[0], weight_sems.at[0])
        for copy in copies:
            copy.wait()

    any_spec = pl.BlockSpec(memory_space=pl.ANY)
    weight_shapes = [jax.ShapeDtypeStruct((depth, columns), jnp.bfloat16)] * chunks
    outputs = pl.pallas_call(
        body,
        grid_spec=pltpu.PrefetchScalarGridSpec(
            num_scalar_prefetch=2,
            grid=(1,),
            in_specs=[full_spec((1, rows))] + [any_spec] * 4,
            out_specs=[any_spec] * (count + chunks),
            scratch_shapes=[
                pltpu.VMEM((3, rows, features), jnp.bfloat16),
                pltpu.VMEM((count, rows, width), jnp.bfloat16),
                pltpu.VMEM((depth, staged), jnp.bfloat16),
                pltpu.SemaphoreType.DMA((4,)),
                pltpu.SemaphoreType.DMA((count, 3)),
                pltpu.SemaphoreType.DMA((1,)),
            ],
        ),
        out_shape=[jax.ShapeDtypeStruct((3, rows, width), jnp.bfloat16)] * count + weight_shapes,
        compiler_params=params(56),
        cost_estimate=pl.CostEstimate(
            flops=0, bytes_accessed=12 * rows * features, transcendentals=0
        ),
        name="pack",
    )(place, block_counts, row_mask, queries, keys, values, out_weight)
    if slicing:
        return list(outputs[:count]), outputs[count]
    start = place[0] * columns
    return list(outputs[:count]), lax.dynamic_slice_in_dim(out_weight, start, columns, axis=1)


def pass_weight(shards, distance):
    groups = lax.axis_size("fsdp")
    for sign in (1, -1):
        pairs = []
        for source in range(groups):
            origin, target = source - sign * (distance - 1), source + sign
            if 0 <= origin < groups and 0 <= target < groups:
                pairs.append((source, target))
        shards[sign * distance] = lax.ppermute(shards[sign * (distance - 1)], "fsdp", pairs)


def packed_offsets(place_ref, counts_ref, table, count):
    by_mask, running = [], 0
    for mask in range(count):
        by_mask.append(running)
        table[mask] = running
        running = running + counts_ref[mask] * BLOCK
    by_view, position = [], 0
    for view in range(count):
        by_view.append(position)
        position = position + counts_ref[place_ref[0] ^ view] * BLOCK
    return by_mask, by_view, running


def rows_at(start, size):
    return pl.ds(start if isinstance(start, int) else pl.multiple_of(start, BLOCK), size)


def tile_of(size):
    return max(rows for rows in range(UNIT, 6 * UNIT + 1, UNIT) if size % rows == 0)


def attend(place, received, rows, lengths):
    count = len(received)
    width = received[0].shape[2]
    total = count * rows
    span = 2 * HEAD_DIM
    factor = math.log2(math.e) / math.sqrt(HEAD_DIM)

    def body(place_ref, *refs):
        parts = refs[:count]
        out_refs = refs[count : count + len(lengths)]
        counts_ref, used_ref = refs[count + len(lengths) : count + len(lengths) + 2]
        query_all, key_all, value_all, result, ordered, table = refs[count + len(lengths) + 2 :]

        @pl.when(pl.program_id(0) == 0)
        def _():
            value_all[...] = jnp.zeros_like(value_all)
            for mask in range(count):
                blocks = jnp.zeros((1, HEAD_DIM), jnp.float32)
                for first in range(0, rows, BLOCK):
                    row = parts[mask][1, first : first + 16, :HEAD_DIM].astype(jnp.float32)[:1]
                    blocks = blocks + jnp.where(row < LIMIT, 1.0, 0.0)
                counts_ref[mask] = jnp.max(blocks).astype(jnp.int32)

        by_mask, by_view, used = packed_offsets(place_ref, counts_ref, table, count)
        used_ref[0] = used
        for mask in range(count):
            where = rows_at(by_mask[mask], rows)
            query_all[where, :] = parts[mask][0]
            key_all[where, :] = parts[mask][1]
            value_all[where, :] = parts[mask][2]
        key_all[rows_at(used, total // 5), :] = jnp.full((total // 5, span), SENTINEL, jnp.bfloat16)
        below = 0
        for size in variants(total):

            @pl.when((used > below) & (used <= size))
            def _(size=size):
                step = tile_of(size)
                key_mask = key_all[:size, :HEAD_DIM].astype(jnp.float32) > LIMIT
                bias = jnp.where(key_mask, jnp.float32(-1e30), 0.0)
                bias = jnp.concatenate([bias] * (step // HEAD_DIM), axis=1)
                values_t = [
                    value_all[:size, first : first + HEAD_DIM].T
                    for first in range(0, span, HEAD_DIM)
                ]

                def tile(index, carry):
                    if isinstance(index, int):
                        where = pl.ds(index * step, step)
                    else:
                        where = pl.ds(pl.multiple_of(index * step, UNIT), step)
                    for head in range(span // HEAD_DIM):
                        lanes = slice(head * HEAD_DIM, (head + 1) * HEAD_DIM)
                        scores = lax.dot_general(
                            key_all[:size, lanes],
                            query_all[where, lanes],
                            (((1,), (1,)), ((), ())),
                            preferred_element_type=jnp.float32,
                        )
                        scores = scores + bias
                        top = jnp.max(scores, axis=0, keepdims=True)
                        raised = jnp.exp2((scores - top) * factor)
                        norm = jnp.sum(raised, axis=0, keepdims=True)
                        summed = jnp.dot(
                            values_t[head],
                            raised.astype(jnp.bfloat16),
                            preferred_element_type=jnp.float32,
                        )
                        result[where, lanes] = (summed / norm).T.astype(jnp.bfloat16)
                    return carry

                if size == step:
                    tile(0, 0)
                else:
                    lax.fori_loop(0, size // step, tile, 0)

            below = size
        for view in range(count):
            moved = result[rows_at(table[place_ref[0] ^ view], rows), :]
            ordered[rows_at(by_view[view], rows), :] = moved
        first = 0
        for length, out_ref in zip(lengths, out_refs):
            out_ref[...] = ordered[first : first + length, :]
            first += length

    flops = 4 * total * total * width // 4
    return pl.pallas_call(
        body,
        grid_spec=pltpu.PrefetchScalarGridSpec(
            num_scalar_prefetch=1,
            grid=(width // span,),
            in_specs=[pl.BlockSpec((3, rows, span), lambda h, *_: (0, 0, h))] * count,
            out_specs=[pl.BlockSpec((length, span), lambda h, *_: (0, h)) for length in lengths]
            + [pl.BlockSpec(memory_space=pltpu.SMEM)] * 2,
            scratch_shapes=[
                pltpu.VMEM((total, span), jnp.bfloat16),
                pltpu.VMEM((total + total // 5, span), jnp.bfloat16),
                pltpu.VMEM((total, span), jnp.bfloat16),
                pltpu.VMEM((total, span), jnp.bfloat16),
                pltpu.VMEM((total, span), jnp.bfloat16),
                pltpu.SMEM((count,), jnp.int32),
            ],
        ),
        out_shape=[jax.ShapeDtypeStruct((length, width), jnp.bfloat16) for length in lengths]
        + [jax.ShapeDtypeStruct((count,), jnp.int32), jax.ShapeDtypeStruct((1,), jnp.int32)],
        compiler_params=params(40),
        cost_estimate=pl.CostEstimate(
            flops=flops, bytes_accessed=8 * total * width, transcendentals=flops // 512
        ),
        name="attend",
    )(place, pltpu.with_memory_space_constraint(received[0], pltpu.HBM), *received[1:])


def gather_features(own, count, between=lambda arrived: arrived):
    held = {0: list(own)}
    if count == 8:
        over_x_0 = xor_permute(held[0][0], 2, count)
        over_y_1 = xor_permute(held[0][1], 4, count)
        over_x_1 = xor_permute(held[0][1], 2, count)
        over_y_0 = xor_permute(held[0][0], 4, count)
        over_x_0, over_y_1 = between((over_x_0, over_y_1))
        diagonal_0 = xor_permute(over_x_0, 4, count)
        diagonal_1 = xor_permute(over_y_1, 2, count)
        held[2] = [over_x_0, over_x_1]
        held[4] = [over_y_0, over_y_1]
        held[6] = [diagonal_0, diagonal_1]
    else:
        for mask in range(2, count, 2):
            held[mask] = [xor_permute(piece, mask, count) for piece in held[0]]
        held[2] = list(between(tuple(held[2])))
    for mask in range(0, count, 2):
        held[mask + 1] = [xor_permute(piece, 1, count) for piece in held[mask]]
    return [held[mask] for mask in range(count)]


def unfilled(shape):
    def body(out_ref):
        pass

    return pl.pallas_call(
        body,
        out_specs=pl.BlockSpec(memory_space=pl.ANY),
        out_shape=shape,
        name="unfilled",
    )()


def project(place, group, counts, features, more, shards, rows):
    count = len(features)
    half, width = features[0][0].shape
    total = count * rows
    distances = sorted(shards)
    columns = shards[0].shape[1]
    each = shards[0].shape[0] // width
    bounds = [size for size in variants(total) if size <= 2 * half] + [total]

    def body(place_ref, group_ref, counts_ref, *refs):
        flat = refs[: 2 * count]
        more_ref = refs[2 * count]
        shard_refs = refs[2 * count + 1 : 2 * count + 1 + len(distances)]
        out_refs = refs[2 * count + 1 + len(distances) : 3 * count + 1 + len(distances)]
        landed, weight_all, sums, sems, weight_sems = refs[3 * count + 1 + len(distances) :]
        used = sum(counts_ref[mask] for mask in range(count)) * BLOCK

        for mask in range(count):
            owner = place_ref[0] ^ mask
            apart = group_ref[0] - owner // each
            start = pl.multiple_of((owner % each) * width, width)
            lower = mask % 2 * width
            for distance, shard_ref in zip(distances, shard_refs):

                @pl.when(apart == distance)
                def _(mask=mask, start=start, lower=lower, shard_ref=shard_ref):
                    pltpu.make_async_copy(
                        shard_ref.at[pl.ds(start, width), :],
                        weight_all.at[mask // 2, lower : lower + width, :],
                        weight_sems.at[mask // 2],
                    ).start()

        below = 0
        for size in bounds:

            @pl.when((used > below) & (used <= size))
            def _(size=size):
                for mask in range(count):
                    lanes = slice(mask % 2 * width, (mask % 2 + 1) * width)
                    sources = [flat[2 * mask], flat[2 * mask + 1]]
                    if size > 2 * half:
                        sources += [more_ref.at[2 * mask], more_ref.at[2 * mask + 1]]
                    first = 0
                    for source in sources:
                        length = min(source.shape[0], size - first)
                        pltpu.make_async_copy(
                            source.at[:length, :],
                            landed.at[mask // 2, first : first + length, lanes],
                            sems.at[mask // 2],
                        ).start()
                        first += length
                sums[:size, :] = jnp.zeros((size, columns), jnp.float32)

                def pair(index, carry):
                    for buffer, sem in (
                        (weight_all.at[index], weight_sems.at[index]),
                        (landed.at[index, :size, :], sems.at[index]),
                    ):
                        pltpu.make_async_copy(buffer, buffer, sem).wait()
                    sums[:size, :] += jnp.dot(
                        landed[index, :size, :],
                        weight_all[index],
                        preferred_element_type=jnp.float32,
                    )
                    return carry

                lax.fori_loop(0, count // 2, pair, 0)

            below = size
        for mask in range(count):
            position = 0
            for view in range(count):
                position = position + jnp.where(
                    view < (place_ref[0] ^ mask), counts_ref[place_ref[0] ^ view], 0
                )
            moved = sums[rows_at(position * BLOCK, rows), :]
            out_refs[mask][...] = moved.astype(jnp.bfloat16)

    any_spec = pl.BlockSpec(memory_space=pl.ANY)
    inputs = [piece for pair in features for piece in pair] + [more]
    inputs += [shards[distance] for distance in distances]
    inputs = [pltpu.with_memory_space_constraint(array, pltpu.HBM) for array in inputs]
    return pl.pallas_call(
        body,
        grid_spec=pltpu.PrefetchScalarGridSpec(
            num_scalar_prefetch=3,
            grid=(1,),
            in_specs=[any_spec] * len(inputs),
            out_specs=[full_spec((rows, columns))] * count,
            scratch_shapes=[
                pltpu.VMEM((count // 2, total, 2 * width), jnp.bfloat16),
                pltpu.VMEM((count // 2, 2 * width, columns), jnp.bfloat16),
                pltpu.VMEM((total, columns), jnp.float32),
                pltpu.SemaphoreType.DMA((count // 2,)),
                pltpu.SemaphoreType.DMA((count // 2,)),
            ],
        ),
        out_shape=[jax.ShapeDtypeStruct((rows, columns), jnp.bfloat16)] * count,
        compiler_params=params(56),
        cost_estimate=pl.CostEstimate(
            flops=total * count * width * columns,
            bytes_accessed=total * count * width,
            transcendentals=0,
        ),
        name="project",
    )(place, group, counts, *inputs)


def assemble(place, block_counts, row_mask, pieces, count):
    rows, columns = pieces[0].shape
    if columns % HEAD_DIM:
        stacked = jnp.stack(pieces)[jnp.arange(count) ^ place[0]]
        result = jnp.moveaxis(stacked, 0, 1).reshape(rows, count * columns)
        offsets = jnp.arange(rows, dtype=jnp.int32)
        good = (row_mask[0] == 1) & (offsets // BLOCK < block_counts[0, 0])
        return jnp.where(good[:, None], result, jnp.bfloat16(0.0))

    def body(place_ref, blocks_ref, mask_ref, *refs):
        out_ref = refs[-1]
        good = valid_column(mask_ref, blocks_ref[0, 0]) > 0.5
        for mask in range(count):
            start = pl.multiple_of((place_ref[0] ^ mask) * columns, HEAD_DIM)
            out_ref[:, pl.ds(start, columns)] = jnp.where(
                good, refs[mask][...], jnp.bfloat16(0.0)
            )

    return pl.pallas_call(
        body,
        grid_spec=pltpu.PrefetchScalarGridSpec(
            num_scalar_prefetch=2,
            grid=(1,),
            in_specs=[full_spec((1, rows))] + [full_spec((rows, columns))] * count,
            out_specs=full_spec((rows, count * columns)),
        ),
        out_shape=jax.ShapeDtypeStruct((rows, count * columns), jnp.bfloat16),
        compiler_params=params(16),
        cost_estimate=pl.CostEstimate(
            flops=0, bytes_accessed=4 * rows * count * columns, transcendentals=0
        ),
        name="assemble",
    )(
        place,
        block_counts,
        row_mask,
        pltpu.with_memory_space_constraint(pieces[0], pltpu.HBM),
        *pieces[1:],
    )


def local(queries, keys, values, out_weight, block_counts, row_mask):
    rows = queries.shape[1]
    count = lax.axis_size("cam")
    total = count * rows
    place_array = jnp.full((1,), lax.axis_index("cam"), jnp.int32)
    group_array = jnp.full((1,), lax.axis_index("fsdp"), jnp.int32)

    payloads, weight_part = pack(
        place_array, block_counts, row_mask, queries, keys, values, out_weight, count
    )
    shards = {0: weight_part}
    groups = lax.axis_size("fsdp")

    received = [payloads[0]] + [None] * (count - 1)
    early = [mask for mask in order(count) if mask & 1 == 0]
    late = [mask for mask in order(count) if mask & 1]
    pass_weight(shards, 1)
    for mask in early:
        received[mask] = xor_permute(payloads[mask], mask, count)
    received, payloads = lax.optimization_barrier((received, payloads))
    for mask in (late[0], 1):
        received[mask] = xor_permute(payloads[mask], mask, count)
    received, payloads, shards[1], shards[-1] = lax.optimization_barrier(
        (received, payloads, shards[1], shards[-1])
    )
    pass_weight(shards, 2)
    for mask in late[1:-1]:
        received[mask] = xor_permute(payloads[mask], mask, count)
    half = total * 3 // 10
    first, second, rest, counts, used = attend(
        place_array, received, rows, (half, half, total - 2 * half)
    )

    quarter = rest.shape[0] // 2
    shape = jax.ShapeDtypeStruct((2 * count, quarter, rest.shape[1]), rest.dtype)

    def gather_rest(part):
        pieces = gather_features((part[:quarter], part[quarter:]), count)
        return jnp.stack([piece for pair in pieces for piece in pair])

    def weight_step(arrived):
        arrived, shards[2], shards[-2] = lax.optimization_barrier((arrived, shards[2], shards[-2]))
        pass_weight(shards, 3)
        return arrived

    features = gather_features((first, second), count, weight_step)
    for distance in range(4, groups):
        pass_weight(shards, distance)
    rest, features, shards = lax.optimization_barrier((rest, features, shards))
    more = lax.cond(used[0] > 2 * half, gather_rest, lambda part: unfilled(shape), rest)
    pieces = project(place_array, group_array, counts, features, more, shards, rows)
    landed = [pieces[0]] + [None] * (count - 1)
    for mask in order(count):
        landed[mask] = xor_permute(pieces[mask], mask, count)
    return assemble(place_array, block_counts, row_mask, landed, count)[None]


def solution(mesh):
    in_specs = (
        P("fsdp", "cam", None),
        P("fsdp", "cam", None),
        P("fsdp", "cam", None),
        P("fsdp", None),
        P("fsdp", "cam"),
        P("fsdp", "cam"),
    )
    out_specs = P("fsdp", "cam", None)
    return jax.shard_map(local, mesh=mesh, in_specs=in_specs, out_specs=out_specs, check_vma=False)
```

profile of v0, /device:TPU:0, one launch (start us, length us, event | category | flops | bytes accessed | tf_op | source)
XLA Modules:
  0.0 159.0 jit_solution(112525681763450360)
XLA Ops:
  0.7 5.1 %pack.1 = (bf16[3,160,512]{2,1,0:T(8,128)(2,1)}, bf16[3,160,512]{2,1,0:T(8,128)(2,1)}, bf16[3,160,512]{2,1,0:T(8,128)(2,1)}, bf16[3,160,512]{2,1,0:T(8,128)(2,1)...) custom-call(s32[1]{0:T(128)} %bitcast.16.place_ref, ...), custom_call_target="tpu_custom_call" | custom-call | bytes 7864320 | tf_op jit(solution)/shard_map/pack/pallas_call | solution.py:103
  5.7 5.0 %collective-permute-start.19 = (bf16[1024,640]{1,0:T(8,128)(2,1)}, bf16[1024,640]{1,0:T(8,128)(2,1)S(1)}, u32[]{:S(2)}, u32[]{:S(2)}) collective-permute-start(bf16[1024,640]{1,0:T(8,128)(2,1)} %get-tuple-element.133.refs_20_), channel_id=1, source_target_pairs={{0,1},{1,2},{2,3},{4,5},{5,6},{6,7},{8,9},{9,10},{10,11},{12,13},{... | collective-permute-start | bytes 3932168 | tf_op jit(solution)/shard_map/ppermute | solution.py:140
  10.7 1.3 collective-permute-start.20
  12.0 1.6 collective-permute-start.14
  13.6 1.5 collective-permute-start.15
  15.1 0.5 collective-permute-start.16
  15.6 10.9 %collective-permute-done.14.refs_2_ = bf16[3,160,512]{2,1,0:T(8,128)(2,1)S(1)} collective-permute-done((bf16[3,160,512]{2,1,0:T(8,128)(2,1)}, bf16[3,160,512]{2,1,0:T(8,128)(2,1)S(1)}, u32[]{:S(2)}, u32[]{:S(2)}) %collective-permute-start.14) | collective-permute-done | bytes 491552 | tf_op jit(solution)/shard_map/ppermute | solution.py:48
  26.5 10.3 %collective-permute-done.15.refs_4_ = bf16[3,160,512]{2,1,0:T(8,128)(2,1)S(1)} collective-permute-done((bf16[3,160,512]{2,1,0:T(8,128)(2,1)}, bf16[3,160,512]{2,1,0:T(8,128)(2,1)S(1)}, u32[]{:S(2)}, u32[]{:S(2)}) %collective-permute-start.15) | collective-permute-done | bytes 491552 | tf_op jit(solution)/shard_map/ppermute | solution.py:48
  36.8 1.6 %collective-permute-start.18 = (bf16[3,160,512]{2,1,0:T(8,128)(2,1)}, bf16[3,160,512]{2,1,0:T(8,128)(2,1)S(1)}, u32[]{:S(2)}, u32[]{:S(2)}) collective-permute-start(bf16[3,160,512]{2,1,0:T(8,128)(2,1)} %get-tuple-element.90), channel_id=1, source_target_pairs={{0,28},{4,24},{8,20},{12,16},{16,12},{20,8},{24,4},{28,0},{1,29},{... | collective-permute-start | bytes 1474568 | tf_op jit(solution)/shard_map/ppermute | solution.py:48
  38.4 0.5 collective-permute-done.17.refs_1_
  38.8 11.9 %collective-permute-done.18.refs_7_ = bf16[3,160,512]{2,1,0:T(8,128)(2,1)S(1)} collective-permute-done((bf16[3,160,512]{2,1,0:T(8,128)(2,1)}, bf16[3,160,512]{2,1,0:T(8,128)(2,1)S(1)}, u32[]{:S(2)}, u32[]{:S(2)}) %collective-permute-start.18) | collective-permute-done | bytes 491552 | tf_op jit(solution)/shard_map/ppermute | solution.py:48
  50.8 1.9 %collective-permute-start.27 = (bf16[1024,640]{1,0:T(8,128)(2,1)S(1)}, bf16[1024,640]{1,0:T(8,128)(2,1)}, u32[]{:S(2)}, u32[]{:S(2)}) collective-permute-start(bf16[1024,640]{1,0:T(8,128)(2,1)S(1)} %collective-permute-done.19.refs_21_), channel_id=1, source_target_pairs={{1,2},{2,3},{5,6},{6,7},{9,10},{10,11},{13,14},{14,15},{17,18},{18... | collective-permute-start | bytes 3932168 | tf_op jit(solution)/shard_map/ppermute | solution.py:140
  52.7 1.3 collective-permute-start.28
  54.0 1.4 collective-permute-start.21
  55.3 0.5 collective-permute-start.22
  55.8 11.4 %collective-permute-done.21.refs_3_ = bf16[3,160,512]{2,1,0:T(8,128)(2,1)S(1)} collective-permute-done((bf16[3,160,512]{2,1,0:T(8,128)(2,1)}, bf16[3,160,512]{2,1,0:T(8,128)(2,1)S(1)}, u32[]{:S(2)}, u32[]{:S(2)}) %collective-permute-start.21) | collective-permute-done | bytes 491552 | tf_op jit(solution)/shard_map/ppermute | solution.py:48
  67.2 1.7 %collective-permute-done.22.refs_5_ = bf16[3,160,512]{2,1,0:T(8,128)(2,1)S(1)} collective-permute-done((bf16[3,160,512]{2,1,0:T(8,128)(2,1)}, bf16[3,160,512]{2,1,0:T(8,128)(2,1)S(1)}, u32[]{:S(2)}, u32[]{:S(2)}) %collective-permute-start.22) | collective-permute-done | bytes 491552 | tf_op jit(solution)/shard_map/ppermute | solution.py:48
  68.8 5.7 %attend.1 = (bf16[384,512]{1,0:T(8,128)(2,1)S(1)}, bf16[384,512]{1,0:T(8,128)(2,1)S(1)}, bf16[512,512]{1,0:T(8,128)(2,1)S(1)}, s32[8]{0:T(128)S(1)}, s32[1]{0:T(128)}) custom-call(s32[1]{0:T(128)} %bitcast.16.place_ref, bf16[3,160,512]{2,1,0:T(8,128)(2,1)} %get-tuple-element.94.refs_0_, bf16[3,160,512]{2,1,0:T(8,128)(2,1)S(1)} %collective-permute-done.17.refs_1_, ...), custom_call_target="tpu_custom_call" | custom-call | flops 838860800 | bytes 5242880 | tf_op jit(solution)/shard_map/attend/pallas_call | solution.py:249
  74.5 0.5 copy-done.3
  75.0 0.8 collective-permute-start.25
  75.8 1.5 collective-permute-start.26
  77.3 9.1 %collective-permute-done.25.refs_4_ = bf16[384,512]{1,0:T(8,128)(2,1)S(1)} collective-permute-done((bf16[384,512]{1,0:T(8,128)(2,1)S(1)}, bf16[384,512]{1,0:T(8,128)(2,1)S(1)}, u32[]{:S(2)}, u32[]{:S(2)}) %collective-permute-start.25) | collective-permute-done | bytes 393248 | tf_op jit(solution)/shard_map/ppermute | solution.py:48
  86.5 0.8 collective-permute-start.29
  87.3 1.5 collective-permute-start.32
  88.8 1.3 collective-permute-start.39
  90.1 1.8 %collective-permute-start.40 = (bf16[1024,640]{1,0:T(8,128)(2,1)}, bf16[1024,640]{1,0:T(8,128)(2,1)}, u32[]{:S(2)}, u32[]{:S(2)}) collective-permute-start(bf16[1024,640]{1,0:T(8,128)(2,1)} %collective-permute-done.27.refs_22_), channel_id=1, source_target_pairs={{2,3},{6,7},{10,11},{14,15},{18,19},{22,23},{26,27},{30,31}} | collective-permute-start | bytes 3932168 | tf_op jit(solution)/shard_map/ppermute | solution.py:140
  91.9 5.4 %collective-permute-done.29.refs_5_ = bf16[384,512]{1,0:T(8,128)(2,1)S(1)} collective-permute-done((bf16[384,512]{1,0:T(8,128)(2,1)S(1)}, bf16[384,512]{1,0:T(8,128)(2,1)S(1)}, u32[]{:S(2)}, u32[]{:S(2)}) %collective-permute-start.29) | collective-permute-done | bytes 393248 | tf_op jit(solution)/shard_map/ppermute | solution.py:48
  97.2 0.5 collective-permute-done.32.refs_8_
  97.8 0.6 collective-permute-start.30
  98.4 0.6 collective-permute-done.31.refs_7_
  99.0 0.9 collective-permute-start.35
  99.9 1.4 collective-permute-start.36
  101.3 8.9 %collective-permute-done.35.refs_12_ = bf16[384,512]{1,0:T(8,128)(2,1)} collective-permute-done((bf16[384,512]{1,0:T(8,128)(2,1)S(1)}, bf16[384,512]{1,0:T(8,128)(2,1)}, u32[]{:S(2)}, u32[]{:S(2)}) %collective-permute-start.35) | collective-permute-done | bytes 393248 | tf_op jit(solution)/shard_map/ppermute | solution.py:48
  110.2 0.6 collective-permute-done.36.refs_13_
  111.6 0.7 collective-permute-done.37.refs_14_
  112.3 0.6 collective-permute-done.38.refs_15_
  112.9 11.7 %collective-permute-done.39.refs_17_ = bf16[1024,640]{1,0:T(8,128)(2,1)} collective-permute-done((bf16[1024,640]{1,0:T(8,128)(2,1)}, bf16[1024,640]{1,0:T(8,128)(2,1)}, u32[]{:S(2)}, u32[]{:S(2)}) %collective-permute-start.39) | collective-permute-done | bytes 1310752 | tf_op jit(solution)/shard_map/ppermute | solution.py:140
  124.7 9.8 %project.1 = (bf16[160,640]{1,0:T(8,128)(2,1)}, bf16[160,640]{1,0:T(8,128)(2,1)}, bf16[160,640]{1,0:T(8,128)(2,1)}, bf16[160,640]{1,0:T(8,128)(2,1)}, bf16[160,6...) custom-call(s32[1]{0:T(128)} %bitcast.16.place_ref, ...), custom_call_target="tpu_custom_call" | custom-call | flops 3355443200 | bytes 5242880 | tf_op jit(solution)/shard_map/project/pallas_call | solution.py:392
  134.5 0.1 collective-permute-start.41
  134.6 0.6 collective-permute-start.42
  135.2 1.2 collective-permute-start.43
  136.4 0.5 collective-permute-start.44
  136.9 1.2 collective-permute-start.45
  138.1 1.2 collective-permute-start.46
  139.3 3.4 %collective-permute-done.42.refs_2_ = bf16[160,640]{1,0:T(8,128)(2,1)S(1)} collective-permute-done((bf16[160,640]{1,0:T(8,128)(2,1)}, bf16[160,640]{1,0:T(8,128)(2,1)S(1)}, u32[]{:S(2)}, u32[]{:S(2)}) %collective-permute-start.42) | collective-permute-done | bytes 204832 | tf_op jit(solution)/shard_map/ppermute | solution.py:48
  142.7 3.5 %collective-permute-done.43.refs_3_ = bf16[160,640]{1,0:T(8,128)(2,1)S(1)} collective-permute-done((bf16[160,640]{1,0:T(8,128)(2,1)}, bf16[160,640]{1,0:T(8,128)(2,1)S(1)}, u32[]{:S(2)}, u32[]{:S(2)}) %collective-permute-start.43) | collective-permute-done | bytes 204832 | tf_op jit(solution)/shard_map/ppermute | solution.py:48
  146.2 10.3 %collective-permute-done.45.refs_5_ = bf16[160,640]{1,0:T(8,128)(2,1)S(1)} collective-permute-done((bf16[160,640]{1,0:T(8,128)(2,1)}, bf16[160,640]{1,0:T(8,128)(2,1)S(1)}, u32[]{:S(2)}, u32[]{:S(2)}) %collective-permute-start.45) | collective-permute-done | bytes 204832 | tf_op jit(solution)/shard_map/ppermute | solution.py:48
  156.6 2.4 %assemble.1 = bf16[160,5120]{1,0:T(8,128)(2,1)} custom-call(s32[1]{0:T(128)} %bitcast.16.place_ref, s32[1,1]{1,0:T(1,128)S(6)} %copy.24.blocks_ref, s32[1,160]{1,0:T(1,128)S(1)} %copy-done.2, bf16[160,640]{1,0:T(8,128)(2,1)} %get-tuple-element.137.refs_0_, bf16[160,640]{1,0:T(8,128)(2,1)S(1)} %collective-permute-done.41.refs_1_, ...), custom_call_target="tpu_custom_call" | custom-call | bytes 3276800 | tf_op jit(solution)/shard_map/assemble/pallas_call | solution.py:436
  (56 shorter events, 0.1 us)
Async XLA Ops:
  5.7 45.0 %collective-permute-start.19 = (bf16[1024,640]{1,0:T(8,128)(2,1)}, bf16[1024,640]{1,0:T(8,128)(2,1)S(1)}, u32[]{:S(2)}, u32[]{:S(2)}) collective-permute-start(bf16[1024,640]{1,0:T(8,128)(2,1)} %get-tuple-element.133.refs_20_), channel_id=1, source_target_pairs={{0,1},{1,2},{2,3},{4,5},{5,6},{6,7},{8,9},{9,10},{10,11},{12,13},{... | collective-permute-start | bytes 3932168 | tf_op jit(solution)/shard_map/ppermute | solution.py:140
  10.7 40.0 %collective-permute-start.20 = (bf16[1024,640]{1,0:T(8,128)(2,1)}, bf16[1024,640]{1,0:T(8,128)(2,1)S(1)}, u32[]{:S(2)}, u32[]{:S(2)}) collective-permute-start(bf16[1024,640]{1,0:T(8,128)(2,1)} %get-tuple-element.133.refs_20_), channel_id=1, source_target_pairs={{1,0},{2,1},{3,2},{5,4},{6,5},{7,6},{9,8},{10,9},{11,10},{13,12},{... | collective-permute-start | bytes 3932168 | tf_op jit(solution)/shard_map/ppermute | solution.py:140
  12.0 14.4 %collective-permute-start.14 = (bf16[3,160,512]{2,1,0:T(8,128)(2,1)}, bf16[3,160,512]{2,1,0:T(8,128)(2,1)S(1)}, u32[]{:S(2)}, u32[]{:S(2)}) collective-permute-start(bf16[3,160,512]{2,1,0:T(8,128)(2,1)} %get-tuple-element.78), channel_id=1, source_target_pairs={{0,8},{4,12},{8,0},{12,4},{16,24},{20,28},{24,16},{28,20},{1,9},{5... | collective-permute-start | bytes 1474568 | tf_op jit(solution)/shard_map/ppermute | solution.py:48
  13.6 23.1 %collective-permute-start.15 = (bf16[3,160,512]{2,1,0:T(8,128)(2,1)}, bf16[3,160,512]{2,1,0:T(8,128)(2,1)S(1)}, u32[]{:S(2)}, u32[]{:S(2)}) collective-permute-start(bf16[3,160,512]{2,1,0:T(8,128)(2,1)} %get-tuple-element.79), channel_id=1, source_target_pairs={{0,16},{4,20},{8,24},{12,28},{16,0},{20,4},{24,8},{28,12},{1,17},{... | collective-permute-start | bytes 1474568 | tf_op jit(solution)/shard_map/ppermute | solution.py:48
  15.1 21.6 %collective-permute-start.16 = (bf16[3,160,512]{2,1,0:T(8,128)(2,1)}, bf16[3,160,512]{2,1,0:T(8,128)(2,1)S(1)}, u32[]{:S(2)}, u32[]{:S(2)}) collective-permute-start(bf16[3,160,512]{2,1,0:T(8,128)(2,1)} %get-tuple-element.80), channel_id=1, source_target_pairs={{0,24},{4,28},{8,16},{12,20},{16,8},{20,12},{24,0},{28,4},{1,25},{... | collective-permute-start | bytes 1474568 | tf_op jit(solution)/shard_map/ppermute | solution.py:48
  36.7 2.1 %collective-permute-start.17 = (bf16[3,160,512]{2,1,0:T(8,128)(2,1)}, bf16[3,160,512]{2,1,0:T(8,128)(2,1)S(1)}, u32[]{:S(2)}, u32[]{:S(2)}) collective-permute-start(bf16[3,160,512]{2,1,0:T(8,128)(2,1)} %get-tuple-element.86), channel_id=1, source_target_pairs={{0,4},{4,0},{8,12},{12,8},{16,20},{20,16},{24,28},{28,24},{1,5},{5... | collective-permute-start | bytes 1474568 | tf_op jit(solution)/shard_map/ppermute | solution.py:48
  36.8 14.0 %collective-permute-start.18 = (bf16[3,160,512]{2,1,0:T(8,128)(2,1)}, bf16[3,160,512]{2,1,0:T(8,128)(2,1)S(1)}, u32[]{:S(2)}, u32[]{:S(2)}) collective-permute-start(bf16[3,160,512]{2,1,0:T(8,128)(2,1)} %get-tuple-element.90), channel_id=1, source_target_pairs={{0,28},{4,24},{8,20},{12,16},{16,12},{20,8},{24,4},{28,0},{1,29},{... | collective-permute-start | bytes 1474568 | tf_op jit(solution)/shard_map/ppermute | solution.py:48
  50.7 73.9 %copy-start.4 = (bf16[1024,640]{1,0:T(8,128)(2,1)}, bf16[1024,640]{1,0:T(8,128)(2,1)S(1)}, u32[]{:S(2)}) copy-start(bf16[1024,640]{1,0:T(8,128)(2,1)S(1)} %collective-permute-done.19.refs_21_) | copy-start | bytes 3932164
  50.7 47.0 %copy-start.5 = (bf16[1024,640]{1,0:T(8,128)(2,1)}, bf16[1024,640]{1,0:T(8,128)(2,1)S(1)}, u32[]{:S(2)}) copy-start(bf16[1024,640]{1,0:T(8,128)(2,1)S(1)} %collective-permute-done.20.refs_19_) | copy-start | bytes 3932164
  50.8 38.0 %collective-permute-start.27 = (bf16[1024,640]{1,0:T(8,128)(2,1)S(1)}, bf16[1024,640]{1,0:T(8,128)(2,1)}, u32[]{:S(2)}, u32[]{:S(2)}) collective-permute-start(bf16[1024,640]{1,0:T(8,128)(2,1)S(1)} %collective-permute-done.19.refs_21_), channel_id=1, source_target_pairs={{1,2},{2,3},{5,6},{6,7},{9,10},{10,11},{13,14},{14,15},{17,18},{18... | collective-permute-start | bytes 3932168 | tf_op jit(solution)/shard_map/ppermute | solution.py:140
  52.7 36.1 %collective-permute-start.28 = (bf16[1024,640]{1,0:T(8,128)(2,1)S(1)}, bf16[1024,640]{1,0:T(8,128)(2,1)}, u32[]{:S(2)}, u32[]{:S(2)}) collective-permute-start(bf16[1024,640]{1,0:T(8,128)(2,1)S(1)} %collective-permute-done.20.refs_19_), channel_id=1, source_target_pairs={{1,0},{2,1},{5,4},{6,5},{9,8},{10,9},{13,12},{14,13},{17,16},{18,1... | collective-permute-start | bytes 3932168 | tf_op jit(solution)/shard_map/ppermute | solution.py:140
  54.0 13.2 %collective-permute-start.21 = (bf16[3,160,512]{2,1,0:T(8,128)(2,1)}, bf16[3,160,512]{2,1,0:T(8,128)(2,1)S(1)}, u32[]{:S(2)}, u32[]{:S(2)}) collective-permute-start(bf16[3,160,512]{2,1,0:T(8,128)(2,1)} %get-tuple-element.97), channel_id=1, source_target_pairs={{0,12},{4,8},{8,4},{12,0},{16,28},{20,24},{24,20},{28,16},{1,13},{... | collective-permute-start | bytes 1474568 | tf_op jit(solution)/shard_map/ppermute | solution.py:48
  55.3 13.5 %collective-permute-start.22 = (bf16[3,160,512]{2,1,0:T(8,128)(2,1)}, bf16[3,160,512]{2,1,0:T(8,128)(2,1)S(1)}, u32[]{:S(2)}, u32[]{:S(2)}) collective-permute-start(bf16[3,160,512]{2,1,0:T(8,128)(2,1)} %get-tuple-element.99), channel_id=1, source_target_pairs={{0,20},{4,16},{8,28},{12,24},{16,4},{20,0},{24,12},{28,8},{1,21},{... | collective-permute-start | bytes 1474568 | tf_op jit(solution)/shard_map/ppermute | solution.py:48
  75.0 49.6 %copy-start = (bf16[384,512]{1,0:T(8,128)(2,1)}, bf16[384,512]{1,0:T(8,128)(2,1)S(1)}, u32[]{:S(2)}) copy-start(bf16[384,512]{1,0:T(8,128)(2,1)S(1)} %get-tuple-element.112.refs_0_) | copy-start | bytes 1179652
  75.0 49.6 %copy-start.1 = (bf16[384,512]{1,0:T(8,128)(2,1)}, bf16[384,512]{1,0:T(8,128)(2,1)S(1)}, u32[]{:S(2)}) copy-start(bf16[384,512]{1,0:T(8,128)(2,1)S(1)} %get-tuple-element.113.refs_1_) | copy-start | bytes 1179652
  75.0 11.5 %collective-permute-start.25 = (bf16[384,512]{1,0:T(8,128)(2,1)S(1)}, bf16[384,512]{1,0:T(8,128)(2,1)S(1)}, u32[]{:S(2)}, u32[]{:S(2)}) collective-permute-start(bf16[384,512]{1,0:T(8,128)(2,1)S(1)} %get-tuple-element.112.refs_0_), channel_id=1, source_target_pairs={{0,8},{4,12},{8,0},{12,4},{16,24},{20,28},{24,16},{28,20},{1,9},{5... | collective-permute-start | bytes 1179656 | tf_op jit(solution)/shard_map/ppermute | solution.py:48
  75.8 11.5 %collective-permute-start.26 = (bf16[384,512]{1,0:T(8,128)(2,1)S(1)}, bf16[384,512]{1,0:T(8,128)(2,1)S(1)}, u32[]{:S(2)}, u32[]{:S(2)}) collective-permute-start(bf16[384,512]{1,0:T(8,128)(2,1)S(1)} %get-tuple-element.113.refs_1_), channel_id=1, source_target_pairs={{0,16},{4,20},{8,24},{12,28},{16,0},{20,4},{24,8},{28,12},{1,17},{... | collective-permute-start | bytes 1179656 | tf_op jit(solution)/shard_map/ppermute | solution.py:48
  77.3 14.6 %collective-permute-start.23 = (bf16[384,512]{1,0:T(8,128)(2,1)S(1)}, bf16[384,512]{1,0:T(8,128)(2,1)S(1)}, u32[]{:S(2)}, u32[]{:S(2)}) collective-permute-start(bf16[384,512]{1,0:T(8,128)(2,1)S(1)} %get-tuple-element.112.refs_0_), channel_id=1, source_target_pairs={{0,4},{4,0},{8,12},{12,8},{16,20},{20,16},{24,28},{28,24},{1,5},{5... | collective-permute-start | bytes 1179656 | tf_op jit(solution)/shard_map/ppermute | solution.py:48
  86.5 38.2 %copy-start.6 = (bf16[384,512]{1,0:T(8,128)(2,1)}, bf16[384,512]{1,0:T(8,128)(2,1)S(1)}, u32[]{:S(2)}) copy-start(bf16[384,512]{1,0:T(8,128)(2,1)S(1)} %collective-permute-done.25.refs_4_) | copy-start | bytes 1179652
  86.5 10.8 %collective-permute-start.29 = (bf16[384,512]{1,0:T(8,128)(2,1)S(1)}, bf16[384,512]{1,0:T(8,128)(2,1)S(1)}, u32[]{:S(2)}, u32[]{:S(2)}) collective-permute-start(bf16[384,512]{1,0:T(8,128)(2,1)S(1)} %get-tuple-element.113.refs_1_), channel_id=1, source_target_pairs={{0,8},{4,12},{8,0},{12,4},{16,24},{20,28},{24,16},{28,20},{1,9},{5... | collective-permute-start | bytes 1179656 | tf_op jit(solution)/shard_map/ppermute | solution.py:48
  87.3 37.4 %copy-start.7 = (bf16[384,512]{1,0:T(8,128)(2,1)}, bf16[384,512]{1,0:T(8,128)(2,1)S(1)}, u32[]{:S(2)}) copy-start(bf16[384,512]{1,0:T(8,128)(2,1)S(1)} %collective-permute-done.26.refs_9_) | copy-start | bytes 1179652
  87.3 10.5 %collective-permute-start.32 = (bf16[384,512]{1,0:T(8,128)(2,1)S(1)}, bf16[384,512]{1,0:T(8,128)(2,1)S(1)}, u32[]{:S(2)}, u32[]{:S(2)}) collective-permute-start(bf16[384,512]{1,0:T(8,128)(2,1)S(1)} %get-tuple-element.112.refs_0_), channel_id=1, source_target_pairs={{0,16},{4,20},{8,24},{12,28},{16,0},{20,4},{24,8},{28,12},{1,17},{... | collective-permute-start | bytes 1179656 | tf_op jit(solution)/shard_map/ppermute | solution.py:48
  88.8 35.8 %collective-permute-start.39 = (bf16[1024,640]{1,0:T(8,128)(2,1)}, bf16[1024,640]{1,0:T(8,128)(2,1)}, u32[]{:S(2)}, u32[]{:S(2)}) collective-permute-start(bf16[1024,640]{1,0:T(8,128)(2,1)} %collective-permute-done.28.refs_18_), channel_id=1, source_target_pairs={{1,0},{5,4},{9,8},{13,12},{17,16},{21,20},{25,24},{29,28}} | collective-permute-start | bytes 3932168 | tf_op jit(solution)/shard_map/ppermute | solution.py:140
  90.1 34.5 %collective-permute-start.40 = (bf16[1024,640]{1,0:T(8,128)(2,1)}, bf16[1024,640]{1,0:T(8,128)(2,1)}, u32[]{:S(2)}, u32[]{:S(2)}) collective-permute-start(bf16[1024,640]{1,0:T(8,128)(2,1)} %collective-permute-done.27.refs_22_), channel_id=1, source_target_pairs={{2,3},{6,7},{10,11},{14,15},{18,19},{22,23},{26,27},{30,31}} | collective-permute-start | bytes 3932168 | tf_op jit(solution)/shard_map/ppermute | solution.py:140
  91.9 19.0 %copy-start.8 = (bf16[384,512]{1,0:T(8,128)(2,1)}, bf16[384,512]{1,0:T(8,128)(2,1)S(1)}, u32[]{:S(2)}) copy-start(bf16[384,512]{1,0:T(8,128)(2,1)S(1)} %collective-permute-done.23.refs_2_) | copy-start | bytes 1179652
  91.9 5.9 %collective-permute-start.24 = (bf16[384,512]{1,0:T(8,128)(2,1)S(1)}, bf16[384,512]{1,0:T(8,128)(2,1)S(1)}, u32[]{:S(2)}, u32[]{:S(2)}) collective-permute-start(bf16[384,512]{1,0:T(8,128)(2,1)S(1)} %get-tuple-element.113.refs_1_), channel_id=1, source_target_pairs={{0,4},{4,0},{8,12},{12,8},{16,20},{20,16},{24,28},{28,24},{1,5},{5... | collective-permute-start | bytes 1179656 | tf_op jit(solution)/shard_map/ppermute | solution.py:48
  97.2 13.6 %copy-start.9 = (bf16[384,512]{1,0:T(8,128)(2,1)}, bf16[384,512]{1,0:T(8,128)(2,1)S(1)}, u32[]{:S(2)}) copy-start(bf16[384,512]{1,0:T(8,128)(2,1)S(1)} %collective-permute-done.29.refs_5_) | copy-start | bytes 1179652
  97.2 1.7 %collective-permute-start.31 = (bf16[384,512]{1,0:T(8,128)(2,1)S(1)}, bf16[384,512]{1,0:T(8,128)(2,1)S(1)}, u32[]{:S(2)}, u32[]{:S(2)}) collective-permute-start(bf16[384,512]{1,0:T(8,128)(2,1)S(1)} %collective-permute-done.29.refs_5_), channel_id=1, source_target_pairs={{0,4},{4,0},{8,12},{12,8},{16,20},{20,16},{24,28},{28,24},{1,5},{5... | collective-permute-start | bytes 1179656 | tf_op jit(solution)/shard_map/ppermute | solution.py:48
  97.8 13.1 %copy-start.10 = (bf16[384,512]{1,0:T(8,128)(2,1)}, bf16[384,512]{1,0:T(8,128)(2,1)S(1)}, u32[]{:S(2)}) copy-start(bf16[384,512]{1,0:T(8,128)(2,1)S(1)} %collective-permute-done.32.refs_8_) | copy-start | bytes 1179652
  97.8 2.1 %collective-permute-start.33 = (bf16[384,512]{1,0:T(8,128)(2,1)S(1)}, bf16[384,512]{1,0:T(8,128)(2,1)S(1)}, u32[]{:S(2)}, u32[]{:S(2)}) collective-permute-start(bf16[384,512]{1,0:T(8,128)(2,1)S(1)} %collective-permute-done.32.refs_8_), channel_id=1, source_target_pairs={{0,4},{4,0},{8,12},{12,8},{16,20},{20,16},{24,28},{28,24},{1,5},{5... | collective-permute-start | bytes 1179656 | tf_op jit(solution)/shard_map/ppermute | solution.py:48
  97.8 13.1 %copy-start.11 = (bf16[384,512]{1,0:T(8,128)(2,1)}, bf16[384,512]{1,0:T(8,128)(2,1)S(1)}, u32[]{:S(2)}) copy-start(bf16[384,512]{1,0:T(8,128)(2,1)S(1)} %collective-permute-done.24.refs_3_) | copy-start | bytes 1179652
  97.8 3.5 %collective-permute-start.30 = (bf16[384,512]{1,0:T(8,128)(2,1)S(1)}, bf16[384,512]{1,0:T(8,128)(2,1)S(1)}, u32[]{:S(2)}, u32[]{:S(2)}) collective-permute-start(bf16[384,512]{1,0:T(8,128)(2,1)S(1)} %collective-permute-done.25.refs_4_), channel_id=1, source_target_pairs={{0,4},{4,0},{8,12},{12,8},{16,20},{20,16},{24,28},{28,24},{1,5},{5... | collective-permute-start | bytes 1179656 | tf_op jit(solution)/shard_map/ppermute | solution.py:48
  99.0 11.9 %copy-start.12 = (bf16[384,512]{1,0:T(8,128)(2,1)}, bf16[384,512]{1,0:T(8,128)(2,1)S(1)}, u32[]{:S(2)}) copy-start(bf16[384,512]{1,0:T(8,128)(2,1)S(1)} %collective-permute-done.31.refs_7_) | copy-start | bytes 1179652
  99.0 11.3 %collective-permute-start.35 = (bf16[384,512]{1,0:T(8,128)(2,1)S(1)}, bf16[384,512]{1,0:T(8,128)(2,1)}, u32[]{:S(2)}, u32[]{:S(2)}) collective-permute-start(bf16[384,512]{1,0:T(8,128)(2,1)S(1)} %collective-permute-done.25.refs_4_), channel_id=1, source_target_pairs={{0,16},{4,20},{8,24},{12,28},{16,0},{20,4},{24,8},{28,12},{1,17},{... | collective-permute-start | bytes 1179656 | tf_op jit(solution)/shard_map/ppermute | solution.py:48
  99.9 11.0 %copy-start.13 = (bf16[384,512]{1,0:T(8,128)(2,1)}, bf16[384,512]{1,0:T(8,128)(2,1)S(1)}, u32[]{:S(2)}) copy-start(bf16[384,512]{1,0:T(8,128)(2,1)S(1)} %collective-permute-done.33.refs_10_) | copy-start | bytes 1179652
  99.9 10.9 %collective-permute-start.36 = (bf16[384,512]{1,0:T(8,128)(2,1)S(1)}, bf16[384,512]{1,0:T(8,128)(2,1)}, u32[]{:S(2)}, u32[]{:S(2)}) collective-permute-start(bf16[384,512]{1,0:T(8,128)(2,1)S(1)} %collective-permute-done.26.refs_9_), channel_id=1, source_target_pairs={{0,8},{4,12},{8,0},{12,4},{16,24},{20,28},{24,16},{28,20},{1,9},{5... | collective-permute-start | bytes 1179656 | tf_op jit(solution)/shard_map/ppermute | solution.py:48
  101.3 9.6 %copy-start.14 = (bf16[384,512]{1,0:T(8,128)(2,1)}, bf16[384,512]{1,0:T(8,128)(2,1)S(1)}, u32[]{:S(2)}) copy-start(bf16[384,512]{1,0:T(8,128)(2,1)S(1)} %collective-permute-done.30.refs_6_) | copy-start | bytes 1179652
  101.3 10.3 %collective-permute-start.34 = (bf16[384,512]{1,0:T(8,128)(2,1)S(1)}, bf16[384,512]{1,0:T(8,128)(2,1)}, u32[]{:S(2)}, u32[]{:S(2)}) collective-permute-start(bf16[384,512]{1,0:T(8,128)(2,1)S(1)} %collective-permute-done.26.refs_9_), channel_id=1, source_target_pairs={{0,4},{4,0},{8,12},{12,8},{16,20},{20,16},{24,28},{28,24},{1,5},{5... | collective-permute-start | bytes 1179656 | tf_op jit(solution)/shard_map/ppermute | solution.py:48
  110.2 2.1 %collective-permute-start.37 = (bf16[384,512]{1,0:T(8,128)(2,1)}, bf16[384,512]{1,0:T(8,128)(2,1)}, u32[]{:S(2)}, u32[]{:S(2)}) collective-permute-start(bf16[384,512]{1,0:T(8,128)(2,1)} %collective-permute-done.35.refs_12_), channel_id=1, source_target_pairs={{0,4},{4,0},{8,12},{12,8},{16,20},{20,16},{24,28},{28,24},{1,5},{5... | collective-permute-start | bytes 1179656 | tf_op jit(solution)/shard_map/ppermute | solution.py:48
  110.8 2.1 %collective-permute-start.38 = (bf16[384,512]{1,0:T(8,128)(2,1)}, bf16[384,512]{1,0:T(8,128)(2,1)}, u32[]{:S(2)}, u32[]{:S(2)}) collective-permute-start(bf16[384,512]{1,0:T(8,128)(2,1)} %collective-permute-done.36.refs_13_), channel_id=1, source_target_pairs={{0,4},{4,0},{8,12},{12,8},{16,20},{20,16},{24,28},{28,24},{1,5},{5... | collective-permute-start | bytes 1179656 | tf_op jit(solution)/shard_map/ppermute | solution.py:48
  124.7 31.9 %copy-start.2 = (s32[1,160]{1,0:T(1,128)S(1)}, s32[1,160]{1,0:T(1,128)}, u32[]{:S(2)}) copy-start(s32[1,160]{1,0:T(1,128)} %mask_ref.3) | copy-start | bytes 1924
  134.5 3.6 %collective-permute-start.41 = (bf16[160,640]{1,0:T(8,128)(2,1)}, bf16[160,640]{1,0:T(8,128)(2,1)S(1)}, u32[]{:S(2)}, u32[]{:S(2)}) collective-permute-start(bf16[160,640]{1,0:T(8,128)(2,1)} %get-tuple-element.138), channel_id=1, source_target_pairs={{0,4},{4,0},{8,12},{12,8},{16,20},{20,16},{24,28},{28,24},{1,5},{5... | collective-permute-start | bytes 614408 | tf_op jit(solution)/shard_map/ppermute | solution.py:48
  134.6 8.2 %collective-permute-start.42 = (bf16[160,640]{1,0:T(8,128)(2,1)}, bf16[160,640]{1,0:T(8,128)(2,1)S(1)}, u32[]{:S(2)}, u32[]{:S(2)}) collective-permute-start(bf16[160,640]{1,0:T(8,128)(2,1)} %get-tuple-element.139), channel_id=1, source_target_pairs={{0,8},{4,12},{8,0},{12,4},{16,24},{20,28},{24,16},{28,20},{1,9},{5... | collective-permute-start | bytes 614408 | tf_op jit(solution)/shard_map/ppermute | solution.py:48
  135.2 11.0 %collective-permute-start.43 = (bf16[160,640]{1,0:T(8,128)(2,1)}, bf16[160,640]{1,0:T(8,128)(2,1)S(1)}, u32[]{:S(2)}, u32[]{:S(2)}) collective-permute-start(bf16[160,640]{1,0:T(8,128)(2,1)} %get-tuple-element.140), channel_id=1, source_target_pairs={{0,12},{4,8},{8,4},{12,0},{16,28},{20,24},{24,20},{28,16},{1,13},{... | collective-permute-start | bytes 614408 | tf_op jit(solution)/shard_map/ppermute | solution.py:48
  136.4 9.8 %collective-permute-start.44 = (bf16[160,640]{1,0:T(8,128)(2,1)}, bf16[160,640]{1,0:T(8,128)(2,1)S(1)}, u32[]{:S(2)}, u32[]{:S(2)}) collective-permute-start(bf16[160,640]{1,0:T(8,128)(2,1)} %get-tuple-element.141), channel_id=1, source_target_pairs={{0,16},{4,20},{8,24},{12,28},{16,0},{20,4},{24,8},{28,12},{1,17},{... | collective-permute-start | bytes 614408 | tf_op jit(solution)/shard_map/ppermute | solution.py:48
  136.9 19.6 %collective-permute-start.45 = (bf16[160,640]{1,0:T(8,128)(2,1)}, bf16[160,640]{1,0:T(8,128)(2,1)S(1)}, u32[]{:S(2)}, u32[]{:S(2)}) collective-permute-start(bf16[160,640]{1,0:T(8,128)(2,1)} %get-tuple-element.142), channel_id=1, source_target_pairs={{0,20},{4,16},{8,28},{12,24},{16,4},{20,0},{24,12},{28,8},{1,21},{... | collective-permute-start | bytes 614408 | tf_op jit(solution)/shard_map/ppermute | solution.py:48
  138.1 18.4 %collective-permute-start.46 = (bf16[160,640]{1,0:T(8,128)(2,1)}, bf16[160,640]{1,0:T(8,128)(2,1)S(1)}, u32[]{:S(2)}, u32[]{:S(2)}) collective-permute-start(bf16[160,640]{1,0:T(8,128)(2,1)} %get-tuple-element.143), channel_id=1, source_target_pairs={{0,24},{4,28},{8,16},{12,20},{16,8},{20,12},{24,0},{28,4},{1,25},{... | collective-permute-start | bytes 614408 | tf_op jit(solution)/shard_map/ppermute | solution.py:48
  142.7 13.8 %collective-permute-start.47 = (bf16[160,640]{1,0:T(8,128)(2,1)}, bf16[160,640]{1,0:T(8,128)(2,1)S(1)}, u32[]{:S(2)}, u32[]{:S(2)}) collective-permute-start(bf16[160,640]{1,0:T(8,128)(2,1)} %get-tuple-element.144), channel_id=1, source_target_pairs={{0,28},{4,24},{8,20},{12,16},{16,12},{20,8},{24,4},{28,0},{1,29},{... | collective-permute-start | bytes 614408 | tf_op jit(solution)/shard_map/ppermute | solution.py:48
  (1 other events, 0.5 us)
where the time goes:
time: 160 us; the launch traced here: 159 us
  waiting for transfers between devices  102 us (64%)
  starting transfers between devices  31.9 us (20%)
  Pallas kernels  22.9 us (14%)
    ppermute x28, waiting for transfers between devices, xor_permute(): lax.ppermute(array, 'cam', [(place, place ^ mask) for place in range(coun...  90.3 us
    ppermute x28, starting transfers between devices, xor_permute(): lax.ppermute(array, 'cam', [(place, place ^ mask) for place in range(coun...  19.3 us
    ppermute x6, starting transfers between devices, pass_weight(): lax.ppermute(shards[sign * (distance - 1)], 'fsdp', pairs)  12.6 us
    ppermute x6, waiting for transfers between devices, pass_weight(): lax.ppermute(shards[sign * (distance - 1)], 'fsdp', pairs)  11.7 us
    pallas_call x1, Pallas kernels, project(): pl.pallas_call(body, grid_spec=pltpu.PrefetchScalarGridSpec(num_scalar_pr...  9.79 us
    pallas_call x1, Pallas kernels, attend(): pl.pallas_call(body, grid_spec=pltpu.PrefetchScalarGridSpec(num_scalar_pr...  5.66 us
    pallas_call x1, Pallas kernels, pack(): pl.pallas_call(body, grid_spec=pltpu.PrefetchScalarGridSpec(num_scalar_pr...  5.06 us
  transfers between devices with their start and end apart: 34, of which 18 were waited for; matrix products, arithmetic and copies ran while one was open for 0% of the time, Pallas kernels for 4%

commit v1 on v0

--- a/solution.py
+++ b/solution.py
@@ -274,23 +274,19 @@
 
 
 def gather_features(own, count, between=lambda arrived: arrived):
-    held = {0: list(own)}
+    half = own.shape[0] // 2
+    held = {0: [own]}
     if count == 8:
-        over_x_0 = xor_permute(held[0][0], 2, count)
-        over_y_1 = xor_permute(held[0][1], 4, count)
-        over_x_1 = xor_permute(held[0][1], 2, count)
-        over_y_0 = xor_permute(held[0][0], 4, count)
-        over_x_0, over_y_1 = between((over_x_0, over_y_1))
-        diagonal_0 = xor_permute(over_x_0, 4, count)
-        diagonal_1 = xor_permute(over_y_1, 2, count)
-        held[2] = [over_x_0, over_x_1]
-        held[4] = [over_y_0, over_y_1]
-        held[6] = [diagonal_0, diagonal_1]
+        over_x = xor_permute(own, 2, count)
+        over_y = xor_permute(own, 4, count)
+        held[1] = [between(xor_permute(own, 1, count))]
+        held[2], held[4] = [over_x], [over_y]
+        held[6] = [xor_permute(over_x[:half], 4, count), xor_permute(over_y[half:], 2, count)]
     else:
         for mask in range(2, count, 2):
-            held[mask] = [xor_permute(piece, mask, count) for piece in held[0]]
-        held[2] = list(between(tuple(held[2])))
-    for mask in range(0, count, 2):
+            held[mask] = [xor_permute(own, mask, count)]
+        held[1] = [between(xor_permute(own, 1, count))]
+    for mask in range(2, count, 2):
         held[mask + 1] = [xor_permute(piece, 1, count) for piece in held[mask]]
     return [held[mask] for mask in range(count)]
 
@@ -309,19 +305,21 @@
 
 def project(place, group, counts, features, more, shards, rows):
     count = len(features)
-    half, width = features[0][0].shape
+    width = more.shape[2]
     total = count * rows
+    always = total - more.shape[1]
     distances = sorted(shards)
     columns = shards[0].shape[1]
     each = shards[0].shape[0] // width
-    bounds = [size for size in variants(total) if size <= 2 * half] + [total]
+    bounds = [size for size in variants(total) if size <= always] + [total]
+    flat = [piece for pieces in features for piece in pieces]
 
     def body(place_ref, group_ref, counts_ref, *refs):
-        flat = refs[: 2 * count]
-        more_ref = refs[2 * count]
-        shard_refs = refs[2 * count + 1 : 2 * count + 1 + len(distances)]
-        out_refs = refs[2 * count + 1 + len(distances) : 3 * count + 1 + len(distances)]
-        landed, weight_all, sums, sems, weight_sems = refs[3 * count + 1 + len(distances) :]
+        flat_refs = list(refs[: len(flat)])
+        more_ref = refs[len(flat)]
+        shard_refs = refs[len(flat) + 1 : len(flat) + 1 + len(distances)]
+        out_refs = refs[len(flat) + 1 + len(distances) :][:count]
+        landed, weight_all, sums, sems, weight_sems = refs[len(flat) + 1 + len(distances) + count :]
         used = sum(counts_ref[mask] for mask in range(count)) * BLOCK
 
         for mask in range(count):
@@ -344,11 +342,13 @@
 
             @pl.when((used > below) & (used <= size))
             def _(size=size):
+                taken = 0
                 for mask in range(count):
                     lanes = slice(mask % 2 * width, (mask % 2 + 1) * width)
-                    sources = [flat[2 * mask], flat[2 * mask + 1]]
-                    if size > 2 * half:
-                        sources += [more_ref.at[2 * mask], more_ref.at[2 * mask + 1]]
+                    sources = flat_refs[taken : taken + len(features[mask])]
+                    taken += len(sources)
+                    if size > always:
+                        sources.append(more_ref.at[mask])
                     first = 0
                     for source in sources:
                         length = min(source.shape[0], size - first)
@@ -386,7 +386,7 @@
             out_refs[mask][...] = moved.astype(jnp.bfloat16)
 
     any_spec = pl.BlockSpec(memory_space=pl.ANY)
-    inputs = [piece for pair in features for piece in pair] + [more]
+    inputs = flat + [more]
     inputs += [shards[distance] for distance in distances]
     inputs = [pltpu.with_memory_space_constraint(array, pltpu.HBM) for array in inputs]
     return pl.pallas_call(
@@ -484,28 +484,25 @@
     pass_weight(shards, 2)
     for mask in late[1:-1]:
         received[mask] = xor_permute(payloads[mask], mask, count)
-    half = total * 3 // 10
-    first, second, rest, counts, used = attend(
-        place_array, received, rows, (half, half, total - 2 * half)
+    always = total * 3 // 5
+    attended, rest, counts, used = attend(
+        place_array, received, rows, (always, total - always)
     )
-
-    quarter = rest.shape[0] // 2
-    shape = jax.ShapeDtypeStruct((2 * count, quarter, rest.shape[1]), rest.dtype)
+    shape = jax.ShapeDtypeStruct((count,) + rest.shape, rest.dtype)
 
     def gather_rest(part):
-        pieces = gather_features((part[:quarter], part[quarter:]), count)
-        return jnp.stack([piece for pair in pieces for piece in pair])
+        return jnp.stack([jnp.concatenate(pieces) for pieces in gather_features(part, count)])
 
     def weight_step(arrived):
         arrived, shards[2], shards[-2] = lax.optimization_barrier((arrived, shards[2], shards[-2]))
         pass_weight(shards, 3)
         return arrived
 
-    features = gather_features((first, second), count, weight_step)
+    features = gather_features(attended, count, weight_step)
     for distance in range(4, groups):
         pass_weight(shards, distance)
     rest, features, shards = lax.optimization_barrier((rest, features, shards))
-    more = lax.cond(used[0] > 2 * half, gather_rest, lambda part: unfilled(shape), rest)
+    more = lax.cond(used[0] > always, gather_rest, lambda part: unfilled(shape), rest)
     pieces = project(place_array, group_array, counts, features, more, shards, rows)
     landed = [pieces[0]] + [None] * (count - 1)
     for mask in order(count):

time: 160 us -> 157 us (0.981)
  Pallas kernels: 22.9 us -> 21.2 us
  starting transfers between devices: 31.9 us -> 30.2 us
    ppermute x6, waiting for transfers between devices: 11.7 us -> 31.1 us  [pass_weight(): lax.ppermute(shards[sign * (distance - 1)], 'fsdp', pairs)]
    ppermute x28 -> x23, waiting for transfers between devices: 90.3 us -> 72.2 us  [xor_permute(): lax.ppermute(array, 'cam', [(place, place ^ mask) for place in range(coun...]
    ppermute x28 -> x23, starting transfers between devices: 19.3 us -> 17.8 us  [xor_permute(): lax.ppermute(array, 'cam', [(place, place ^ mask) for place in range(coun...]
  transfers between devices with their start and end apart: 34 -> 29, of which waited for: 18 -> 15; matrix products, arithmetic and copies ran while one was open for 0% -> 0% of each run, Pallas kernels for 4% -> 3%
where the time goes in v1:
time: 157 us
  waiting for transfers between devices  103 us (66%)
  starting transfers between devices  30.2 us (19%)
  Pallas kernels  21.2 us (14%)
    ppermute x23, waiting for transfers between devices, xor_permute(): lax.ppermute(array, 'cam', [(place, place ^ mask) for place in range(coun...  72.2 us
    ppermute x6, waiting for transfers between devices, pass_weight(): lax.ppermute(shards[sign * (distance - 1)], 'fsdp', pairs)  31.1 us
    ppermute x23, starting transfers between devices, xor_permute(): lax.ppermute(array, 'cam', [(place, place ^ mask) for place in range(coun...  17.8 us
    ppermute x6, starting transfers between devices, pass_weight(): lax.ppermute(shards[sign * (distance - 1)], 'fsdp', pairs)  12.4 us
    pallas_call x1, Pallas kernels, project(): pl.pallas_call(body, grid_spec=pltpu.PrefetchScalarGridSpec(num_scalar_pr...  8.88 us
    pallas_call x1, Pallas kernels, pack(): pl.pallas_call(body, grid_spec=pltpu.PrefetchScalarGridSpec(num_scalar_pr...  5.06 us
    pallas_call x1, Pallas kernels, attend(): pl.pallas_call(body, grid_spec=pltpu.PrefetchScalarGridSpec(num_scalar_pr...  4.87 us
  transfers between devices with their start and end apart: 29, of which 15 were waited for; matrix products, arithmetic and copies ran while one was open for 0% of the time, Pallas kernels for 3%

profile of v1, /device:TPU:0, one launch (start us, length us, event | category | flops | bytes accessed | tf_op | source)
XLA Modules:
  0.0 156.6 jit_solution(5767155316620371184)
XLA Ops:
  0.7 5.1 %pack.1 = (bf16[3,160,512]{2,1,0:T(8,128)(2,1)}, bf16[3,160,512]{2,1,0:T(8,128)(2,1)}, bf16[3,160,512]{2,1,0:T(8,128)(2,1)}, bf16[3,160,512]{2,1,0:T(8,128)(2,1)...) custom-call(s32[1]{0:T(128)} %bitcast.8.place_ref, ...), custom_call_target="tpu_custom_call" | custom-call | bytes 7864320 | tf_op jit(solution)/shard_map/pack/pallas_call | solution.py:103
  5.7 5.0 %collective-permute-start.14 = (bf16[1024,640]{1,0:T(8,128)(2,1)}, bf16[1024,640]{1,0:T(8,128)(2,1)S(1)}, u32[]{:S(2)}, u32[]{:S(2)}) collective-permute-start(bf16[1024,640]{1,0:T(8,128)(2,1)} %get-tuple-element.117.refs_14_), channel_id=1, source_target_pairs={{0,1},{1,2},{2,3},{4,5},{5,6},{6,7},{8,9},{9,10},{10,11},{12,13},{... | collective-permute-start | bytes 3932168 | tf_op jit(solution)/shard_map/ppermute | solution.py:140
  10.7 1.3 collective-permute-start.15
  12.0 1.6 collective-permute-start.9
  13.6 1.5 collective-permute-start.10
  15.1 0.5 collective-permute-start.11
  15.6 10.9 %collective-permute-done.9.refs_2_ = bf16[3,160,512]{2,1,0:T(8,128)(2,1)S(1)} collective-permute-done((bf16[3,160,512]{2,1,0:T(8,128)(2,1)}, bf16[3,160,512]{2,1,0:T(8,128)(2,1)S(1)}, u32[]{:S(2)}, u32[]{:S(2)}) %collective-permute-start.9) | collective-permute-done | bytes 491552 | tf_op jit(solution)/shard_map/ppermute | solution.py:48
  26.5 10.3 %collective-permute-done.10.refs_4_ = bf16[3,160,512]{2,1,0:T(8,128)(2,1)S(1)} collective-permute-done((bf16[3,160,512]{2,1,0:T(8,128)(2,1)}, bf16[3,160,512]{2,1,0:T(8,128)(2,1)S(1)}, u32[]{:S(2)}, u32[]{:S(2)}) %collective-permute-start.10) | collective-permute-done | bytes 491552 | tf_op jit(solution)/shard_map/ppermute | solution.py:48
  36.7 0.0 collective-permute-done.11.refs_6_
  36.7 0.0 collective-permute-start.12
  36.8 1.6 %collective-permute-start.13 = (bf16[3,160,512]{2,1,0:T(8,128)(2,1)}, bf16[3,160,512]{2,1,0:T(8,128)(2,1)S(1)}, u32[]{:S(2)}, u32[]{:S(2)}) collective-permute-start(bf16[3,160,512]{2,1,0:T(8,128)(2,1)} %get-tuple-element.82), channel_id=1, source_target_pairs={{0,28},{4,24},{8,20},{12,16},{16,12},{20,8},{24,4},{28,0},{1,29},{... | collective-permute-start | bytes 1474568 | tf_op jit(solution)/shard_map/ppermute | solution.py:48
  38.4 0.5 collective-permute-done.12.refs_1_
  38.8 11.9 %collective-permute-done.13.refs_7_ = bf16[3,160,512]{2,1,0:T(8,128)(2,1)S(1)} collective-permute-done((bf16[3,160,512]{2,1,0:T(8,128)(2,1)}, bf16[3,160,512]{2,1,0:T(8,128)(2,1)S(1)}, u32[]{:S(2)}, u32[]{:S(2)}) %collective-permute-start.13) | collective-permute-done | bytes 491552 | tf_op jit(solution)/shard_map/ppermute | solution.py:48
  50.8 1.4 collective-permute-start.16
  52.1 0.5 collective-permute-start.17
  52.6 1.8 %collective-permute-start.19 = (bf16[1024,640]{1,0:T(8,128)(2,1)S(1)}, bf16[1024,640]{1,0:T(8,128)(2,1)}, u32[]{:S(2)}, u32[]{:S(2)}) collective-permute-start(bf16[1024,640]{1,0:T(8,128)(2,1)S(1)} %collective-permute-done.14.refs_15_), channel_id=1, source_target_pairs={{1,2},{2,3},{5,6},{6,7},{9,10},{10,11},{13,14},{14,15},{17,18},{18... | collective-permute-start | bytes 3932168 | tf_op jit(solution)/shard_map/ppermute | solution.py:140
  54.4 1.3 collective-permute-start.20
  55.7 8.3 %collective-permute-done.16.refs_3_ = bf16[3,160,512]{2,1,0:T(8,128)(2,1)S(1)} collective-permute-done((bf16[3,160,512]{2,1,0:T(8,128)(2,1)}, bf16[3,160,512]{2,1,0:T(8,128)(2,1)S(1)}, u32[]{:S(2)}, u32[]{:S(2)}) %collective-permute-start.16) | collective-permute-done | bytes 491552 | tf_op jit(solution)/shard_map/ppermute | solution.py:48
  64.0 1.7 %collective-permute-done.17.refs_5_ = bf16[3,160,512]{2,1,0:T(8,128)(2,1)S(1)} collective-permute-done((bf16[3,160,512]{2,1,0:T(8,128)(2,1)}, bf16[3,160,512]{2,1,0:T(8,128)(2,1)S(1)}, u32[]{:S(2)}, u32[]{:S(2)}) %collective-permute-start.17) | collective-permute-done | bytes 491552 | tf_op jit(solution)/shard_map/ppermute | solution.py:48
  65.6 4.9 %attend.1 = (bf16[768,512]{1,0:T(8,128)(2,1)S(1)}, bf16[512,512]{1,0:T(8,128)(2,1)}, s32[8]{0:T(128)S(1)}, s32[1]{0:T(128)}) custom-call(s32[1]{0:T(128)} %bitcast.8.place_ref, bf16[3,160,512]{2,1,0:T(8,128)(2,1)} %get-tuple-element.86.refs_0_, bf16[3,160,512]{2,1,0:T(8,128)(2,1)S(1)} %collective-permute-done.12.refs_1_, ...), custom_call_target="tpu_custom_call" | custom-call | flops 838860800 | bytes 5242880 | tf_op jit(solution)/shard_map/attend/pallas_call | solution.py:249
  70.5 0.5 collective-permute-start.18
  71.0 0.8 collective-permute-start.21
  71.8 1.5 collective-permute-start.23
  73.3 17.3 %collective-permute-done.20.refs_12_ = bf16[1024,640]{1,0:T(8,128)(2,1)} collective-permute-done((bf16[1024,640]{1,0:T(8,128)(2,1)S(1)}, bf16[1024,640]{1,0:T(8,128)(2,1)}, u32[]{:S(2)}, u32[]{:S(2)}) %collective-permute-start.20) | collective-permute-done | bytes 1310752 | tf_op jit(solution)/shard_map/ppermute | solution.py:140
  90.6 1.3 collective-permute-start.29
  91.9 1.8 %collective-permute-start.30 = (bf16[1024,640]{1,0:T(8,128)(2,1)}, bf16[1024,640]{1,0:T(8,128)(2,1)}, u32[]{:S(2)}, u32[]{:S(2)}) collective-permute-start(bf16[1024,640]{1,0:T(8,128)(2,1)} %collective-permute-done.19.refs_16_), channel_id=1, source_target_pairs={{2,3},{6,7},{10,11},{14,15},{18,19},{22,23},{26,27},{30,31}} | collective-permute-start | bytes 3932168 | tf_op jit(solution)/shard_map/ppermute | solution.py:140
  93.7 1.3 collective-permute-start.25
  95.0 0.9 collective-permute-start.26
  95.9 8.6 %collective-permute-done.25.refs_6_ = bf16[384,512]{1,0:T(8,128)(2,1)S(1)} collective-permute-done((bf16[384,512]{1,0:T(8,128)(2,1)S(1)}, bf16[384,512]{1,0:T(8,128)(2,1)S(1)}, u32[]{:S(2)}, u32[]{:S(2)}) %collective-permute-start.25) | collective-permute-done | bytes 393248 | tf_op jit(solution)/shard_map/ppermute | solution.py:48
  104.5 2.2 %collective-permute-done.26.refs_7_ = bf16[384,512]{1,0:T(8,128)(2,1)} collective-permute-done((bf16[384,512]{1,0:T(8,128)(2,1)S(1)}, bf16[384,512]{1,0:T(8,128)(2,1)}, u32[]{:S(2)}, u32[]{:S(2)}) %collective-permute-start.26) | collective-permute-done | bytes 393248 | tf_op jit(solution)/shard_map/ppermute | solution.py:48
  106.8 0.6 collective-permute-start.28
  107.3 0.3 copy-done.8
  108.2 0.4 collective-permute-done.27.refs_8_
  108.6 0.8 collective-permute-done.28.refs_9_
  109.4 13.8 %collective-permute-done.29.refs_11_ = bf16[1024,640]{1,0:T(8,128)(2,1)} collective-permute-done((bf16[1024,640]{1,0:T(8,128)(2,1)}, bf16[1024,640]{1,0:T(8,128)(2,1)}, u32[]{:S(2)}, u32[]{:S(2)}) %collective-permute-start.29) | collective-permute-done | bytes 1310752 | tf_op jit(solution)/shard_map/ppermute | solution.py:140
  123.2 0.0 copy-start.1
  123.2 8.9 %project.1 = (bf16[160,640]{1,0:T(8,128)(2,1)}, bf16[160,640]{1,0:T(8,128)(2,1)}, bf16[160,640]{1,0:T(8,128)(2,1)}, bf16[160,640]{1,0:T(8,128)(2,1)}, bf16[160,6...) custom-call(s32[1]{0:T(128)} %bitcast.8.place_ref, ...), custom_call_target="tpu_custom_call" | custom-call | flops 3355443200 | bytes 5242880 | tf_op jit(solution)/shard_map/project/pallas_call | solution.py:392
  132.1 0.1 collective-permute-start.31
  132.2 1.6 collective-permute-start.32
  133.8 0.3 collective-permute-start.33
  134.1 1.2 collective-permute-start.34
  135.3 0.5 collective-permute-start.35
  135.8 1.4 collective-permute-start.36
  137.2 3.2 %collective-permute-done.32.refs_2_ = bf16[160,640]{1,0:T(8,128)(2,1)S(1)} collective-permute-done((bf16[160,640]{1,0:T(8,128)(2,1)}, bf16[160,640]{1,0:T(8,128)(2,1)S(1)}, u32[]{:S(2)}, u32[]{:S(2)}) %collective-permute-start.32) | collective-permute-done | bytes 204832 | tf_op jit(solution)/shard_map/ppermute | solution.py:48
  140.4 0.2 collective-permute-start.37
  140.6 3.3 %collective-permute-done.33.refs_3_ = bf16[160,640]{1,0:T(8,128)(2,1)S(1)} collective-permute-done((bf16[160,640]{1,0:T(8,128)(2,1)}, bf16[160,640]{1,0:T(8,128)(2,1)S(1)}, u32[]{:S(2)}, u32[]{:S(2)}) %collective-permute-start.33) | collective-permute-done | bytes 204832 | tf_op jit(solution)/shard_map/ppermute | solution.py:48
  143.9 10.3 %collective-permute-done.35.refs_5_ = bf16[160,640]{1,0:T(8,128)(2,1)S(1)} collective-permute-done((bf16[160,640]{1,0:T(8,128)(2,1)}, bf16[160,640]{1,0:T(8,128)(2,1)S(1)}, u32[]{:S(2)}, u32[]{:S(2)}) %collective-permute-start.35) | collective-permute-done | bytes 204832 | tf_op jit(solution)/shard_map/ppermute | solution.py:48
  154.2 2.4 %assemble.1 = bf16[160,5120]{1,0:T(8,128)(2,1)} custom-call(s32[1]{0:T(128)} %bitcast.8.place_ref, s32[1,1]{1,0:T(1,128)S(6)} %copy.16.blocks_ref, s32[1,160]{1,0:T(1,128)S(1)} %copy-done.1, bf16[160,640]{1,0:T(8,128)(2,1)} %get-tuple-element.121.refs_0_, bf16[160,640]{1,0:T(8,128)(2,1)S(1)} %collective-permute-done.31.refs_1_, ...), custom_call_target="tpu_custom_call" | custom-call | bytes 3276800 | tf_op jit(solution)/shard_map/assemble/pallas_call | solution.py:436
  (38 shorter events, 0.2 us)
Async XLA Ops:
  5.7 45.0 %collective-permute-start.14 = (bf16[1024,640]{1,0:T(8,128)(2,1)}, bf16[1024,640]{1,0:T(8,128)(2,1)S(1)}, u32[]{:S(2)}, u32[]{:S(2)}) collective-permute-start(bf16[1024,640]{1,0:T(8,128)(2,1)} %get-tuple-element.117.refs_14_), channel_id=1, source_target_pairs={{0,1},{1,2},{2,3},{4,5},{5,6},{6,7},{8,9},{9,10},{10,11},{12,13},{... | collective-permute-start | bytes 3932168 | tf_op jit(solution)/shard_map/ppermute | solution.py:140
  10.7 40.0 %collective-permute-start.15 = (bf16[1024,640]{1,0:T(8,128)(2,1)}, bf16[1024,640]{1,0:T(8,128)(2,1)S(1)}, u32[]{:S(2)}, u32[]{:S(2)}) collective-permute-start(bf16[1024,640]{1,0:T(8,128)(2,1)} %get-tuple-element.117.refs_14_), channel_id=1, source_target_pairs={{1,0},{2,1},{3,2},{5,4},{6,5},{7,6},{9,8},{10,9},{11,10},{13,12},{... | collective-permute-start | bytes 3932168 | tf_op jit(solution)/shard_map/ppermute | solution.py:140
  12.0 14.4 %collective-permute-start.9 = (bf16[3,160,512]{2,1,0:T(8,128)(2,1)}, bf16[3,160,512]{2,1,0:T(8,128)(2,1)S(1)}, u32[]{:S(2)}, u32[]{:S(2)}) collective-permute-start(bf16[3,160,512]{2,1,0:T(8,128)(2,1)} %get-tuple-element.70), channel_id=1, source_target_pairs={{0,8},{4,12},{8,0},{12,4},{16,24},{20,28},{24,16},{28,20},{1,9},{5... | collective-permute-start | bytes 1474568 | tf_op jit(solution)/shard_map/ppermute | solution.py:48
  13.6 23.1 %collective-permute-start.10 = (bf16[3,160,512]{2,1,0:T(8,128)(2,1)}, bf16[3,160,512]{2,1,0:T(8,128)(2,1)S(1)}, u32[]{:S(2)}, u32[]{:S(2)}) collective-permute-start(bf16[3,160,512]{2,1,0:T(8,128)(2,1)} %get-tuple-element.71), channel_id=1, source_target_pairs={{0,16},{4,20},{8,24},{12,28},{16,0},{20,4},{24,8},{28,12},{1,17},{... | collective-permute-start | bytes 1474568 | tf_op jit(solution)/shard_map/ppermute | solution.py:48
  15.1 21.6 %collective-permute-start.11 = (bf16[3,160,512]{2,1,0:T(8,128)(2,1)}, bf16[3,160,512]{2,1,0:T(8,128)(2,1)S(1)}, u32[]{:S(2)}, u32[]{:S(2)}) collective-permute-start(bf16[3,160,512]{2,1,0:T(8,128)(2,1)} %get-tuple-element.72), channel_id=1, source_target_pairs={{0,24},{4,28},{8,16},{12,20},{16,8},{20,12},{24,0},{28,4},{1,25},{... | collective-permute-start | bytes 1474568 | tf_op jit(solution)/shard_map/ppermute | solution.py:48
  36.7 2.1 %collective-permute-start.12 = (bf16[3,160,512]{2,1,0:T(8,128)(2,1)}, bf16[3,160,512]{2,1,0:T(8,128)(2,1)S(1)}, u32[]{:S(2)}, u32[]{:S(2)}) collective-permute-start(bf16[3,160,512]{2,1,0:T(8,128)(2,1)} %get-tuple-element.78), channel_id=1, source_target_pairs={{0,4},{4,0},{8,12},{12,8},{16,20},{20,16},{24,28},{28,24},{1,5},{5... | collective-permute-start | bytes 1474568 | tf_op jit(solution)/shard_map/ppermute | solution.py:48
  36.8 14.0 %collective-permute-start.13 = (bf16[3,160,512]{2,1,0:T(8,128)(2,1)}, bf16[3,160,512]{2,1,0:T(8,128)(2,1)S(1)}, u32[]{:S(2)}, u32[]{:S(2)}) collective-permute-start(bf16[3,160,512]{2,1,0:T(8,128)(2,1)} %get-tuple-element.82), channel_id=1, source_target_pairs={{0,28},{4,24},{8,20},{12,16},{16,12},{20,8},{24,4},{28,0},{1,29},{... | collective-permute-start | bytes 1474568 | tf_op jit(solution)/shard_map/ppermute | solution.py:48
  50.7 56.0 %copy-start.5 = (bf16[1024,640]{1,0:T(8,128)(2,1)}, bf16[1024,640]{1,0:T(8,128)(2,1)S(1)}, u32[]{:S(2)}) copy-start(bf16[1024,640]{1,0:T(8,128)(2,1)S(1)} %collective-permute-done.14.refs_15_) | copy-start | bytes 3932164
  50.7 56.6 %copy-start.6 = (bf16[1024,640]{1,0:T(8,128)(2,1)}, bf16[1024,640]{1,0:T(8,128)(2,1)S(1)}, u32[]{:S(2)}) copy-start(bf16[1024,640]{1,0:T(8,128)(2,1)S(1)} %collective-permute-done.15.refs_13_) | copy-start | bytes 3932164
  50.8 13.2 %collective-permute-start.16 = (bf16[3,160,512]{2,1,0:T(8,128)(2,1)}, bf16[3,160,512]{2,1,0:T(8,128)(2,1)S(1)}, u32[]{:S(2)}, u32[]{:S(2)}) collective-permute-start(bf16[3,160,512]{2,1,0:T(8,128)(2,1)} %get-tuple-element.89), channel_id=1, source_target_pairs={{0,12},{4,8},{8,4},{12,0},{16,28},{20,24},{24,20},{28,16},{1,13},{... | collective-permute-start | bytes 1474568 | tf_op jit(solution)/shard_map/ppermute | solution.py:48
  52.1 13.5 %collective-permute-start.17 = (bf16[3,160,512]{2,1,0:T(8,128)(2,1)}, bf16[3,160,512]{2,1,0:T(8,128)(2,1)S(1)}, u32[]{:S(2)}, u32[]{:S(2)}) collective-permute-start(bf16[3,160,512]{2,1,0:T(8,128)(2,1)} %get-tuple-element.91), channel_id=1, source_target_pairs={{0,20},{4,16},{8,28},{12,24},{16,4},{20,0},{24,12},{28,8},{1,21},{... | collective-permute-start | bytes 1474568 | tf_op jit(solution)/shard_map/ppermute | solution.py:48
  52.6 20.7 %collective-permute-start.19 = (bf16[1024,640]{1,0:T(8,128)(2,1)S(1)}, bf16[1024,640]{1,0:T(8,128)(2,1)}, u32[]{:S(2)}, u32[]{:S(2)}) collective-permute-start(bf16[1024,640]{1,0:T(8,128)(2,1)S(1)} %collective-permute-done.14.refs_15_), channel_id=1, source_target_pairs={{1,2},{2,3},{5,6},{6,7},{9,10},{10,11},{13,14},{14,15},{17,18},{18... | collective-permute-start | bytes 3932168 | tf_op jit(solution)/shard_map/ppermute | solution.py:140
  54.4 36.2 %collective-permute-start.20 = (bf16[1024,640]{1,0:T(8,128)(2,1)S(1)}, bf16[1024,640]{1,0:T(8,128)(2,1)}, u32[]{:S(2)}, u32[]{:S(2)}) collective-permute-start(bf16[1024,640]{1,0:T(8,128)(2,1)S(1)} %collective-permute-done.15.refs_13_), channel_id=1, source_target_pairs={{1,0},{2,1},{5,4},{6,5},{9,8},{10,9},{13,12},{14,13},{17,16},{18,1... | collective-permute-start | bytes 3932168 | tf_op jit(solution)/shard_map/ppermute | solution.py:140
  70.5 24.5 %copy-start.2 = (s32[8]{0:T(128)}, s32[8]{0:T(128)S(1)}, u32[]{:S(2)}) copy-start(s32[8]{0:T(128)S(1)} %get-tuple-element.94.counts_ref) | copy-start | bytes 100
  70.5 52.7 %copy-start = (bf16[768,512]{1,0:T(8,128)(2,1)}, bf16[768,512]{1,0:T(8,128)(2,1)S(1)}, u32[]{:S(2)}) copy-start(bf16[768,512]{1,0:T(8,128)(2,1)S(1)} %get-tuple-element.102.refs_0_) | copy-start | bytes 2359300
  70.5 2.8 %collective-permute-start.18 = (bf16[768,512]{1,0:T(8,128)(2,1)S(1)}, bf16[768,512]{1,0:T(8,128)(2,1)S(1)}, u32[]{:S(2)}, u32[]{:S(2)}) collective-permute-start(bf16[768,512]{1,0:T(8,128)(2,1)S(1)} %get-tuple-element.102.refs_0_), channel_id=1, source_target_pairs={{0,4},{4,0},{8,12},{12,8},{16,20},{20,16},{24,28},{28,24},{1,5},{5... | collective-permute-start | bytes 2359304 | tf_op jit(solution)/shard_map/ppermute | solution.py:48
  71.0 22.7 %collective-permute-start.21 = (bf16[768,512]{1,0:T(8,128)(2,1)S(1)}, bf16[768,512]{1,0:T(8,128)(2,1)S(1)}, u32[]{:S(2)}, u32[]{:S(2)}) collective-permute-start(bf16[768,512]{1,0:T(8,128)(2,1)S(1)} %get-tuple-element.102.refs_0_), channel_id=1, source_target_pairs={{0,8},{4,12},{8,0},{12,4},{16,24},{20,28},{24,16},{28,20},{1,9},{5... | collective-permute-start | bytes 2359304 | tf_op jit(solution)/shard_map/ppermute | solution.py:48
  71.8 23.2 %collective-permute-start.23 = (bf16[768,512]{1,0:T(8,128)(2,1)S(1)}, bf16[768,512]{1,0:T(8,128)(2,1)S(1)}, u32[]{:S(2)}, u32[]{:S(2)}) collective-permute-start(bf16[768,512]{1,0:T(8,128)(2,1)S(1)} %get-tuple-element.102.refs_0_), channel_id=1, source_target_pairs={{0,16},{4,20},{8,24},{12,28},{16,0},{20,4},{24,8},{28,12},{1,17},{... | collective-permute-start | bytes 2359304 | tf_op jit(solution)/shard_map/ppermute | solution.py:48
  73.3 49.9 %copy-start.7 = (bf16[768,512]{1,0:T(8,128)(2,1)}, bf16[768,512]{1,0:T(8,128)(2,1)S(1)}, u32[]{:S(2)}) copy-start(bf16[768,512]{1,0:T(8,128)(2,1)S(1)} %collective-permute-done.18.refs_1_) | copy-start | bytes 2359300
  90.6 32.6 %collective-permute-start.29 = (bf16[1024,640]{1,0:T(8,128)(2,1)}, bf16[1024,640]{1,0:T(8,128)(2,1)}, u32[]{:S(2)}, u32[]{:S(2)}) collective-permute-start(bf16[1024,640]{1,0:T(8,128)(2,1)} %collective-permute-done.20.refs_12_), channel_id=1, source_target_pairs={{1,0},{5,4},{9,8},{13,12},{17,16},{21,20},{25,24},{29,28}} | collective-permute-start | bytes 3932168 | tf_op jit(solution)/shard_map/ppermute | solution.py:140
  91.9 31.3 %collective-permute-start.30 = (bf16[1024,640]{1,0:T(8,128)(2,1)}, bf16[1024,640]{1,0:T(8,128)(2,1)}, u32[]{:S(2)}, u32[]{:S(2)}) collective-permute-start(bf16[1024,640]{1,0:T(8,128)(2,1)} %collective-permute-done.19.refs_16_), channel_id=1, source_target_pairs={{2,3},{6,7},{10,11},{14,15},{18,19},{22,23},{26,27},{30,31}} | collective-permute-start | bytes 3932168 | tf_op jit(solution)/shard_map/ppermute | solution.py:140
  93.7 29.5 %copy-start.3 = (bf16[768,512]{1,0:T(8,128)(2,1)}, bf16[768,512]{1,0:T(8,128)(2,1)S(1)}, u32[]{:S(2)}) copy-start(bf16[768,512]{1,0:T(8,128)(2,1)S(1)} %collective-permute-done.21.refs_2_) | copy-start | bytes 2359300
  93.7 10.8 %collective-permute-start.25 = (bf16[384,512]{1,0:T(8,128)(2,1)S(1)}, bf16[384,512]{1,0:T(8,128)(2,1)S(1)}, u32[]{:S(2)}, u32[]{:S(2)}) collective-permute-start(bf16[384,512]{1,0:T(8,128)(2,1)S(1)} %slice.16), channel_id=1, source_target_pairs={{0,16},{4,20},{8,24},{12,28},{16,0},{20,4},{24,8},{28,12},{1,17},{... | collective-permute-start | bytes 1179656 | tf_op jit(solution)/shard_map/ppermute | solution.py:48
  95.0 11.7 %collective-permute-start.22 = (bf16[768,512]{1,0:T(8,128)(2,1)S(1)}, bf16[768,512]{1,0:T(8,128)(2,1)S(1)}, u32[]{:S(2)}, u32[]{:S(2)}) collective-permute-start(bf16[768,512]{1,0:T(8,128)(2,1)S(1)} %collective-permute-done.21.refs_2_), channel_id=1, source_target_pairs={{0,4},{4,0},{8,12},{12,8},{16,20},{20,16},{24,28},{28,24},{1,5},{5... | collective-permute-start | bytes 2359304 | tf_op jit(solution)/shard_map/ppermute | solution.py:48
  95.0 28.2 %copy-start.4 = (bf16[768,512]{1,0:T(8,128)(2,1)}, bf16[768,512]{1,0:T(8,128)(2,1)S(1)}, u32[]{:S(2)}) copy-start(bf16[768,512]{1,0:T(8,128)(2,1)S(1)} %collective-permute-done.23.refs_4_) | copy-start | bytes 2359300
  95.0 11.7 %collective-permute-start.26 = (bf16[384,512]{1,0:T(8,128)(2,1)S(1)}, bf16[384,512]{1,0:T(8,128)(2,1)}, u32[]{:S(2)}, u32[]{:S(2)}) collective-permute-start(bf16[384,512]{1,0:T(8,128)(2,1)S(1)} %slice.17), channel_id=1, source_target_pairs={{0,8},{4,12},{8,0},{12,4},{16,24},{20,28},{24,16},{28,20},{1,9},{5... | collective-permute-start | bytes 1179656 | tf_op jit(solution)/shard_map/ppermute | solution.py:48
  104.5 18.7 %copy-start.9 = (bf16[384,512]{1,0:T(8,128)(2,1)}, bf16[384,512]{1,0:T(8,128)(2,1)S(1)}, u32[]{:S(2)}) copy-start(bf16[384,512]{1,0:T(8,128)(2,1)S(1)} %collective-permute-done.25.refs_6_) | copy-start | bytes 1179652
  104.5 3.7 %collective-permute-start.24 = (bf16[768,512]{1,0:T(8,128)(2,1)S(1)}, bf16[768,512]{1,0:T(8,128)(2,1)}, u32[]{:S(2)}, u32[]{:S(2)}) collective-permute-start(bf16[768,512]{1,0:T(8,128)(2,1)S(1)} %collective-permute-done.23.refs_4_), channel_id=1, source_target_pairs={{0,4},{4,0},{8,12},{12,8},{16,20},{20,16},{24,28},{28,24},{1,5},{5... | collective-permute-start | bytes 2359304 | tf_op jit(solution)/shard_map/ppermute | solution.py:48
  106.7 1.9 %collective-permute-start.27 = (bf16[384,512]{1,0:T(8,128)(2,1)S(1)}, bf16[384,512]{1,0:T(8,128)(2,1)}, u32[]{:S(2)}, u32[]{:S(2)}) collective-permute-start(bf16[384,512]{1,0:T(8,128)(2,1)S(1)} %collective-permute-done.25.refs_6_), channel_id=1, source_target_pairs={{0,4},{4,0},{8,12},{12,8},{16,20},{20,16},{24,28},{28,24},{1,5},{5... | collective-permute-start | bytes 1179656 | tf_op jit(solution)/shard_map/ppermute | solution.py:48
  106.7 0.9 copy-start.8
  106.8 2.6 %collective-permute-start.28 = (bf16[384,512]{1,0:T(8,128)(2,1)}, bf16[384,512]{1,0:T(8,128)(2,1)}, u32[]{:S(2)}, u32[]{:S(2)}) collective-permute-start(bf16[384,512]{1,0:T(8,128)(2,1)} %collective-permute-done.26.refs_7_), channel_id=1, source_target_pairs={{0,4},{4,0},{8,12},{12,8},{16,20},{20,16},{24,28},{28,24},{1,5},{5... | collective-permute-start | bytes 1179656 | tf_op jit(solution)/shard_map/ppermute | solution.py:48
  123.2 31.0 %copy-start.1 = (s32[1,160]{1,0:T(1,128)S(1)}, s32[1,160]{1,0:T(1,128)}, u32[]{:S(2)}) copy-start(s32[1,160]{1,0:T(1,128)} %mask_ref.3) | copy-start | bytes 1924
  132.1 3.6 %collective-permute-start.31 = (bf16[160,640]{1,0:T(8,128)(2,1)}, bf16[160,640]{1,0:T(8,128)(2,1)S(1)}, u32[]{:S(2)}, u32[]{:S(2)}) collective-permute-start(bf16[160,640]{1,0:T(8,128)(2,1)} %get-tuple-element.122), channel_id=1, source_target_pairs={{0,4},{4,0},{8,12},{12,8},{16,20},{20,16},{24,28},{28,24},{1,5},{5... | collective-permute-start | bytes 614408 | tf_op jit(solution)/shard_map/ppermute | solution.py:48
  132.2 8.2 %collective-permute-start.32 = (bf16[160,640]{1,0:T(8,128)(2,1)}, bf16[160,640]{1,0:T(8,128)(2,1)S(1)}, u32[]{:S(2)}, u32[]{:S(2)}) collective-permute-start(bf16[160,640]{1,0:T(8,128)(2,1)} %get-tuple-element.123), channel_id=1, source_target_pairs={{0,8},{4,12},{8,0},{12,4},{16,24},{20,28},{24,16},{28,20},{1,9},{5... | collective-permute-start | bytes 614408 | tf_op jit(solution)/shard_map/ppermute | solution.py:48
  133.8 10.1 %collective-permute-start.33 = (bf16[160,640]{1,0:T(8,128)(2,1)}, bf16[160,640]{1,0:T(8,128)(2,1)S(1)}, u32[]{:S(2)}, u32[]{:S(2)}) collective-permute-start(bf16[160,640]{1,0:T(8,128)(2,1)} %get-tuple-element.124), channel_id=1, source_target_pairs={{0,12},{4,8},{8,4},{12,0},{16,28},{20,24},{24,20},{28,16},{1,13},{... | collective-permute-start | bytes 614408 | tf_op jit(solution)/shard_map/ppermute | solution.py:48
  134.1 9.8 %collective-permute-start.34 = (bf16[160,640]{1,0:T(8,128)(2,1)}, bf16[160,640]{1,0:T(8,128)(2,1)S(1)}, u32[]{:S(2)}, u32[]{:S(2)}) collective-permute-start(bf16[160,640]{1,0:T(8,128)(2,1)} %get-tuple-element.125), channel_id=1, source_target_pairs={{0,16},{4,20},{8,24},{12,28},{16,0},{20,4},{24,8},{28,12},{1,17},{... | collective-permute-start | bytes 614408 | tf_op jit(solution)/shard_map/ppermute | solution.py:48
  135.3 18.9 %collective-permute-start.35 = (bf16[160,640]{1,0:T(8,128)(2,1)}, bf16[160,640]{1,0:T(8,128)(2,1)S(1)}, u32[]{:S(2)}, u32[]{:S(2)}) collective-permute-start(bf16[160,640]{1,0:T(8,128)(2,1)} %get-tuple-element.126), channel_id=1, source_target_pairs={{0,20},{4,16},{8,28},{12,24},{16,4},{20,0},{24,12},{28,8},{1,21},{... | collective-permute-start | bytes 614408 | tf_op jit(solution)/shard_map/ppermute | solution.py:48
  135.8 18.4 %collective-permute-start.36 = (bf16[160,640]{1,0:T(8,128)(2,1)}, bf16[160,640]{1,0:T(8,128)(2,1)S(1)}, u32[]{:S(2)}, u32[]{:S(2)}) collective-permute-start(bf16[160,640]{1,0:T(8,128)(2,1)} %get-tuple-element.127), channel_id=1, source_target_pairs={{0,24},{4,28},{8,16},{12,20},{16,8},{20,12},{24,0},{28,4},{1,25},{... | collective-permute-start | bytes 614408 | tf_op jit(solution)/shard_map/ppermute | solution.py:48
  140.4 13.8 %collective-permute-start.37 = (bf16[160,640]{1,0:T(8,128)(2,1)}, bf16[160,640]{1,0:T(8,128)(2,1)S(1)}, u32[]{:S(2)}, u32[]{:S(2)}) collective-permute-start(bf16[160,640]{1,0:T(8,128)(2,1)} %get-tuple-element.128), channel_id=1, source_target_pairs={{0,28},{4,24},{8,20},{12,16},{16,12},{20,8},{24,4},{28,0},{1,29},{... | collective-permute-start | bytes 614408 | tf_op jit(solution)/shard_map/ppermute | solution.py:48

commit v2 on v1

--- a/solution.py
+++ b/solution.py
@@ -48,29 +48,43 @@
     return lax.ppermute(array, "cam", [(place, place ^ mask) for place in range(count)])
 
 
-def pack(place, block_counts, row_mask, queries, keys, values, out_weight, count):
+def cut_weight(place, out_weight, count):
+    depth = out_weight.shape[0]
+    columns = out_weight.shape[1] // count
+    if columns % HEAD_DIM:
+        return lax.dynamic_slice_in_dim(out_weight, place[0] * columns, columns, axis=1)
+    step = depth // 4
+
+    def body(place_ref, w_ref, out_ref):
+        out_ref[...] = w_ref[...]
+
+    return pl.pallas_call(
+        body,
+        grid_spec=pltpu.PrefetchScalarGridSpec(
+            num_scalar_prefetch=1,
+            grid=(depth // step,),
+            in_specs=[pl.BlockSpec((step, columns), lambda i, place_ref: (i, place_ref[0]))],
+            out_specs=pl.BlockSpec((step, columns), lambda i, place_ref: (i, 0)),
+        ),
+        out_shape=jax.ShapeDtypeStruct((depth, columns), jnp.bfloat16),
+        compiler_params=params(56),
+        cost_estimate=pl.CostEstimate(
+            flops=0, bytes_accessed=4 * depth * columns, transcendentals=0
+        ),
+        name="cut_weight",
+    )(place, out_weight)
+
+
+def pack(place, block_counts, row_mask, queries, keys, values, count):
     _, rows, features = queries.shape
     width = features // count
-    depth = out_weight.shape[0]
-    columns = out_weight.shape[1] // count
-    slicing = columns % HEAD_DIM == 0
-    chunks = 1 if slicing else 0
-    staged = columns if slicing else HEAD_DIM
-
-    def body(place_ref, blocks_ref, mask_ref, q_ref, k_ref, v_ref, w_ref, *refs):
+
+    def body(place_ref, blocks_ref, mask_ref, q_ref, k_ref, v_ref, *refs):
         out_refs = refs[:count]
-        weight_refs = refs[count : count + chunks]
-        held, key_out, w_held, load_sems, sems, weight_sems = refs[count + chunks :]
+        held, key_out, load_sems, sems = refs[count:]
         loads = []
         for slot, ref in enumerate((k_ref, q_ref, v_ref)):
             load = pltpu.make_async_copy(ref.at[0], held.at[slot], load_sems.at[slot])
-            load.start()
-            loads.append(load)
-        if chunks:
-            start = pl.multiple_of(place_ref[0] * columns, HEAD_DIM)
-            load = pltpu.make_async_copy(
-                w_ref.at[:, pl.ds(start, columns)], w_held, load_sems.at[3]
-            )
             load.start()
             loads.append(load)
         starts = [pl.multiple_of((place_ref[0] ^ m) * width, HEAD_DIM) for m in range(count)]
@@ -92,41 +106,31 @@
             for mask in range(count):
                 source = held.at[slot, :, pl.ds(starts[mask], width)]
                 send(source, out_refs[mask].at[target], sems.at[mask, target])
-        if chunks:
-            loads[3].wait()
-            send(w_held, weight_refs[0], weight_sems.at[0])
         for copy in copies:
             copy.wait()
 
     any_spec = pl.BlockSpec(memory_space=pl.ANY)
-    weight_shapes = [jax.ShapeDtypeStruct((depth, columns), jnp.bfloat16)] * chunks
-    outputs = pl.pallas_call(
+    return pl.pallas_call(
         body,
         grid_spec=pltpu.PrefetchScalarGridSpec(
             num_scalar_prefetch=2,
             grid=(1,),
-            in_specs=[full_spec((1, rows))] + [any_spec] * 4,
-            out_specs=[any_spec] * (count + chunks),
+            in_specs=[full_spec((1, rows))] + [any_spec] * 3,
+            out_specs=[any_spec] * count,
             scratch_shapes=[
                 pltpu.VMEM((3, rows, features), jnp.bfloat16),
                 pltpu.VMEM((count, rows, width), jnp.bfloat16),
-                pltpu.VMEM((depth, staged), jnp.bfloat16),
-                pltpu.SemaphoreType.DMA((4,)),
+                pltpu.SemaphoreType.DMA((3,)),
                 pltpu.SemaphoreType.DMA((count, 3)),
-                pltpu.SemaphoreType.DMA((1,)),
             ],
         ),
-        out_shape=[jax.ShapeDtypeStruct((3, rows, width), jnp.bfloat16)] * count + weight_shapes,
+        out_shape=[jax.ShapeDtypeStruct((3, rows, width), jnp.bfloat16)] * count,
         compiler_params=params(56),
         cost_estimate=pl.CostEstimate(
             flops=0, bytes_accessed=12 * rows * features, transcendentals=0
         ),
         name="pack",
-    )(place, block_counts, row_mask, queries, keys, values, out_weight)
-    if slicing:
-        return list(outputs[:count]), outputs[count]
-    start = place[0] * columns
-    return list(outputs[:count]), lax.dynamic_slice_in_dim(out_weight, start, columns, axis=1)
+    )(place, block_counts, row_mask, queries, keys, values)
 
 
 def pass_weight(shards, distance):
@@ -463,10 +467,9 @@
     place_array = jnp.full((1,), lax.axis_index("cam"), jnp.int32)
     group_array = jnp.full((1,), lax.axis_index("fsdp"), jnp.int32)
 
-    payloads, weight_part = pack(
-        place_array, block_counts, row_mask, queries, keys, values, out_weight, count
-    )
-    shards = {0: weight_part}
+    shards = {0: cut_weight(place_array, out_weight, count)}
+    queries, shards[0] = lax.optimization_barrier((queries, shards[0]))
+    payloads = pack(place_array, block_counts, row_mask, queries, keys, values, count)
     groups = lax.axis_size("fsdp")
 
     received = [payloads[0]] + [None] * (count - 1)
@@ -475,14 +478,11 @@
     pass_weight(shards, 1)
     for mask in early:
         received[mask] = xor_permute(payloads[mask], mask, count)
-    received, payloads = lax.optimization_barrier((received, payloads))
-    for mask in (late[0], 1):
-        received[mask] = xor_permute(payloads[mask], mask, count)
     received, payloads, shards[1], shards[-1] = lax.optimization_barrier(
         (received, payloads, shards[1], shards[-1])
     )
     pass_weight(shards, 2)
-    for mask in late[1:-1]:
+    for mask in late:
         received[mask] = xor_permute(payloads[mask], mask, count)
     always = total * 3 // 5
     attended, rest, counts, used = attend(

time: 157 us -> 147 us (0.936)
  waiting for transfers between devices: 103 us -> 88 us
  Pallas kernels: 21.2 us -> 25.6 us
  starting transfers between devices: 30.2 us -> 31.8 us
    ppermute x6, waiting for transfers between devices: 31.1 us -> 12.3 us  [pass_weight(): lax.ppermute(shards[sign * (distance - 1)], 'fsdp', pairs)]
    ppermute x23, waiting for transfers between devices: 72.2 us -> 75.7 us  [xor_permute(): lax.ppermute(array, 'cam', [(place, place ^ mask) for place in range(coun...]
    pallas_call x0 -> x1, Pallas kernels: none -> 3.47 us  [cut_weight(): pl.pallas_call(body, grid_spec=pltpu.PrefetchScalarGridSpec(num_scalar_pr...]
    ppermute x23, starting transfers between devices: 17.8 us -> 19.5 us  [xor_permute(): lax.ppermute(array, 'cam', [(place, place ^ mask) for place in range(coun...]
  transfers between devices with their start and end apart: 29 -> 29, of which waited for: 15 -> 15; matrix products, arithmetic and copies ran while one was open for 0% -> 0% of each run, Pallas kernels for 3% -> 7%
where the time goes in v2:
time: 147 us
  waiting for transfers between devices  88 us (60%)
  starting transfers between devices  31.8 us (22%)
  Pallas kernels  25.6 us (17%)
    ppermute x23, waiting for transfers between devices, xor_permute(): lax.ppermute(array, 'cam', [(place, place ^ mask) for place in range(coun...  75.7 us
    ppermute x23, starting transfers between devices, xor_permute(): lax.ppermute(array, 'cam', [(place, place ^ mask) for place in range(coun...  19.5 us
    ppermute x6, starting transfers between devices, pass_weight(): lax.ppermute(shards[sign * (distance - 1)], 'fsdp', pairs)  12.4 us
    ppermute x6, waiting for transfers between devices, pass_weight(): lax.ppermute(shards[sign * (distance - 1)], 'fsdp', pairs)  12.3 us
    pallas_call x1, Pallas kernels, project(): pl.pallas_call(body, grid_spec=pltpu.PrefetchScalarGridSpec(num_scalar_pr...  9.78 us
    pallas_call x1, Pallas kernels, attend(): pl.pallas_call(body, grid_spec=pltpu.PrefetchScalarGridSpec(num_scalar_pr...  5.7 us
    pallas_call x1, Pallas kernels, pack(): pl.pallas_call(body, grid_spec=pltpu.PrefetchScalarGridSpec(num_scalar_pr...  4.22 us
    pallas_call x1, Pallas kernels, cut_weight(): pl.pallas_call(body, grid_spec=pltpu.PrefetchScalarGridSpec(num_scalar_pr...  3.47 us
  transfers between devices with their start and end apart: 29, of which 15 were waited for; matrix products, arithmetic and copies ran while one was open for 0% of the time, Pallas kernels for 7%

profile of v2, /device:TPU:0, one launch (start us, length us, event | category | flops | bytes accessed | tf_op | source)
XLA Modules:
  0.0 147.2 jit_solution(17027486973465521428)
XLA Ops:
  0.0 3.5 %cut_weight.1.refs_14_ = bf16[1024,640]{1,0:T(8,128)(2,1)} custom-call(s32[1]{0:T(128)} %bitcast.8.place_ref, bf16[1024,5120]{1,0:T(8,128)(2,1)} %w_ref.1), custom_call_target="tpu_custom_call" | custom-call | bytes 2621440 | tf_op jit(solution)/shard_map/cut_weight/pallas_call | solution.py:61
  3.5 5.0 %collective-permute-start.12 = (bf16[1024,640]{1,0:T(8,128)(2,1)}, bf16[1024,640]{1,0:T(8,128)(2,1)S(1)}, u32[]{:S(2)}, u32[]{:S(2)}) collective-permute-start(bf16[1024,640]{1,0:T(8,128)(2,1)} %cut_weight.1.refs_14_), channel_id=1, source_target_pairs={{0,1},{1,2},{2,3},{4,5},{5,6},{6,7},{8,9},{9,10},{10,11},{12,13},{... | collective-permute-start | bytes 3932168 | tf_op jit(solution)/shard_map/ppermute | solution.py:144
  8.5 1.3 collective-permute-start.13
  10.4 4.2 %pack.1 = (bf16[3,160,512]{2,1,0:T(8,128)(2,1)}, bf16[3,160,512]{2,1,0:T(8,128)(2,1)}, bf16[3,160,512]{2,1,0:T(8,128)(2,1)}, bf16[3,160,512]{2,1,0:T(8,128)(2,1)...) custom-call(s32[1]{0:T(128)} %bitcast.8.place_ref, ...), custom_call_target="tpu_custom_call" | custom-call | bytes 7864320 | tf_op jit(solution)/shard_map/pack/pallas_call | solution.py:113
  14.7 1.6 %collective-permute-start.9 = (bf16[3,160,512]{2,1,0:T(8,128)(2,1)}, bf16[3,160,512]{2,1,0:T(8,128)(2,1)S(1)}, u32[]{:S(2)}, u32[]{:S(2)}) collective-permute-start(bf16[3,160,512]{2,1,0:T(8,128)(2,1)} %get-tuple-element.64), channel_id=1, source_target_pairs={{0,8},{4,12},{8,0},{12,4},{16,24},{20,28},{24,16},{28,20},{1,9},{5... | collective-permute-start | bytes 1474568 | tf_op jit(solution)/shard_map/ppermute | solution.py:48
  16.2 1.5 %collective-permute-start.10 = (bf16[3,160,512]{2,1,0:T(8,128)(2,1)}, bf16[3,160,512]{2,1,0:T(8,128)(2,1)S(1)}, u32[]{:S(2)}, u32[]{:S(2)}) collective-permute-start(bf16[3,160,512]{2,1,0:T(8,128)(2,1)} %get-tuple-element.65), channel_id=1, source_target_pairs={{0,16},{4,20},{8,24},{12,28},{16,0},{20,4},{24,8},{28,12},{1,17},{... | collective-permute-start | bytes 1474568 | tf_op jit(solution)/shard_map/ppermute | solution.py:48
  17.7 0.5 collective-permute-start.11
  18.2 10.9 %collective-permute-done.9.refs_2_ = bf16[3,160,512]{2,1,0:T(8,128)(2,1)S(1)} collective-permute-done((bf16[3,160,512]{2,1,0:T(8,128)(2,1)}, bf16[3,160,512]{2,1,0:T(8,128)(2,1)S(1)}, u32[]{:S(2)}, u32[]{:S(2)}) %collective-permute-start.9) | collective-permute-done | bytes 491552 | tf_op jit(solution)/shard_map/ppermute | solution.py:48
  29.1 10.3 %collective-permute-done.10.refs_4_ = bf16[3,160,512]{2,1,0:T(8,128)(2,1)S(1)} collective-permute-done((bf16[3,160,512]{2,1,0:T(8,128)(2,1)}, bf16[3,160,512]{2,1,0:T(8,128)(2,1)S(1)}, u32[]{:S(2)}, u32[]{:S(2)}) %collective-permute-start.10) | collective-permute-done | bytes 491552 | tf_op jit(solution)/shard_map/ppermute | solution.py:48
  39.4 1.5 collective-permute-done.13.refs_13_
  40.8 1.6 %collective-permute-start.15 = (bf16[3,160,512]{2,1,0:T(8,128)(2,1)}, bf16[3,160,512]{2,1,0:T(8,128)(2,1)S(1)}, u32[]{:S(2)}, u32[]{:S(2)}) collective-permute-start(bf16[3,160,512]{2,1,0:T(8,128)(2,1)} %get-tuple-element.75), channel_id=1, source_target_pairs={{0,12},{4,8},{8,4},{12,0},{16,28},{20,24},{24,20},{28,16},{1,13},{... | collective-permute-start | bytes 1474568 | tf_op jit(solution)/shard_map/ppermute | solution.py:48
  42.4 1.1 collective-permute-start.16
  43.6 0.6 collective-permute-start.17
  44.1 1.7 %collective-permute-start.19 = (bf16[1024,640]{1,0:T(8,128)(2,1)S(1)}, bf16[1024,640]{1,0:T(8,128)(2,1)}, u32[]{:S(2)}, u32[]{:S(2)}) collective-permute-start(bf16[1024,640]{1,0:T(8,128)(2,1)S(1)} %collective-permute-done.12.refs_15_), channel_id=1, source_target_pairs={{1,2},{2,3},{5,6},{6,7},{9,10},{10,11},{13,14},{14,15},{17,18},{18... | collective-permute-start | bytes 3932168 | tf_op jit(solution)/shard_map/ppermute | solution.py:144
  45.9 0.0 collective-permute-done.14.refs_1_
  45.9 1.3 collective-permute-start.20
  47.2 7.2 %collective-permute-done.15.refs_3_ = bf16[3,160,512]{2,1,0:T(8,128)(2,1)S(1)} collective-permute-done((bf16[3,160,512]{2,1,0:T(8,128)(2,1)}, bf16[3,160,512]{2,1,0:T(8,128)(2,1)S(1)}, u32[]{:S(2)}, u32[]{:S(2)}) %collective-permute-start.15) | collective-permute-done | bytes 491552 | tf_op jit(solution)/shard_map/ppermute | solution.py:48
  54.3 12.2 %collective-permute-done.16.refs_5_ = bf16[3,160,512]{2,1,0:T(8,128)(2,1)S(1)} collective-permute-done((bf16[3,160,512]{2,1,0:T(8,128)(2,1)}, bf16[3,160,512]{2,1,0:T(8,128)(2,1)S(1)}, u32[]{:S(2)}, u32[]{:S(2)}) %collective-permute-start.16) | collective-permute-done | bytes 491552 | tf_op jit(solution)/shard_map/ppermute | solution.py:48
  66.5 5.7 %attend.1 = (bf16[768,512]{1,0:T(8,128)(2,1)S(1)}, bf16[512,512]{1,0:T(8,128)(2,1)}, s32[8]{0:T(128)S(1)}, s32[1]{0:T(128)}) custom-call(s32[1]{0:T(128)} %bitcast.8.place_ref, bf16[3,160,512]{2,1,0:T(8,128)(2,1)} %get-tuple-element.72.refs_0_, bf16[3,160,512]{2,1,0:T(8,128)(2,1)S(1)} %collective-permute-done.14.refs_1_, ...), custom_call_target="tpu_custom_call" | custom-call | flops 838860800 | bytes 5242880 | tf_op jit(solution)/shard_map/attend/pallas_call | solution.py:253
  72.2 0.4 collective-permute-start.18
  72.7 0.4 collective-permute-start.21
  73.1 1.6 %collective-permute-start.23 = (bf16[768,512]{1,0:T(8,128)(2,1)S(1)}, bf16[768,512]{1,0:T(8,128)(2,1)S(1)}, u32[]{:S(2)}, u32[]{:S(2)}) collective-permute-start(bf16[768,512]{1,0:T(8,128)(2,1)S(1)} %get-tuple-element.88.refs_0_), channel_id=1, source_target_pairs={{0,16},{4,20},{8,24},{12,28},{16,0},{20,4},{24,8},{28,12},{1,17},{... | collective-permute-start | bytes 2359304 | tf_op jit(solution)/shard_map/ppermute | solution.py:48
  74.7 6.1 %collective-permute-done.20.refs_12_ = bf16[1024,640]{1,0:T(8,128)(2,1)} collective-permute-done((bf16[1024,640]{1,0:T(8,128)(2,1)S(1)}, bf16[1024,640]{1,0:T(8,128)(2,1)}, u32[]{:S(2)}, u32[]{:S(2)}) %collective-permute-start.20) | collective-permute-done | bytes 1310752 | tf_op jit(solution)/shard_map/ppermute | solution.py:144
  80.8 1.3 collective-permute-start.29
  82.1 1.8 %collective-permute-start.30 = (bf16[1024,640]{1,0:T(8,128)(2,1)}, bf16[1024,640]{1,0:T(8,128)(2,1)}, u32[]{:S(2)}, u32[]{:S(2)}) collective-permute-start(bf16[1024,640]{1,0:T(8,128)(2,1)} %collective-permute-done.19.refs_16_), channel_id=1, source_target_pairs={{2,3},{6,7},{10,11},{14,15},{18,19},{22,23},{26,27},{30,31}} | collective-permute-start | bytes 3932168 | tf_op jit(solution)/shard_map/ppermute | solution.py:144
  83.9 8.3 %collective-permute-done.21.refs_2_ = bf16[768,512]{1,0:T(8,128)(2,1)S(1)} collective-permute-done((bf16[768,512]{1,0:T(8,128)(2,1)S(1)}, bf16[768,512]{1,0:T(8,128)(2,1)S(1)}, u32[]{:S(2)}, u32[]{:S(2)}) %collective-permute-start.21) | collective-permute-done | bytes 786464 | tf_op jit(solution)/shard_map/ppermute | solution.py:48
  92.2 1.6 %collective-permute-start.25 = (bf16[384,512]{1,0:T(8,128)(2,1)S(1)}, bf16[384,512]{1,0:T(8,128)(2,1)S(1)}, u32[]{:S(2)}, u32[]{:S(2)}) collective-permute-start(bf16[384,512]{1,0:T(8,128)(2,1)S(1)} %slice.16), channel_id=1, source_target_pairs={{0,16},{4,20},{8,24},{12,28},{16,0},{20,4},{24,8},{28,12},{1,17},{... | collective-permute-start | bytes 1179656 | tf_op jit(solution)/shard_map/ppermute | solution.py:48
  93.9 0.6 collective-permute-start.26
  94.5 8.2 %collective-permute-done.25.refs_6_ = bf16[384,512]{1,0:T(8,128)(2,1)S(1)} collective-permute-done((bf16[384,512]{1,0:T(8,128)(2,1)S(1)}, bf16[384,512]{1,0:T(8,128)(2,1)S(1)}, u32[]{:S(2)}, u32[]{:S(2)}) %collective-permute-start.25) | collective-permute-done | bytes 393248 | tf_op jit(solution)/shard_map/ppermute | solution.py:48
  102.7 2.9 %collective-permute-done.26.refs_7_ = bf16[384,512]{1,0:T(8,128)(2,1)} collective-permute-done((bf16[384,512]{1,0:T(8,128)(2,1)S(1)}, bf16[384,512]{1,0:T(8,128)(2,1)}, u32[]{:S(2)}, u32[]{:S(2)}) %collective-permute-start.26) | collective-permute-done | bytes 393248 | tf_op jit(solution)/shard_map/ppermute | solution.py:48
  105.6 0.6 collective-permute-start.28
  106.1 0.3 copy-done.8
  107.0 0.4 collective-permute-done.27.refs_8_
  107.4 0.8 collective-permute-done.28.refs_9_
  108.2 4.7 %collective-permute-done.29.refs_11_ = bf16[1024,640]{1,0:T(8,128)(2,1)} collective-permute-done((bf16[1024,640]{1,0:T(8,128)(2,1)}, bf16[1024,640]{1,0:T(8,128)(2,1)}, u32[]{:S(2)}, u32[]{:S(2)}) %collective-permute-start.29) | collective-permute-done | bytes 1310752 | tf_op jit(solution)/shard_map/ppermute | solution.py:144
  113.0 0.0 copy-start.1
  113.0 9.8 %project.1 = (bf16[160,640]{1,0:T(8,128)(2,1)}, bf16[160,640]{1,0:T(8,128)(2,1)}, bf16[160,640]{1,0:T(8,128)(2,1)}, bf16[160,640]{1,0:T(8,128)(2,1)}, bf16[160,6...) custom-call(s32[1]{0:T(128)} %bitcast.8.place_ref, ...), custom_call_target="tpu_custom_call" | custom-call | flops 3355443200 | bytes 5242880 | tf_op jit(solution)/shard_map/project/pallas_call | solution.py:396
  122.7 0.1 collective-permute-start.31
  122.8 1.6 %collective-permute-start.32 = (bf16[160,640]{1,0:T(8,128)(2,1)}, bf16[160,640]{1,0:T(8,128)(2,1)S(1)}, u32[]{:S(2)}, u32[]{:S(2)}) collective-permute-start(bf16[160,640]{1,0:T(8,128)(2,1)} %get-tuple-element.109), channel_id=1, source_target_pairs={{0,8},{4,12},{8,0},{12,4},{16,24},{20,28},{24,16},{28,20},{1,9},{5... | collective-permute-start | bytes 614408 | tf_op jit(solution)/shard_map/ppermute | solution.py:48
  124.4 0.3 collective-permute-start.33
  124.7 1.5 %collective-permute-start.34 = (bf16[160,640]{1,0:T(8,128)(2,1)}, bf16[160,640]{1,0:T(8,128)(2,1)S(1)}, u32[]{:S(2)}, u32[]{:S(2)}) collective-permute-start(bf16[160,640]{1,0:T(8,128)(2,1)} %get-tuple-element.111), channel_id=1, source_target_pairs={{0,16},{4,20},{8,24},{12,28},{16,0},{20,4},{24,8},{28,12},{1,17},{... | collective-permute-start | bytes 614408 | tf_op jit(solution)/shard_map/ppermute | solution.py:48
  126.2 0.2 collective-permute-start.35
  126.4 2.4 %collective-permute-start.36 = (bf16[160,640]{1,0:T(8,128)(2,1)}, bf16[160,640]{1,0:T(8,128)(2,1)S(1)}, u32[]{:S(2)}, u32[]{:S(2)}) collective-permute-start(bf16[160,640]{1,0:T(8,128)(2,1)} %get-tuple-element.113), channel_id=1, source_target_pairs={{0,24},{4,28},{8,16},{12,20},{16,8},{20,12},{24,0},{28,4},{1,25},{... | collective-permute-start | bytes 614408 | tf_op jit(solution)/shard_map/ppermute | solution.py:48
  128.8 2.1 %collective-permute-done.32.refs_2_ = bf16[160,640]{1,0:T(8,128)(2,1)S(1)} collective-permute-done((bf16[160,640]{1,0:T(8,128)(2,1)}, bf16[160,640]{1,0:T(8,128)(2,1)S(1)}, u32[]{:S(2)}, u32[]{:S(2)}) %collective-permute-start.32) | collective-permute-done | bytes 204832 | tf_op jit(solution)/shard_map/ppermute | solution.py:48
  131.0 1.3 collective-permute-start.37
  132.2 2.2 %collective-permute-done.33.refs_3_ = bf16[160,640]{1,0:T(8,128)(2,1)S(1)} collective-permute-done((bf16[160,640]{1,0:T(8,128)(2,1)}, bf16[160,640]{1,0:T(8,128)(2,1)S(1)}, u32[]{:S(2)}, u32[]{:S(2)}) %collective-permute-start.33) | collective-permute-done | bytes 204832 | tf_op jit(solution)/shard_map/ppermute | solution.py:48
  134.5 10.3 %collective-permute-done.35.refs_5_ = bf16[160,640]{1,0:T(8,128)(2,1)S(1)} collective-permute-done((bf16[160,640]{1,0:T(8,128)(2,1)}, bf16[160,640]{1,0:T(8,128)(2,1)S(1)}, u32[]{:S(2)}, u32[]{:S(2)}) %collective-permute-start.35) | collective-permute-done | bytes 204832 | tf_op jit(solution)/shard_map/ppermute | solution.py:48
  144.8 2.4 %assemble.1 = bf16[160,5120]{1,0:T(8,128)(2,1)} custom-call(s32[1]{0:T(128)} %bitcast.8.place_ref, s32[1,1]{1,0:T(1,128)S(6)} %copy.16.blocks_ref, s32[1,160]{1,0:T(1,128)S(1)} %copy-done.1, bf16[160,640]{1,0:T(8,128)(2,1)} %get-tuple-element.107.refs_0_, bf16[160,640]{1,0:T(8,128)(2,1)S(1)} %collective-permute-done.31.refs_1_, ...), custom_call_target="tpu_custom_call" | custom-call | bytes 3276800 | tf_op jit(solution)/shard_map/assemble/pallas_call | solution.py:440
  (39 shorter events, 0.2 us)
Async XLA Ops:
  3.5 35.9 %collective-permute-start.12 = (bf16[1024,640]{1,0:T(8,128)(2,1)}, bf16[1024,640]{1,0:T(8,128)(2,1)S(1)}, u32[]{:S(2)}, u32[]{:S(2)}) collective-permute-start(bf16[1024,640]{1,0:T(8,128)(2,1)} %cut_weight.1.refs_14_), channel_id=1, source_target_pairs={{0,1},{1,2},{2,3},{4,5},{5,6},{6,7},{8,9},{9,10},{10,11},{12,13},{... | collective-permute-start | bytes 3932168 | tf_op jit(solution)/shard_map/ppermute | solution.py:144
  8.5 32.3 %collective-permute-start.13 = (bf16[1024,640]{1,0:T(8,128)(2,1)}, bf16[1024,640]{1,0:T(8,128)(2,1)S(1)}, u32[]{:S(2)}, u32[]{:S(2)}) collective-permute-start(bf16[1024,640]{1,0:T(8,128)(2,1)} %cut_weight.1.refs_14_), channel_id=1, source_target_pairs={{1,0},{2,1},{3,2},{5,4},{6,5},{7,6},{9,8},{10,9},{11,10},{13,12},{... | collective-permute-start | bytes 3932168 | tf_op jit(solution)/shard_map/ppermute | solution.py:144
  14.7 14.4 %collective-permute-start.9 = (bf16[3,160,512]{2,1,0:T(8,128)(2,1)}, bf16[3,160,512]{2,1,0:T(8,128)(2,1)S(1)}, u32[]{:S(2)}, u32[]{:S(2)}) collective-permute-start(bf16[3,160,512]{2,1,0:T(8,128)(2,1)} %get-tuple-element.64), channel_id=1, source_target_pairs={{0,8},{4,12},{8,0},{12,4},{16,24},{20,28},{24,16},{28,20},{1,9},{5... | collective-permute-start | bytes 1474568 | tf_op jit(solution)/shard_map/ppermute | solution.py:48
  16.2 23.1 %collective-permute-start.10 = (bf16[3,160,512]{2,1,0:T(8,128)(2,1)}, bf16[3,160,512]{2,1,0:T(8,128)(2,1)S(1)}, u32[]{:S(2)}, u32[]{:S(2)}) collective-permute-start(bf16[3,160,512]{2,1,0:T(8,128)(2,1)} %get-tuple-element.65), channel_id=1, source_target_pairs={{0,16},{4,20},{8,24},{12,28},{16,0},{20,4},{24,8},{28,12},{1,17},{... | collective-permute-start | bytes 1474568 | tf_op jit(solution)/shard_map/ppermute | solution.py:48
  17.7 21.6 %collective-permute-start.11 = (bf16[3,160,512]{2,1,0:T(8,128)(2,1)}, bf16[3,160,512]{2,1,0:T(8,128)(2,1)S(1)}, u32[]{:S(2)}, u32[]{:S(2)}) collective-permute-start(bf16[3,160,512]{2,1,0:T(8,128)(2,1)} %get-tuple-element.66), channel_id=1, source_target_pairs={{0,24},{4,28},{8,16},{12,20},{16,8},{20,12},{24,0},{28,4},{1,25},{... | collective-permute-start | bytes 1474568 | tf_op jit(solution)/shard_map/ppermute | solution.py:48
  39.4 66.2 %copy-start.5 = (bf16[1024,640]{1,0:T(8,128)(2,1)}, bf16[1024,640]{1,0:T(8,128)(2,1)S(1)}, u32[]{:S(2)}) copy-start(bf16[1024,640]{1,0:T(8,128)(2,1)S(1)} %collective-permute-done.12.refs_15_) | copy-start | bytes 3932164
  40.8 65.3 %copy-start.6 = (bf16[1024,640]{1,0:T(8,128)(2,1)}, bf16[1024,640]{1,0:T(8,128)(2,1)S(1)}, u32[]{:S(2)}) copy-start(bf16[1024,640]{1,0:T(8,128)(2,1)S(1)} %collective-permute-done.13.refs_13_) | copy-start | bytes 3932164
  40.8 5.1 %collective-permute-start.14 = (bf16[3,160,512]{2,1,0:T(8,128)(2,1)}, bf16[3,160,512]{2,1,0:T(8,128)(2,1)S(1)}, u32[]{:S(2)}, u32[]{:S(2)}) collective-permute-start(bf16[3,160,512]{2,1,0:T(8,128)(2,1)} %get-tuple-element.73), channel_id=1, source_target_pairs={{0,4},{4,0},{8,12},{12,8},{16,20},{20,16},{24,28},{28,24},{1,5},{5... | collective-permute-start | bytes 1474568 | tf_op jit(solution)/shard_map/ppermute | solution.py:48
  40.8 13.5 %collective-permute-start.15 = (bf16[3,160,512]{2,1,0:T(8,128)(2,1)}, bf16[3,160,512]{2,1,0:T(8,128)(2,1)S(1)}, u32[]{:S(2)}, u32[]{:S(2)}) collective-permute-start(bf16[3,160,512]{2,1,0:T(8,128)(2,1)} %get-tuple-element.75), channel_id=1, source_target_pairs={{0,12},{4,8},{8,4},{12,0},{16,28},{20,24},{24,20},{28,16},{1,13},{... | collective-permute-start | bytes 1474568 | tf_op jit(solution)/shard_map/ppermute | solution.py:48
  42.4 24.1 %collective-permute-start.16 = (bf16[3,160,512]{2,1,0:T(8,128)(2,1)}, bf16[3,160,512]{2,1,0:T(8,128)(2,1)S(1)}, u32[]{:S(2)}, u32[]{:S(2)}) collective-permute-start(bf16[3,160,512]{2,1,0:T(8,128)(2,1)} %get-tuple-element.77), channel_id=1, source_target_pairs={{0,20},{4,16},{8,28},{12,24},{16,4},{20,0},{24,12},{28,8},{1,21},{... | collective-permute-start | bytes 1474568 | tf_op jit(solution)/shard_map/ppermute | solution.py:48
  43.6 23.0 %collective-permute-start.17 = (bf16[3,160,512]{2,1,0:T(8,128)(2,1)}, bf16[3,160,512]{2,1,0:T(8,128)(2,1)S(1)}, u32[]{:S(2)}, u32[]{:S(2)}) collective-permute-start(bf16[3,160,512]{2,1,0:T(8,128)(2,1)} %get-tuple-element.79), channel_id=1, source_target_pairs={{0,28},{4,24},{8,20},{12,16},{16,12},{20,8},{24,4},{28,0},{1,29},{... | collective-permute-start | bytes 1474568 | tf_op jit(solution)/shard_map/ppermute | solution.py:48
  44.1 30.6 %collective-permute-start.19 = (bf16[1024,640]{1,0:T(8,128)(2,1)S(1)}, bf16[1024,640]{1,0:T(8,128)(2,1)}, u32[]{:S(2)}, u32[]{:S(2)}) collective-permute-start(bf16[1024,640]{1,0:T(8,128)(2,1)S(1)} %collective-permute-done.12.refs_15_), channel_id=1, source_target_pairs={{1,2},{2,3},{5,6},{6,7},{9,10},{10,11},{13,14},{14,15},{17,18},{18... | collective-permute-start | bytes 3932168 | tf_op jit(solution)/shard_map/ppermute | solution.py:144
  45.9 35.0 %collective-permute-start.20 = (bf16[1024,640]{1,0:T(8,128)(2,1)S(1)}, bf16[1024,640]{1,0:T(8,128)(2,1)}, u32[]{:S(2)}, u32[]{:S(2)}) collective-permute-start(bf16[1024,640]{1,0:T(8,128)(2,1)S(1)} %collective-permute-done.13.refs_13_), channel_id=1, source_target_pairs={{1,0},{2,1},{5,4},{6,5},{9,8},{10,9},{13,12},{14,13},{17,16},{18,1... | collective-permute-start | bytes 3932168 | tf_op jit(solution)/shard_map/ppermute | solution.py:144
  72.2 21.6 %copy-start.2 = (s32[8]{0:T(128)}, s32[8]{0:T(128)S(1)}, u32[]{:S(2)}) copy-start(s32[8]{0:T(128)S(1)} %get-tuple-element.80.counts_ref) | copy-start | bytes 100
  72.2 40.7 %copy-start = (bf16[768,512]{1,0:T(8,128)(2,1)}, bf16[768,512]{1,0:T(8,128)(2,1)S(1)}, u32[]{:S(2)}) copy-start(bf16[768,512]{1,0:T(8,128)(2,1)S(1)} %get-tuple-element.88.refs_0_) | copy-start | bytes 2359300
  72.2 2.5 %collective-permute-start.18 = (bf16[768,512]{1,0:T(8,128)(2,1)S(1)}, bf16[768,512]{1,0:T(8,128)(2,1)S(1)}, u32[]{:S(2)}, u32[]{:S(2)}) collective-permute-start(bf16[768,512]{1,0:T(8,128)(2,1)S(1)} %get-tuple-element.88.refs_0_), channel_id=1, source_target_pairs={{0,4},{4,0},{8,12},{12,8},{16,20},{20,16},{24,28},{28,24},{1,5},{5... | collective-permute-start | bytes 2359304 | tf_op jit(solution)/shard_map/ppermute | solution.py:48
  72.7 19.6 %collective-permute-start.21 = (bf16[768,512]{1,0:T(8,128)(2,1)S(1)}, bf16[768,512]{1,0:T(8,128)(2,1)S(1)}, u32[]{:S(2)}, u32[]{:S(2)}) collective-permute-start(bf16[768,512]{1,0:T(8,128)(2,1)S(1)} %get-tuple-element.88.refs_0_), channel_id=1, source_target_pairs={{0,8},{4,12},{8,0},{12,4},{16,24},{20,28},{24,16},{28,20},{1,9},{5... | collective-permute-start | bytes 2359304 | tf_op jit(solution)/shard_map/ppermute | solution.py:48
  73.1 20.7 %collective-permute-start.23 = (bf16[768,512]{1,0:T(8,128)(2,1)S(1)}, bf16[768,512]{1,0:T(8,128)(2,1)S(1)}, u32[]{:S(2)}, u32[]{:S(2)}) collective-permute-start(bf16[768,512]{1,0:T(8,128)(2,1)S(1)} %get-tuple-element.88.refs_0_), channel_id=1, source_target_pairs={{0,16},{4,20},{8,24},{12,28},{16,0},{20,4},{24,8},{28,12},{1,17},{... | collective-permute-start | bytes 2359304 | tf_op jit(solution)/shard_map/ppermute | solution.py:48
  74.7 38.2 %copy-start.7 = (bf16[768,512]{1,0:T(8,128)(2,1)}, bf16[768,512]{1,0:T(8,128)(2,1)S(1)}, u32[]{:S(2)}) copy-start(bf16[768,512]{1,0:T(8,128)(2,1)S(1)} %collective-permute-done.18.refs_1_) | copy-start | bytes 2359300
  80.8 32.0 %collective-permute-start.29 = (bf16[1024,640]{1,0:T(8,128)(2,1)}, bf16[1024,640]{1,0:T(8,128)(2,1)}, u32[]{:S(2)}, u32[]{:S(2)}) collective-permute-start(bf16[1024,640]{1,0:T(8,128)(2,1)} %collective-permute-done.20.refs_12_), channel_id=1, source_target_pairs={{1,0},{5,4},{9,8},{13,12},{17,16},{21,20},{25,24},{29,28}} | collective-permute-start | bytes 3932168 | tf_op jit(solution)/shard_map/ppermute | solution.py:144
  82.1 30.7 %collective-permute-start.30 = (bf16[1024,640]{1,0:T(8,128)(2,1)}, bf16[1024,640]{1,0:T(8,128)(2,1)}, u32[]{:S(2)}, u32[]{:S(2)}) collective-permute-start(bf16[1024,640]{1,0:T(8,128)(2,1)} %collective-permute-done.19.refs_16_), channel_id=1, source_target_pairs={{2,3},{6,7},{10,11},{14,15},{18,19},{22,23},{26,27},{30,31}} | collective-permute-start | bytes 3932168 | tf_op jit(solution)/shard_map/ppermute | solution.py:144
  92.2 20.7 %copy-start.3 = (bf16[768,512]{1,0:T(8,128)(2,1)}, bf16[768,512]{1,0:T(8,128)(2,1)S(1)}, u32[]{:S(2)}) copy-start(bf16[768,512]{1,0:T(8,128)(2,1)S(1)} %collective-permute-done.21.refs_2_) | copy-start | bytes 2359300
  92.2 10.5 %collective-permute-start.25 = (bf16[384,512]{1,0:T(8,128)(2,1)S(1)}, bf16[384,512]{1,0:T(8,128)(2,1)S(1)}, u32[]{:S(2)}, u32[]{:S(2)}) collective-permute-start(bf16[384,512]{1,0:T(8,128)(2,1)S(1)} %slice.16), channel_id=1, source_target_pairs={{0,16},{4,20},{8,24},{12,28},{16,0},{20,4},{24,8},{28,12},{1,17},{... | collective-permute-start | bytes 1179656 | tf_op jit(solution)/shard_map/ppermute | solution.py:48
  93.8 11.7 %collective-permute-start.22 = (bf16[768,512]{1,0:T(8,128)(2,1)S(1)}, bf16[768,512]{1,0:T(8,128)(2,1)S(1)}, u32[]{:S(2)}, u32[]{:S(2)}) collective-permute-start(bf16[768,512]{1,0:T(8,128)(2,1)S(1)} %collective-permute-done.21.refs_2_), channel_id=1, source_target_pairs={{0,4},{4,0},{8,12},{12,8},{16,20},{20,16},{24,28},{28,24},{1,5},{5... | collective-permute-start | bytes 2359304 | tf_op jit(solution)/shard_map/ppermute | solution.py:48
  93.8 19.1 %copy-start.4 = (bf16[768,512]{1,0:T(8,128)(2,1)}, bf16[768,512]{1,0:T(8,128)(2,1)S(1)}, u32[]{:S(2)}) copy-start(bf16[768,512]{1,0:T(8,128)(2,1)S(1)} %collective-permute-done.23.refs_4_) | copy-start | bytes 2359300
  93.9 11.7 %collective-permute-start.26 = (bf16[384,512]{1,0:T(8,128)(2,1)S(1)}, bf16[384,512]{1,0:T(8,128)(2,1)}, u32[]{:S(2)}, u32[]{:S(2)}) collective-permute-start(bf16[384,512]{1,0:T(8,128)(2,1)S(1)} %slice.17), channel_id=1, source_target_pairs={{0,8},{4,12},{8,0},{12,4},{16,24},{20,28},{24,16},{28,20},{1,9},{5... | collective-permute-start | bytes 1179656 | tf_op jit(solution)/shard_map/ppermute | solution.py:48
  102.7 10.2 %copy-start.9 = (bf16[384,512]{1,0:T(8,128)(2,1)}, bf16[384,512]{1,0:T(8,128)(2,1)S(1)}, u32[]{:S(2)}) copy-start(bf16[384,512]{1,0:T(8,128)(2,1)S(1)} %collective-permute-done.25.refs_6_) | copy-start | bytes 1179652
  102.7 4.3 %collective-permute-start.24 = (bf16[768,512]{1,0:T(8,128)(2,1)S(1)}, bf16[768,512]{1,0:T(8,128)(2,1)}, u32[]{:S(2)}, u32[]{:S(2)}) collective-permute-start(bf16[768,512]{1,0:T(8,128)(2,1)S(1)} %collective-permute-done.23.refs_4_), channel_id=1, source_target_pairs={{0,4},{4,0},{8,12},{12,8},{16,20},{20,16},{24,28},{28,24},{1,5},{5... | collective-permute-start | bytes 2359304 | tf_op jit(solution)/shard_map/ppermute | solution.py:48
  105.6 1.9 %collective-permute-start.27 = (bf16[384,512]{1,0:T(8,128)(2,1)S(1)}, bf16[384,512]{1,0:T(8,128)(2,1)}, u32[]{:S(2)}, u32[]{:S(2)}) collective-permute-start(bf16[384,512]{1,0:T(8,128)(2,1)S(1)} %collective-permute-done.25.refs_6_), channel_id=1, source_target_pairs={{0,4},{4,0},{8,12},{12,8},{16,20},{20,16},{24,28},{28,24},{1,5},{5... | collective-permute-start | bytes 1179656 | tf_op jit(solution)/shard_map/ppermute | solution.py:48
  105.6 0.9 copy-start.8
  105.6 2.6 %collective-permute-start.28 = (bf16[384,512]{1,0:T(8,128)(2,1)}, bf16[384,512]{1,0:T(8,128)(2,1)}, u32[]{:S(2)}, u32[]{:S(2)}) collective-permute-start(bf16[384,512]{1,0:T(8,128)(2,1)} %collective-permute-done.26.refs_7_), channel_id=1, source_target_pairs={{0,4},{4,0},{8,12},{12,8},{16,20},{20,16},{24,28},{28,24},{1,5},{5... | collective-permute-start | bytes 1179656 | tf_op jit(solution)/shard_map/ppermute | solution.py:48
  113.0 31.9 %copy-start.1 = (s32[1,160]{1,0:T(1,128)S(1)}, s32[1,160]{1,0:T(1,128)}, u32[]{:S(2)}) copy-start(s32[1,160]{1,0:T(1,128)} %mask_ref.3) | copy-start | bytes 1924
  122.7 3.6 %collective-permute-start.31 = (bf16[160,640]{1,0:T(8,128)(2,1)}, bf16[160,640]{1,0:T(8,128)(2,1)S(1)}, u32[]{:S(2)}, u32[]{:S(2)}) collective-permute-start(bf16[160,640]{1,0:T(8,128)(2,1)} %get-tuple-element.108), channel_id=1, source_target_pairs={{0,4},{4,0},{8,12},{12,8},{16,20},{20,16},{24,28},{28,24},{1,5},{5... | collective-permute-start | bytes 614408 | tf_op jit(solution)/shard_map/ppermute | solution.py:48
  122.8 8.2 %collective-permute-start.32 = (bf16[160,640]{1,0:T(8,128)(2,1)}, bf16[160,640]{1,0:T(8,128)(2,1)S(1)}, u32[]{:S(2)}, u32[]{:S(2)}) collective-permute-start(bf16[160,640]{1,0:T(8,128)(2,1)} %get-tuple-element.109), channel_id=1, source_target_pairs={{0,8},{4,12},{8,0},{12,4},{16,24},{20,28},{24,16},{28,20},{1,9},{5... | collective-permute-start | bytes 614408 | tf_op jit(solution)/shard_map/ppermute | solution.py:48
  124.4 10.1 %collective-permute-start.33 = (bf16[160,640]{1,0:T(8,128)(2,1)}, bf16[160,640]{1,0:T(8,128)(2,1)S(1)}, u32[]{:S(2)}, u32[]{:S(2)}) collective-permute-start(bf16[160,640]{1,0:T(8,128)(2,1)} %get-tuple-element.110), channel_id=1, source_target_pairs={{0,12},{4,8},{8,4},{12,0},{16,28},{20,24},{24,20},{28,16},{1,13},{... | collective-permute-start | bytes 614408 | tf_op jit(solution)/shard_map/ppermute | solution.py:48
  124.7 9.8 %collective-permute-start.34 = (bf16[160,640]{1,0:T(8,128)(2,1)}, bf16[160,640]{1,0:T(8,128)(2,1)S(1)}, u32[]{:S(2)}, u32[]{:S(2)}) collective-permute-start(bf16[160,640]{1,0:T(8,128)(2,1)} %get-tuple-element.111), channel_id=1, source_target_pairs={{0,16},{4,20},{8,24},{12,28},{16,0},{20,4},{24,8},{28,12},{1,17},{... | collective-permute-start | bytes 614408 | tf_op jit(solution)/shard_map/ppermute | solution.py:48
  126.2 18.6 %collective-permute-start.35 = (bf16[160,640]{1,0:T(8,128)(2,1)}, bf16[160,640]{1,0:T(8,128)(2,1)S(1)}, u32[]{:S(2)}, u32[]{:S(2)}) collective-permute-start(bf16[160,640]{1,0:T(8,128)(2,1)} %get-tuple-element.112), channel_id=1, source_target_pairs={{0,20},{4,16},{8,28},{12,24},{16,4},{20,0},{24,12},{28,8},{1,21},{... | collective-permute-start | bytes 614408 | tf_op jit(solution)/shard_map/ppermute | solution.py:48
  126.4 18.4 %collective-permute-start.36 = (bf16[160,640]{1,0:T(8,128)(2,1)}, bf16[160,640]{1,0:T(8,128)(2,1)S(1)}, u32[]{:S(2)}, u32[]{:S(2)}) collective-permute-start(bf16[160,640]{1,0:T(8,128)(2,1)} %get-tuple-element.113), channel_id=1, source_target_pairs={{0,24},{4,28},{8,16},{12,20},{16,8},{20,12},{24,0},{28,4},{1,25},{... | collective-permute-start | bytes 614408 | tf_op jit(solution)/shard_map/ppermute | solution.py:48
  131.0 13.8 %collective-permute-start.37 = (bf16[160,640]{1,0:T(8,128)(2,1)}, bf16[160,640]{1,0:T(8,128)(2,1)S(1)}, u32[]{:S(2)}, u32[]{:S(2)}) collective-permute-start(bf16[160,640]{1,0:T(8,128)(2,1)} %get-tuple-element.114), channel_id=1, source_target_pairs={{0,28},{4,24},{8,20},{12,16},{16,12},{20,8},{24,4},{28,0},{1,29},{... | collective-permute-start | bytes 614408 | tf_op jit(solution)/shard_map/ppermute | solution.py:48

commit v3 on v2

--- a/solution.py
+++ b/solution.py
@@ -53,18 +53,40 @@
     columns = out_weight.shape[1] // count
     if columns % HEAD_DIM:
         return lax.dynamic_slice_in_dim(out_weight, place[0] * columns, columns, axis=1)
-    step = depth // 4
-
-    def body(place_ref, w_ref, out_ref):
-        out_ref[...] = w_ref[...]
+    parts = 4
+    step = depth // parts
+
+    def body(place_ref, w_ref, out_ref, held, load_sems, store_sems):
+        start = pl.multiple_of(place_ref[0] * columns, HEAD_DIM)
+        loads, stores = [], []
+        for part in range(parts):
+            inside = pl.ds(part * step, step)
+            load = pltpu.make_async_copy(
+                w_ref.at[inside, pl.ds(start, columns)], held.at[part], load_sems.at[part]
+            )
+            load.start()
+            loads.append(load)
+        for part in range(parts):
+            inside = pl.ds(part * step, step)
+            loads[part].wait()
+            store = pltpu.make_async_copy(held.at[part], out_ref.at[inside, :], store_sems.at[part])
+            store.start()
+            stores.append(store)
+        for store in stores:
+            store.wait()
 
     return pl.pallas_call(
         body,
         grid_spec=pltpu.PrefetchScalarGridSpec(
             num_scalar_prefetch=1,
-            grid=(depth // step,),
-            in_specs=[pl.BlockSpec((step, columns), lambda i, place_ref: (i, place_ref[0]))],
-            out_specs=pl.BlockSpec((step, columns), lambda i, place_ref: (i, 0)),
+            grid=(1,),
+            in_specs=[pl.BlockSpec(memory_space=pl.ANY)],
+            out_specs=pl.BlockSpec(memory_space=pl.ANY),
+            scratch_shapes=[
+                pltpu.VMEM((parts, step, columns), jnp.bfloat16),
+                pltpu.SemaphoreType.DMA((parts,)),
+                pltpu.SemaphoreType.DMA((parts,)),
+            ],
         ),
         out_shape=jax.ShapeDtypeStruct((depth, columns), jnp.bfloat16),
         compiler_params=params(56),
@@ -249,7 +271,7 @@
             out_ref[...] = ordered[first : first + length, :]
             first += length
 
-    flops = 4 * total * total * width // 4
+    flops = 4 * total * total * width // 25
     return pl.pallas_call(
         body,
         grid_spec=pltpu.PrefetchScalarGridSpec(
@@ -271,7 +293,7 @@
         + [jax.ShapeDtypeStruct((count,), jnp.int32), jax.ShapeDtypeStruct((1,), jnp.int32)],
         compiler_params=params(40),
         cost_estimate=pl.CostEstimate(
-            flops=flops, bytes_accessed=8 * total * width, transcendentals=flops // 512
+            flops=flops, bytes_accessed=total * width, transcendentals=flops // 512
         ),
         name="attend",
     )(place, pltpu.with_memory_space_constraint(received[0], pltpu.HBM), *received[1:])
@@ -326,7 +348,7 @@
         landed, weight_all, sums, sems, weight_sems = refs[len(flat) + 1 + len(distances) + count :]
         used = sum(counts_ref[mask] for mask in range(count)) * BLOCK
 
-        for mask in range(count):
+        def send_weight(mask):
             owner = place_ref[0] ^ mask
             apart = group_ref[0] - owner // each
             start = pl.multiple_of((owner % each) * width, width)
@@ -334,7 +356,7 @@
             for distance, shard_ref in zip(distances, shard_refs):
 
                 @pl.when(apart == distance)
-                def _(mask=mask, start=start, lower=lower, shard_ref=shard_ref):
+                def _():
                     pltpu.make_async_copy(
                         shard_ref.at[pl.ds(start, width), :],
                         weight_all.at[mask // 2, lower : lower + width, :],
@@ -348,6 +370,7 @@
             def _(size=size):
                 taken = 0
                 for mask in range(count):
+                    send_weight(mask)
                     lanes = slice(mask % 2 * width, (mask % 2 + 1) * width)
                     sources = flat_refs[taken : taken + len(features[mask])]
                     taken += len(sources)
@@ -429,21 +452,40 @@
         return jnp.where(good[:, None], result, jnp.bfloat16(0.0))
 
     def body(place_ref, blocks_ref, mask_ref, *refs):
-        out_ref = refs[-1]
+        piece_refs, out_ref = refs[:count], refs[count]
+        held, masked, load_sems, store_sems = refs[count + 1 :]
+        loads, stores = [], []
+        for mask in range(count):
+            load = pltpu.make_async_copy(piece_refs[mask], held.at[mask], load_sems.at[mask])
+            load.start()
+            loads.append(load)
         good = valid_column(mask_ref, blocks_ref[0, 0]) > 0.5
         for mask in range(count):
+            loads[mask].wait()
+            masked[mask] = jnp.where(good, held[mask], jnp.bfloat16(0.0))
             start = pl.multiple_of((place_ref[0] ^ mask) * columns, HEAD_DIM)
-            out_ref[:, pl.ds(start, columns)] = jnp.where(
-                good, refs[mask][...], jnp.bfloat16(0.0)
+            store = pltpu.make_async_copy(
+                masked.at[mask], out_ref.at[:, pl.ds(start, columns)], store_sems.at[mask]
             )
-
+            store.start()
+            stores.append(store)
+        for store in stores:
+            store.wait()
+
+    any_spec = pl.BlockSpec(memory_space=pl.ANY)
     return pl.pallas_call(
         body,
         grid_spec=pltpu.PrefetchScalarGridSpec(
             num_scalar_prefetch=2,
             grid=(1,),
-            in_specs=[full_spec((1, rows))] + [full_spec((rows, columns))] * count,
-            out_specs=full_spec((rows, count * columns)),
+            in_specs=[full_spec((1, rows))] + [any_spec] * count,
+            out_specs=any_spec,
+            scratch_shapes=[
+                pltpu.VMEM((count, rows, columns), jnp.bfloat16),
+                pltpu.VMEM((count, rows, columns), jnp.bfloat16),
+                pltpu.SemaphoreType.DMA((count,)),
+                pltpu.SemaphoreType.DMA((count,)),
+            ],
         ),
         out_shape=jax.ShapeDtypeStruct((rows, count * columns), jnp.bfloat16),
         compiler_params=params(16),

time: 147 us -> 149 us (1.014); the launches traced: 147 us -> 146 us
  waiting for transfers between devices: 88 us -> 91.1 us
  Pallas kernels: 25.6 us -> 23.1 us
  starting transfers between devices: 31.8 us -> 30 us
    ppermute x23, waiting for transfers between devices: 75.7 us -> 85.7 us  [xor_permute(): lax.ppermute(array, 'cam', [(place, place ^ mask) for place in range(coun...]
    ppermute x6, waiting for transfers between devices: 12.3 us -> 5.33 us  [pass_weight(): lax.ppermute(shards[sign * (distance - 1)], 'fsdp', pairs)]
    ppermute x23, starting transfers between devices: 19.5 us -> 17.6 us  [xor_permute(): lax.ppermute(array, 'cam', [(place, place ^ mask) for place in range(coun...]
  transfers between devices with their start and end apart: 29 -> 29, of which waited for: 15 -> 15; matrix products, arithmetic and copies ran while one was open for 0% -> 0% of each run, Pallas kernels for 7% -> 6%
where the time goes in v3:
time: 149 us; the launch traced here: 146 us
  waiting for transfers between devices  91.1 us (61%)
  starting transfers between devices  30 us (20%)
  Pallas kernels  23.1 us (16%)
  between operations  1.57 us (1%)
    ppermute x23, waiting for transfers between devices, xor_permute(): lax.ppermute(array, 'cam', [(place, place ^ mask) for place in range(coun...  85.7 us
    ppermute x23, starting transfers between devices, xor_permute(): lax.ppermute(array, 'cam', [(place, place ^ mask) for place in range(coun...  17.6 us
    ppermute x6, starting transfers between devices, pass_weight(): lax.ppermute(shards[sign * (distance - 1)], 'fsdp', pairs)  12.4 us
    pallas_call x1, Pallas kernels, project(): pl.pallas_call(body, grid_spec=pltpu.PrefetchScalarGridSpec(num_scalar_pr...  8.69 us
    ppermute x6, waiting for transfers between devices, pass_weight(): lax.ppermute(shards[sign * (distance - 1)], 'fsdp', pairs)  5.33 us
    pallas_call x1, Pallas kernels, attend(): pl.pallas_call(body, grid_spec=pltpu.PrefetchScalarGridSpec(num_scalar_pr...  4.87 us
    pallas_call x1, Pallas kernels, pack(): pl.pallas_call(body, grid_spec=pltpu.PrefetchScalarGridSpec(num_scalar_pr...  4.19 us
    pallas_call x1, Pallas kernels, assemble(): pl.pallas_call(body, grid_spec=pltpu.PrefetchScalarGridSpec(num_scalar_pr...  3.3 us
  transfers between devices with their start and end apart: 29, of which 15 were waited for; matrix products, arithmetic and copies ran while one was open for 0% of the time, Pallas kernels for 6%

profile of v3, /device:TPU:0, one launch (start us, length us, event | category | flops | bytes accessed | tf_op | source)
XLA Modules:
  0.0 146.2 jit_solution(5508805184753892906)
XLA Ops:
  0.0 2.1 %cut_weight.1.refs_14_ = bf16[1024,640]{1,0:T(8,128)(2,1)} custom-call(s32[1]{0:T(128)} %bitcast.8.place_ref, bf16[1024,5120]{1,0:T(8,128)(2,1)} %w_ref.1), custom_call_target="tpu_custom_call" | custom-call | bytes 2621440 | tf_op jit(solution)/shard_map/cut_weight/pallas_call | solution.py:78
  2.1 5.0 %collective-permute-start.12 = (bf16[1024,640]{1,0:T(8,128)(2,1)}, bf16[1024,640]{1,0:T(8,128)(2,1)S(1)}, u32[]{:S(2)}, u32[]{:S(2)}) collective-permute-start(bf16[1024,640]{1,0:T(8,128)(2,1)} %cut_weight.1.refs_14_), channel_id=1, source_target_pairs={{0,1},{1,2},{2,3},{4,5},{5,6},{6,7},{8,9},{9,10},{10,11},{12,13},{... | collective-permute-start | bytes 3932168 | tf_op jit(solution)/shard_map/ppermute | solution.py:166
  7.1 1.3 collective-permute-start.13
  9.1 4.2 %pack.1 = (bf16[3,160,512]{2,1,0:T(8,128)(2,1)}, bf16[3,160,512]{2,1,0:T(8,128)(2,1)}, bf16[3,160,512]{2,1,0:T(8,128)(2,1)}, bf16[3,160,512]{2,1,0:T(8,128)(2,1)...) custom-call(s32[1]{0:T(128)} %bitcast.8.place_ref, ...), custom_call_target="tpu_custom_call" | custom-call | bytes 7864320 | tf_op jit(solution)/shard_map/pack/pallas_call | solution.py:135
  13.3 1.6 %collective-permute-start.9 = (bf16[3,160,512]{2,1,0:T(8,128)(2,1)}, bf16[3,160,512]{2,1,0:T(8,128)(2,1)S(1)}, u32[]{:S(2)}, u32[]{:S(2)}) collective-permute-start(bf16[3,160,512]{2,1,0:T(8,128)(2,1)} %get-tuple-element.64), channel_id=1, source_target_pairs={{0,8},{4,12},{8,0},{12,4},{16,24},{20,28},{24,16},{28,20},{1,9},{5... | collective-permute-start | bytes 1474568 | tf_op jit(solution)/shard_map/ppermute | solution.py:48
  14.8 1.5 %collective-permute-start.10 = (bf16[3,160,512]{2,1,0:T(8,128)(2,1)}, bf16[3,160,512]{2,1,0:T(8,128)(2,1)S(1)}, u32[]{:S(2)}, u32[]{:S(2)}) collective-permute-start(bf16[3,160,512]{2,1,0:T(8,128)(2,1)} %get-tuple-element.65), channel_id=1, source_target_pairs={{0,16},{4,20},{8,24},{12,28},{16,0},{20,4},{24,8},{28,12},{1,17},{... | collective-permute-start | bytes 1474568 | tf_op jit(solution)/shard_map/ppermute | solution.py:48
  16.3 0.5 collective-permute-start.11
  16.8 10.9 %collective-permute-done.9.refs_2_ = bf16[3,160,512]{2,1,0:T(8,128)(2,1)S(1)} collective-permute-done((bf16[3,160,512]{2,1,0:T(8,128)(2,1)}, bf16[3,160,512]{2,1,0:T(8,128)(2,1)S(1)}, u32[]{:S(2)}, u32[]{:S(2)}) %collective-permute-start.9) | collective-permute-done | bytes 491552 | tf_op jit(solution)/shard_map/ppermute | solution.py:48
  27.7 10.3 %collective-permute-done.10.refs_4_ = bf16[3,160,512]{2,1,0:T(8,128)(2,1)S(1)} collective-permute-done((bf16[3,160,512]{2,1,0:T(8,128)(2,1)}, bf16[3,160,512]{2,1,0:T(8,128)(2,1)S(1)}, u32[]{:S(2)}, u32[]{:S(2)}) %collective-permute-start.10) | collective-permute-done | bytes 491552 | tf_op jit(solution)/shard_map/ppermute | solution.py:48
  38.0 0.0 collective-permute-done.12.refs_15_
  38.0 1.5 %collective-permute-done.13.refs_13_ = bf16[1024,640]{1,0:T(8,128)(2,1)S(1)} collective-permute-done((bf16[1024,640]{1,0:T(8,128)(2,1)}, bf16[1024,640]{1,0:T(8,128)(2,1)S(1)}, u32[]{:S(2)}, u32[]{:S(2)}) %collective-permute-start.13) | collective-permute-done | bytes 1310752 | tf_op jit(solution)/shard_map/ppermute | solution.py:166
  39.5 1.8 %collective-permute-start.19 = (bf16[1024,640]{1,0:T(8,128)(2,1)S(1)}, bf16[1024,640]{1,0:T(8,128)(2,1)}, u32[]{:S(2)}, u32[]{:S(2)}) collective-permute-start(bf16[1024,640]{1,0:T(8,128)(2,1)S(1)} %collective-permute-done.12.refs_15_), channel_id=1, source_target_pairs={{1,2},{2,3},{5,6},{6,7},{9,10},{10,11},{13,14},{14,15},{17,18},{18... | collective-permute-start | bytes 3932168 | tf_op jit(solution)/shard_map/ppermute | solution.py:166
  41.2 1.3 collective-permute-start.20
  42.5 1.7 %collective-permute-start.15 = (bf16[3,160,512]{2,1,0:T(8,128)(2,1)}, bf16[3,160,512]{2,1,0:T(8,128)(2,1)S(1)}, u32[]{:S(2)}, u32[]{:S(2)}) collective-permute-start(bf16[3,160,512]{2,1,0:T(8,128)(2,1)} %get-tuple-element.75), channel_id=1, source_target_pairs={{0,12},{4,8},{8,4},{12,0},{16,28},{20,24},{24,20},{28,16},{1,13},{... | collective-permute-start | bytes 1474568 | tf_op jit(solution)/shard_map/ppermute | solution.py:48
  44.2 1.1 collective-permute-start.16
  45.3 0.6 collective-permute-start.17
  45.9 10.2 %collective-permute-done.15.refs_3_ = bf16[3,160,512]{2,1,0:T(8,128)(2,1)S(1)} collective-permute-done((bf16[3,160,512]{2,1,0:T(8,128)(2,1)}, bf16[3,160,512]{2,1,0:T(8,128)(2,1)S(1)}, u32[]{:S(2)}, u32[]{:S(2)}) %collective-permute-start.15) | collective-permute-done | bytes 491552 | tf_op jit(solution)/shard_map/ppermute | solution.py:48
  56.1 12.2 %collective-permute-done.16.refs_5_ = bf16[3,160,512]{2,1,0:T(8,128)(2,1)S(1)} collective-permute-done((bf16[3,160,512]{2,1,0:T(8,128)(2,1)}, bf16[3,160,512]{2,1,0:T(8,128)(2,1)S(1)}, u32[]{:S(2)}, u32[]{:S(2)}) %collective-permute-start.16) | collective-permute-done | bytes 491552 | tf_op jit(solution)/shard_map/ppermute | solution.py:48
  68.3 4.9 %attend.1 = (bf16[768,512]{1,0:T(8,128)(2,1)S(1)}, bf16[512,512]{1,0:T(8,128)(2,1)}, s32[8]{0:T(128)S(1)}, s32[1]{0:T(128)}) custom-call(s32[1]{0:T(128)} %bitcast.8.place_ref, bf16[3,160,512]{2,1,0:T(8,128)(2,1)} %get-tuple-element.72.refs_0_, bf16[3,160,512]{2,1,0:T(8,128)(2,1)S(1)} %collective-permute-done.14.refs_1_, ...), custom_call_target="tpu_custom_call" | custom-call | flops 134217728 | bytes 655360 | tf_op jit(solution)/shard_map/attend/pallas_call | solution.py:275
  73.2 0.4 collective-permute-start.18
  73.6 0.4 collective-permute-start.21
  74.0 1.6 %collective-permute-start.23 = (bf16[768,512]{1,0:T(8,128)(2,1)S(1)}, bf16[768,512]{1,0:T(8,128)(2,1)S(1)}, u32[]{:S(2)}, u32[]{:S(2)}) collective-permute-start(bf16[768,512]{1,0:T(8,128)(2,1)S(1)} %get-tuple-element.88.refs_0_), channel_id=1, source_target_pairs={{0,16},{4,20},{8,24},{12,28},{16,0},{20,4},{24,8},{28,12},{1,17},{... | collective-permute-start | bytes 2359304 | tf_op jit(solution)/shard_map/ppermute | solution.py:48
  75.7 1.1 collective-permute-done.20.refs_12_
  76.7 1.3 collective-permute-start.29
  78.0 1.8 %collective-permute-start.30 = (bf16[1024,640]{1,0:T(8,128)(2,1)}, bf16[1024,640]{1,0:T(8,128)(2,1)}, u32[]{:S(2)}, u32[]{:S(2)}) collective-permute-start(bf16[1024,640]{1,0:T(8,128)(2,1)} %collective-permute-done.19.refs_16_), channel_id=1, source_target_pairs={{2,3},{6,7},{10,11},{14,15},{18,19},{22,23},{26,27},{30,31}} | collective-permute-start | bytes 3932168 | tf_op jit(solution)/shard_map/ppermute | solution.py:166
  79.8 13.3 %collective-permute-done.21.refs_2_ = bf16[768,512]{1,0:T(8,128)(2,1)S(1)} collective-permute-done((bf16[768,512]{1,0:T(8,128)(2,1)S(1)}, bf16[768,512]{1,0:T(8,128)(2,1)S(1)}, u32[]{:S(2)}, u32[]{:S(2)}) %collective-permute-start.21) | collective-permute-done | bytes 786464 | tf_op jit(solution)/shard_map/ppermute | solution.py:48
  93.2 1.6 %collective-permute-start.25 = (bf16[384,512]{1,0:T(8,128)(2,1)S(1)}, bf16[384,512]{1,0:T(8,128)(2,1)S(1)}, u32[]{:S(2)}, u32[]{:S(2)}) collective-permute-start(bf16[384,512]{1,0:T(8,128)(2,1)S(1)} %slice.16), channel_id=1, source_target_pairs={{0,16},{4,20},{8,24},{12,28},{16,0},{20,4},{24,8},{28,12},{1,17},{... | collective-permute-start | bytes 1179656 | tf_op jit(solution)/shard_map/ppermute | solution.py:48
  94.8 0.6 collective-permute-start.26
  95.4 8.2 %collective-permute-done.25.refs_6_ = bf16[384,512]{1,0:T(8,128)(2,1)S(1)} collective-permute-done((bf16[384,512]{1,0:T(8,128)(2,1)S(1)}, bf16[384,512]{1,0:T(8,128)(2,1)S(1)}, u32[]{:S(2)}, u32[]{:S(2)}) %collective-permute-start.25) | collective-permute-done | bytes 393248 | tf_op jit(solution)/shard_map/ppermute | solution.py:48
  103.7 2.9 %collective-permute-done.26.refs_7_ = bf16[384,512]{1,0:T(8,128)(2,1)} collective-permute-done((bf16[384,512]{1,0:T(8,128)(2,1)S(1)}, bf16[384,512]{1,0:T(8,128)(2,1)}, u32[]{:S(2)}, u32[]{:S(2)}) %collective-permute-start.26) | collective-permute-done | bytes 393248 | tf_op jit(solution)/shard_map/ppermute | solution.py:48
  106.5 0.6 collective-permute-start.28
  107.1 0.3 copy-done.8
  108.0 0.4 collective-permute-done.27.refs_8_
  108.4 0.8 collective-permute-done.28.refs_9_
  109.1 2.8 %collective-permute-done.29.refs_11_ = bf16[1024,640]{1,0:T(8,128)(2,1)} collective-permute-done((bf16[1024,640]{1,0:T(8,128)(2,1)}, bf16[1024,640]{1,0:T(8,128)(2,1)}, u32[]{:S(2)}, u32[]{:S(2)}) %collective-permute-start.29) | collective-permute-done | bytes 1310752 | tf_op jit(solution)/shard_map/ppermute | solution.py:166
  112.0 0.0 copy-start.1
  112.0 8.7 %project.1 = (bf16[160,640]{1,0:T(8,128)(2,1)}, bf16[160,640]{1,0:T(8,128)(2,1)}, bf16[160,640]{1,0:T(8,128)(2,1)}, bf16[160,640]{1,0:T(8,128)(2,1)}, bf16[160,6...) custom-call(s32[1]{0:T(128)} %bitcast.8.place_ref, ...), custom_call_target="tpu_custom_call" | custom-call | flops 3355443200 | bytes 5242880 | tf_op jit(solution)/shard_map/project/pallas_call | solution.py:419
  120.7 0.1 collective-permute-start.31
  120.8 0.9 collective-permute-start.32
  121.6 1.0 collective-permute-start.33
  122.6 1.5 %collective-permute-start.34 = (bf16[160,640]{1,0:T(8,128)(2,1)}, bf16[160,640]{1,0:T(8,128)(2,1)S(1)}, u32[]{:S(2)}, u32[]{:S(2)}) collective-permute-start(bf16[160,640]{1,0:T(8,128)(2,1)} %get-tuple-element.111), channel_id=1, source_target_pairs={{0,16},{4,20},{8,24},{12,28},{16,0},{20,4},{24,8},{28,12},{1,17},{... | collective-permute-start | bytes 614408 | tf_op jit(solution)/shard_map/ppermute | solution.py:48
  124.2 0.2 collective-permute-start.35
  124.3 1.5 %collective-permute-start.36 = (bf16[160,640]{1,0:T(8,128)(2,1)}, bf16[160,640]{1,0:T(8,128)(2,1)S(1)}, u32[]{:S(2)}, u32[]{:S(2)}) collective-permute-start(bf16[160,640]{1,0:T(8,128)(2,1)} %get-tuple-element.113), channel_id=1, source_target_pairs={{0,24},{4,28},{8,16},{12,20},{16,8},{20,12},{24,0},{28,4},{1,25},{... | collective-permute-start | bytes 614408 | tf_op jit(solution)/shard_map/ppermute | solution.py:48
  125.8 3.1 %collective-permute-done.32.refs_2_ = bf16[160,640]{1,0:T(8,128)(2,1)S(1)} collective-permute-done((bf16[160,640]{1,0:T(8,128)(2,1)}, bf16[160,640]{1,0:T(8,128)(2,1)S(1)}, u32[]{:S(2)}, u32[]{:S(2)}) %collective-permute-start.32) | collective-permute-done | bytes 204832 | tf_op jit(solution)/shard_map/ppermute | solution.py:48
  128.9 0.3 collective-permute-start.37
  129.2 3.2 %collective-permute-done.33.refs_3_ = bf16[160,640]{1,0:T(8,128)(2,1)S(1)} collective-permute-done((bf16[160,640]{1,0:T(8,128)(2,1)}, bf16[160,640]{1,0:T(8,128)(2,1)S(1)}, u32[]{:S(2)}, u32[]{:S(2)}) %collective-permute-start.33) | collective-permute-done | bytes 204832 | tf_op jit(solution)/shard_map/ppermute | solution.py:48
  132.4 10.3 %collective-permute-done.35.refs_5_ = bf16[160,640]{1,0:T(8,128)(2,1)S(1)} collective-permute-done((bf16[160,640]{1,0:T(8,128)(2,1)}, bf16[160,640]{1,0:T(8,128)(2,1)S(1)}, u32[]{:S(2)}, u32[]{:S(2)}) %collective-permute-start.35) | collective-permute-done | bytes 204832 | tf_op jit(solution)/shard_map/ppermute | solution.py:48
  142.8 3.3 %assemble.1 = bf16[160,5120]{1,0:T(8,128)(2,1)} custom-call(s32[1]{0:T(128)} %bitcast.8.place_ref, s32[1,1]{1,0:T(1,128)S(6)} %copy.16.blocks_ref, s32[1,160]{1,0:T(1,128)S(1)} %copy-done.1, bf16[160,640]{1,0:T(8,128)(2,1)} %get-tuple-element.107.refs_0_, bf16[160,640]{1,0:T(8,128)(2,1)S(1)} %collective-permute-done.31.refs_1_, ...), custom_call_target="tpu_custom_call" | custom-call | bytes 3276800 | tf_op jit(solution)/shard_map/assemble/pallas_call | solution.py:476
  (39 shorter events, 0.2 us)
Async XLA Ops:
  2.1 35.9 %collective-permute-start.12 = (bf16[1024,640]{1,0:T(8,128)(2,1)}, bf16[1024,640]{1,0:T(8,128)(2,1)S(1)}, u32[]{:S(2)}, u32[]{:S(2)}) collective-permute-start(bf16[1024,640]{1,0:T(8,128)(2,1)} %cut_weight.1.refs_14_), channel_id=1, source_target_pairs={{0,1},{1,2},{2,3},{4,5},{5,6},{6,7},{8,9},{9,10},{10,11},{12,13},{... | collective-permute-start | bytes 3932168 | tf_op jit(solution)/shard_map/ppermute | solution.py:166
  7.1 32.3 %collective-permute-start.13 = (bf16[1024,640]{1,0:T(8,128)(2,1)}, bf16[1024,640]{1,0:T(8,128)(2,1)S(1)}, u32[]{:S(2)}, u32[]{:S(2)}) collective-permute-start(bf16[1024,640]{1,0:T(8,128)(2,1)} %cut_weight.1.refs_14_), channel_id=1, source_target_pairs={{1,0},{2,1},{3,2},{5,4},{6,5},{7,6},{9,8},{10,9},{11,10},{13,12},{... | collective-permute-start | bytes 3932168 | tf_op jit(solution)/shard_map/ppermute | solution.py:166
  13.3 14.4 %collective-permute-start.9 = (bf16[3,160,512]{2,1,0:T(8,128)(2,1)}, bf16[3,160,512]{2,1,0:T(8,128)(2,1)S(1)}, u32[]{:S(2)}, u32[]{:S(2)}) collective-permute-start(bf16[3,160,512]{2,1,0:T(8,128)(2,1)} %get-tuple-element.64), channel_id=1, source_target_pairs={{0,8},{4,12},{8,0},{12,4},{16,24},{20,28},{24,16},{28,20},{1,9},{5... | collective-permute-start | bytes 1474568 | tf_op jit(solution)/shard_map/ppermute | solution.py:48
  14.8 23.1 %collective-permute-start.10 = (bf16[3,160,512]{2,1,0:T(8,128)(2,1)}, bf16[3,160,512]{2,1,0:T(8,128)(2,1)S(1)}, u32[]{:S(2)}, u32[]{:S(2)}) collective-permute-start(bf16[3,160,512]{2,1,0:T(8,128)(2,1)} %get-tuple-element.65), channel_id=1, source_target_pairs={{0,16},{4,20},{8,24},{12,28},{16,0},{20,4},{24,8},{28,12},{1,17},{... | collective-permute-start | bytes 1474568 | tf_op jit(solution)/shard_map/ppermute | solution.py:48
  16.3 21.6 %collective-permute-start.11 = (bf16[3,160,512]{2,1,0:T(8,128)(2,1)}, bf16[3,160,512]{2,1,0:T(8,128)(2,1)S(1)}, u32[]{:S(2)}, u32[]{:S(2)}) collective-permute-start(bf16[3,160,512]{2,1,0:T(8,128)(2,1)} %get-tuple-element.66), channel_id=1, source_target_pairs={{0,24},{4,28},{8,16},{12,20},{16,8},{20,12},{24,0},{28,4},{1,25},{... | collective-permute-start | bytes 1474568 | tf_op jit(solution)/shard_map/ppermute | solution.py:48
  38.0 68.5 %copy-start.5 = (bf16[1024,640]{1,0:T(8,128)(2,1)}, bf16[1024,640]{1,0:T(8,128)(2,1)S(1)}, u32[]{:S(2)}) copy-start(bf16[1024,640]{1,0:T(8,128)(2,1)S(1)} %collective-permute-done.12.refs_15_) | copy-start | bytes 3932164
  39.5 67.6 %copy-start.6 = (bf16[1024,640]{1,0:T(8,128)(2,1)}, bf16[1024,640]{1,0:T(8,128)(2,1)S(1)}, u32[]{:S(2)}) copy-start(bf16[1024,640]{1,0:T(8,128)(2,1)S(1)} %collective-permute-done.13.refs_13_) | copy-start | bytes 3932164
  39.5 5.9 %collective-permute-start.14 = (bf16[3,160,512]{2,1,0:T(8,128)(2,1)}, bf16[3,160,512]{2,1,0:T(8,128)(2,1)S(1)}, u32[]{:S(2)}, u32[]{:S(2)}) collective-permute-start(bf16[3,160,512]{2,1,0:T(8,128)(2,1)} %get-tuple-element.73), channel_id=1, source_target_pairs={{0,4},{4,0},{8,12},{12,8},{16,20},{20,16},{24,28},{28,24},{1,5},{5... | collective-permute-start | bytes 1474568 | tf_op jit(solution)/shard_map/ppermute | solution.py:48
  39.5 36.2 %collective-permute-start.19 = (bf16[1024,640]{1,0:T(8,128)(2,1)S(1)}, bf16[1024,640]{1,0:T(8,128)(2,1)}, u32[]{:S(2)}, u32[]{:S(2)}) collective-permute-start(bf16[1024,640]{1,0:T(8,128)(2,1)S(1)} %collective-permute-done.12.refs_15_), channel_id=1, source_target_pairs={{1,2},{2,3},{5,6},{6,7},{9,10},{10,11},{13,14},{14,15},{17,18},{18... | collective-permute-start | bytes 3932168 | tf_op jit(solution)/shard_map/ppermute | solution.py:166
  41.2 35.5 %collective-permute-start.20 = (bf16[1024,640]{1,0:T(8,128)(2,1)S(1)}, bf16[1024,640]{1,0:T(8,128)(2,1)}, u32[]{:S(2)}, u32[]{:S(2)}) collective-permute-start(bf16[1024,640]{1,0:T(8,128)(2,1)S(1)} %collective-permute-done.13.refs_13_), channel_id=1, source_target_pairs={{1,0},{2,1},{5,4},{6,5},{9,8},{10,9},{13,12},{14,13},{17,16},{18,1... | collective-permute-start | bytes 3932168 | tf_op jit(solution)/shard_map/ppermute | solution.py:166
  42.5 13.6 %collective-permute-start.15 = (bf16[3,160,512]{2,1,0:T(8,128)(2,1)}, bf16[3,160,512]{2,1,0:T(8,128)(2,1)S(1)}, u32[]{:S(2)}, u32[]{:S(2)}) collective-permute-start(bf16[3,160,512]{2,1,0:T(8,128)(2,1)} %get-tuple-element.75), channel_id=1, source_target_pairs={{0,12},{4,8},{8,4},{12,0},{16,28},{20,24},{24,20},{28,16},{1,13},{... | collective-permute-start | bytes 1474568 | tf_op jit(solution)/shard_map/ppermute | solution.py:48
  44.2 24.1 %collective-permute-start.16 = (bf16[3,160,512]{2,1,0:T(8,128)(2,1)}, bf16[3,160,512]{2,1,0:T(8,128)(2,1)S(1)}, u32[]{:S(2)}, u32[]{:S(2)}) collective-permute-start(bf16[3,160,512]{2,1,0:T(8,128)(2,1)} %get-tuple-element.77), channel_id=1, source_target_pairs={{0,20},{4,16},{8,28},{12,24},{16,4},{20,0},{24,12},{28,8},{1,21},{... | collective-permute-start | bytes 1474568 | tf_op jit(solution)/shard_map/ppermute | solution.py:48
  45.3 22.9 %collective-permute-start.17 = (bf16[3,160,512]{2,1,0:T(8,128)(2,1)}, bf16[3,160,512]{2,1,0:T(8,128)(2,1)S(1)}, u32[]{:S(2)}, u32[]{:S(2)}) collective-permute-start(bf16[3,160,512]{2,1,0:T(8,128)(2,1)} %get-tuple-element.79), channel_id=1, source_target_pairs={{0,28},{4,24},{8,20},{12,16},{16,12},{20,8},{24,4},{28,0},{1,29},{... | collective-permute-start | bytes 1474568 | tf_op jit(solution)/shard_map/ppermute | solution.py:48
  73.1 21.6 %copy-start.2 = (s32[8]{0:T(128)}, s32[8]{0:T(128)S(1)}, u32[]{:S(2)}) copy-start(s32[8]{0:T(128)S(1)} %get-tuple-element.80.counts_ref) | copy-start | bytes 100
  73.2 38.8 %copy-start = (bf16[768,512]{1,0:T(8,128)(2,1)}, bf16[768,512]{1,0:T(8,128)(2,1)S(1)}, u32[]{:S(2)}) copy-start(bf16[768,512]{1,0:T(8,128)(2,1)S(1)} %get-tuple-element.88.refs_0_) | copy-start | bytes 2359300
  73.2 2.5 %collective-permute-start.18 = (bf16[768,512]{1,0:T(8,128)(2,1)S(1)}, bf16[768,512]{1,0:T(8,128)(2,1)S(1)}, u32[]{:S(2)}, u32[]{:S(2)}) collective-permute-start(bf16[768,512]{1,0:T(8,128)(2,1)S(1)} %get-tuple-element.88.refs_0_), channel_id=1, source_target_pairs={{0,4},{4,0},{8,12},{12,8},{16,20},{20,16},{24,28},{28,24},{1,5},{5... | collective-permute-start | bytes 2359304 | tf_op jit(solution)/shard_map/ppermute | solution.py:48
  73.6 19.6 %collective-permute-start.21 = (bf16[768,512]{1,0:T(8,128)(2,1)S(1)}, bf16[768,512]{1,0:T(8,128)(2,1)S(1)}, u32[]{:S(2)}, u32[]{:S(2)}) collective-permute-start(bf16[768,512]{1,0:T(8,128)(2,1)S(1)} %get-tuple-element.88.refs_0_), channel_id=1, source_target_pairs={{0,8},{4,12},{8,0},{12,4},{16,24},{20,28},{24,16},{28,20},{1,9},{5... | collective-permute-start | bytes 2359304 | tf_op jit(solution)/shard_map/ppermute | solution.py:48
  74.0 20.7 %collective-permute-start.23 = (bf16[768,512]{1,0:T(8,128)(2,1)S(1)}, bf16[768,512]{1,0:T(8,128)(2,1)S(1)}, u32[]{:S(2)}, u32[]{:S(2)}) collective-permute-start(bf16[768,512]{1,0:T(8,128)(2,1)S(1)} %get-tuple-element.88.refs_0_), channel_id=1, source_target_pairs={{0,16},{4,20},{8,24},{12,28},{16,0},{20,4},{24,8},{28,12},{1,17},{... | collective-permute-start | bytes 2359304 | tf_op jit(solution)/shard_map/ppermute | solution.py:48
  75.7 36.3 %copy-start.7 = (bf16[768,512]{1,0:T(8,128)(2,1)}, bf16[768,512]{1,0:T(8,128)(2,1)S(1)}, u32[]{:S(2)}) copy-start(bf16[768,512]{1,0:T(8,128)(2,1)S(1)} %collective-permute-done.18.refs_1_) | copy-start | bytes 2359300
  76.7 35.2 %collective-permute-start.29 = (bf16[1024,640]{1,0:T(8,128)(2,1)}, bf16[1024,640]{1,0:T(8,128)(2,1)}, u32[]{:S(2)}, u32[]{:S(2)}) collective-permute-start(bf16[1024,640]{1,0:T(8,128)(2,1)} %collective-permute-done.20.refs_12_), channel_id=1, source_target_pairs={{1,0},{5,4},{9,8},{13,12},{17,16},{21,20},{25,24},{29,28}} | collective-permute-start | bytes 3932168 | tf_op jit(solution)/shard_map/ppermute | solution.py:166
  78.0 33.9 %collective-permute-start.30 = (bf16[1024,640]{1,0:T(8,128)(2,1)}, bf16[1024,640]{1,0:T(8,128)(2,1)}, u32[]{:S(2)}, u32[]{:S(2)}) collective-permute-start(bf16[1024,640]{1,0:T(8,128)(2,1)} %collective-permute-done.19.refs_16_), channel_id=1, source_target_pairs={{2,3},{6,7},{10,11},{14,15},{18,19},{22,23},{26,27},{30,31}} | collective-permute-start | bytes 3932168 | tf_op jit(solution)/shard_map/ppermute | solution.py:166
  93.1 18.8 %copy-start.3 = (bf16[768,512]{1,0:T(8,128)(2,1)}, bf16[768,512]{1,0:T(8,128)(2,1)S(1)}, u32[]{:S(2)}) copy-start(bf16[768,512]{1,0:T(8,128)(2,1)S(1)} %collective-permute-done.21.refs_2_) | copy-start | bytes 2359300
  93.2 10.5 %collective-permute-start.25 = (bf16[384,512]{1,0:T(8,128)(2,1)S(1)}, bf16[384,512]{1,0:T(8,128)(2,1)S(1)}, u32[]{:S(2)}, u32[]{:S(2)}) collective-permute-start(bf16[384,512]{1,0:T(8,128)(2,1)S(1)} %slice.16), channel_id=1, source_target_pairs={{0,16},{4,20},{8,24},{12,28},{16,0},{20,4},{24,8},{28,12},{1,17},{... | collective-permute-start | bytes 1179656 | tf_op jit(solution)/shard_map/ppermute | solution.py:48
  94.8 11.7 %collective-permute-start.22 = (bf16[768,512]{1,0:T(8,128)(2,1)S(1)}, bf16[768,512]{1,0:T(8,128)(2,1)S(1)}, u32[]{:S(2)}, u32[]{:S(2)}) collective-permute-start(bf16[768,512]{1,0:T(8,128)(2,1)S(1)} %collective-permute-done.21.refs_2_), channel_id=1, source_target_pairs={{0,4},{4,0},{8,12},{12,8},{16,20},{20,16},{24,28},{28,24},{1,5},{5... | collective-permute-start | bytes 2359304 | tf_op jit(solution)/shard_map/ppermute | solution.py:48
  94.8 17.2 %copy-start.4 = (bf16[768,512]{1,0:T(8,128)(2,1)}, bf16[768,512]{1,0:T(8,128)(2,1)S(1)}, u32[]{:S(2)}) copy-start(bf16[768,512]{1,0:T(8,128)(2,1)S(1)} %collective-permute-done.23.refs_4_) | copy-start | bytes 2359300
  94.8 11.7 %collective-permute-start.26 = (bf16[384,512]{1,0:T(8,128)(2,1)S(1)}, bf16[384,512]{1,0:T(8,128)(2,1)}, u32[]{:S(2)}, u32[]{:S(2)}) collective-permute-start(bf16[384,512]{1,0:T(8,128)(2,1)S(1)} %slice.17), channel_id=1, source_target_pairs={{0,8},{4,12},{8,0},{12,4},{16,24},{20,28},{24,16},{28,20},{1,9},{5... | collective-permute-start | bytes 1179656 | tf_op jit(solution)/shard_map/ppermute | solution.py:48
  103.6 8.3 %copy-start.9 = (bf16[384,512]{1,0:T(8,128)(2,1)}, bf16[384,512]{1,0:T(8,128)(2,1)S(1)}, u32[]{:S(2)}) copy-start(bf16[384,512]{1,0:T(8,128)(2,1)S(1)} %collective-permute-done.25.refs_6_) | copy-start | bytes 1179652
  103.7 4.3 %collective-permute-start.24 = (bf16[768,512]{1,0:T(8,128)(2,1)S(1)}, bf16[768,512]{1,0:T(8,128)(2,1)}, u32[]{:S(2)}, u32[]{:S(2)}) collective-permute-start(bf16[768,512]{1,0:T(8,128)(2,1)S(1)} %collective-permute-done.23.refs_4_), channel_id=1, source_target_pairs={{0,4},{4,0},{8,12},{12,8},{16,20},{20,16},{24,28},{28,24},{1,5},{5... | collective-permute-start | bytes 2359304 | tf_op jit(solution)/shard_map/ppermute | solution.py:48
  106.5 1.9 %collective-permute-start.27 = (bf16[384,512]{1,0:T(8,128)(2,1)S(1)}, bf16[384,512]{1,0:T(8,128)(2,1)}, u32[]{:S(2)}, u32[]{:S(2)}) collective-permute-start(bf16[384,512]{1,0:T(8,128)(2,1)S(1)} %collective-permute-done.25.refs_6_), channel_id=1, source_target_pairs={{0,4},{4,0},{8,12},{12,8},{16,20},{20,16},{24,28},{28,24},{1,5},{5... | collective-permute-start | bytes 1179656 | tf_op jit(solution)/shard_map/ppermute | solution.py:48
  106.5 0.9 copy-start.8
  106.5 2.6 %collective-permute-start.28 = (bf16[384,512]{1,0:T(8,128)(2,1)}, bf16[384,512]{1,0:T(8,128)(2,1)}, u32[]{:S(2)}, u32[]{:S(2)}) collective-permute-start(bf16[384,512]{1,0:T(8,128)(2,1)} %collective-permute-done.26.refs_7_), channel_id=1, source_target_pairs={{0,4},{4,0},{8,12},{12,8},{16,20},{20,16},{24,28},{28,24},{1,5},{5... | collective-permute-start | bytes 1179656 | tf_op jit(solution)/shard_map/ppermute | solution.py:48
  112.0 30.8 %copy-start.1 = (s32[1,160]{1,0:T(1,128)S(1)}, s32[1,160]{1,0:T(1,128)}, u32[]{:S(2)}) copy-start(s32[1,160]{1,0:T(1,128)} %mask_ref.3) | copy-start | bytes 1924
  120.7 3.6 %collective-permute-start.31 = (bf16[160,640]{1,0:T(8,128)(2,1)}, bf16[160,640]{1,0:T(8,128)(2,1)S(1)}, u32[]{:S(2)}, u32[]{:S(2)}) collective-permute-start(bf16[160,640]{1,0:T(8,128)(2,1)} %get-tuple-element.108), channel_id=1, source_target_pairs={{0,4},{4,0},{8,12},{12,8},{16,20},{20,16},{24,28},{28,24},{1,5},{5... | collective-permute-start | bytes 614408 | tf_op jit(solution)/shard_map/ppermute | solution.py:48
  120.8 8.2 %collective-permute-start.32 = (bf16[160,640]{1,0:T(8,128)(2,1)}, bf16[160,640]{1,0:T(8,128)(2,1)S(1)}, u32[]{:S(2)}, u32[]{:S(2)}) collective-permute-start(bf16[160,640]{1,0:T(8,128)(2,1)} %get-tuple-element.109), channel_id=1, source_target_pairs={{0,8},{4,12},{8,0},{12,4},{16,24},{20,28},{24,16},{28,20},{1,9},{5... | collective-permute-start | bytes 614408 | tf_op jit(solution)/shard_map/ppermute | solution.py:48
  121.6 10.8 %collective-permute-start.33 = (bf16[160,640]{1,0:T(8,128)(2,1)}, bf16[160,640]{1,0:T(8,128)(2,1)S(1)}, u32[]{:S(2)}, u32[]{:S(2)}) collective-permute-start(bf16[160,640]{1,0:T(8,128)(2,1)} %get-tuple-element.110), channel_id=1, source_target_pairs={{0,12},{4,8},{8,4},{12,0},{16,28},{20,24},{24,20},{28,16},{1,13},{... | collective-permute-start | bytes 614408 | tf_op jit(solution)/shard_map/ppermute | solution.py:48
  122.6 9.8 %collective-permute-start.34 = (bf16[160,640]{1,0:T(8,128)(2,1)}, bf16[160,640]{1,0:T(8,128)(2,1)S(1)}, u32[]{:S(2)}, u32[]{:S(2)}) collective-permute-start(bf16[160,640]{1,0:T(8,128)(2,1)} %get-tuple-element.111), channel_id=1, source_target_pairs={{0,16},{4,20},{8,24},{12,28},{16,0},{20,4},{24,8},{28,12},{1,17},{... | collective-permute-start | bytes 614408 | tf_op jit(solution)/shard_map/ppermute | solution.py:48
  124.2 18.6 %collective-permute-start.35 = (bf16[160,640]{1,0:T(8,128)(2,1)}, bf16[160,640]{1,0:T(8,128)(2,1)S(1)}, u32[]{:S(2)}, u32[]{:S(2)}) collective-permute-start(bf16[160,640]{1,0:T(8,128)(2,1)} %get-tuple-element.112), channel_id=1, source_target_pairs={{0,20},{4,16},{8,28},{12,24},{16,4},{20,0},{24,12},{28,8},{1,21},{... | collective-permute-start | bytes 614408 | tf_op jit(solution)/shard_map/ppermute | solution.py:48
  124.3 18.4 %collective-permute-start.36 = (bf16[160,640]{1,0:T(8,128)(2,1)}, bf16[160,640]{1,0:T(8,128)(2,1)S(1)}, u32[]{:S(2)}, u32[]{:S(2)}) collective-permute-start(bf16[160,640]{1,0:T(8,128)(2,1)} %get-tuple-element.113), channel_id=1, source_target_pairs={{0,24},{4,28},{8,16},{12,20},{16,8},{20,12},{24,0},{28,4},{1,25},{... | collective-permute-start | bytes 614408 | tf_op jit(solution)/shard_map/ppermute | solution.py:48
  128.9 13.8 %collective-permute-start.37 = (bf16[160,640]{1,0:T(8,128)(2,1)}, bf16[160,640]{1,0:T(8,128)(2,1)S(1)}, u32[]{:S(2)}, u32[]{:S(2)}) collective-permute-start(bf16[160,640]{1,0:T(8,128)(2,1)} %get-tuple-element.114), channel_id=1, source_target_pairs={{0,28},{4,24},{8,20},{12,16},{16,12},{20,8},{24,4},{28,0},{1,29},{... | collective-permute-start | bytes 614408 | tf_op jit(solution)/shard_map/ppermute | solution.py:48

commit v4 on v3

--- a/solution.py
+++ b/solution.py
@@ -452,40 +452,21 @@
         return jnp.where(good[:, None], result, jnp.bfloat16(0.0))
 
     def body(place_ref, blocks_ref, mask_ref, *refs):
-        piece_refs, out_ref = refs[:count], refs[count]
-        held, masked, load_sems, store_sems = refs[count + 1 :]
-        loads, stores = [], []
-        for mask in range(count):
-            load = pltpu.make_async_copy(piece_refs[mask], held.at[mask], load_sems.at[mask])
-            load.start()
-            loads.append(load)
+        out_ref = refs[-1]
         good = valid_column(mask_ref, blocks_ref[0, 0]) > 0.5
         for mask in range(count):
-            loads[mask].wait()
-            masked[mask] = jnp.where(good, held[mask], jnp.bfloat16(0.0))
             start = pl.multiple_of((place_ref[0] ^ mask) * columns, HEAD_DIM)
-            store = pltpu.make_async_copy(
-                masked.at[mask], out_ref.at[:, pl.ds(start, columns)], store_sems.at[mask]
+            out_ref[:, pl.ds(start, columns)] = jnp.where(
+                good, refs[mask][...], jnp.bfloat16(0.0)
             )
-            store.start()
-            stores.append(store)
-        for store in stores:
-            store.wait()
-
-    any_spec = pl.BlockSpec(memory_space=pl.ANY)
+
     return pl.pallas_call(
         body,
         grid_spec=pltpu.PrefetchScalarGridSpec(
             num_scalar_prefetch=2,
             grid=(1,),
-            in_specs=[full_spec((1, rows))] + [any_spec] * count,
-            out_specs=any_spec,
-            scratch_shapes=[
-                pltpu.VMEM((count, rows, columns), jnp.bfloat16),
-                pltpu.VMEM((count, rows, columns), jnp.bfloat16),
-                pltpu.SemaphoreType.DMA((count,)),
-                pltpu.SemaphoreType.DMA((count,)),
-            ],
+            in_specs=[full_spec((1, rows))] + [full_spec((rows, columns))] * count,
+            out_specs=full_spec((rows, count * columns)),
         ),
         out_shape=jax.ShapeDtypeStruct((rows, count * columns), jnp.bfloat16),
         compiler_params=params(16),
@@ -511,7 +492,9 @@
 
     shards = {0: cut_weight(place_array, out_weight, count)}
     queries, shards[0] = lax.optimization_barrier((queries, shards[0]))
-    payloads = pack(place_array, block_counts, row_mask, queries, keys, values, count)
+    payloads = list(
+        pack(place_array, block_counts, row_mask, queries, keys, values, count)
+    )
     groups = lax.axis_size("fsdp")
 
     received = [payloads[0]] + [None] * (count - 1)
@@ -520,11 +503,17 @@
     pass_weight(shards, 1)
     for mask in early:
         received[mask] = xor_permute(payloads[mask], mask, count)
-    received, payloads, shards[1], shards[-1] = lax.optimization_barrier(
-        (received, payloads, shards[1], shards[-1])
+    received[early[0]], payloads[late[0]] = lax.optimization_barrier(
+        (received[early[0]], payloads[late[0]])
     )
+    received[late[0]] = xor_permute(payloads[late[0]], late[0], count)
+    gate = [received[mask] for mask in early[1:]]
+    gate, shards[1], shards[-1] = lax.optimization_barrier((gate, shards[1], shards[-1]))
+    for mask, block in zip(early[1:], gate):
+        received[mask] = block
     pass_weight(shards, 2)
-    for mask in late:
+    received[late[0]], payloads = lax.optimization_barrier((received[late[0]], payloads))
+    for mask in late[1:]:
         received[mask] = xor_permute(payloads[mask], mask, count)
     always = total * 3 // 5
     attended, rest, counts, used = attend(

time: 149 us -> 144 us (0.966)
  waiting for transfers between devices: 91.1 us -> 84.1 us
  starting transfers between devices: 30 us -> 32.8 us
    ppermute x23, waiting for transfers between devices: 85.7 us -> 73.7 us  [xor_permute(): lax.ppermute(array, 'cam', [(place, place ^ mask) for place in range(coun...]
    ppermute x6, waiting for transfers between devices: 5.33 us -> 10.5 us  [pass_weight(): lax.ppermute(shards[sign * (distance - 1)], 'fsdp', pairs)]
    ppermute x23, starting transfers between devices: 17.6 us -> 20.3 us  [xor_permute(): lax.ppermute(array, 'cam', [(place, place ^ mask) for place in range(coun...]
  transfers between devices with their start and end apart: 29 -> 29, of which waited for: 15 -> 16; matrix products, arithmetic and copies ran while one was open for 0% -> 0% of each run, Pallas kernels for 6% -> 7%
where the time goes in v4:
time: 144 us; the launch traced here: 143 us
  waiting for transfers between devices  84.1 us (58%)
  starting transfers between devices  32.8 us (23%)
  Pallas kernels  24 us (17%)
    ppermute x23, waiting for transfers between devices, xor_permute(): lax.ppermute(array, 'cam', [(place, place ^ mask) for place in range(coun...  73.7 us
    ppermute x23, starting transfers between devices, xor_permute(): lax.ppermute(array, 'cam', [(place, place ^ mask) for place in range(coun...  20.3 us
    ppermute x6, starting transfers between devices, pass_weight(): lax.ppermute(shards[sign * (distance - 1)], 'fsdp', pairs)  12.4 us
    ppermute x6, waiting for transfers between devices, pass_weight(): lax.ppermute(shards[sign * (distance - 1)], 'fsdp', pairs)  10.5 us
    pallas_call x1, Pallas kernels, project(): pl.pallas_call(body, grid_spec=pltpu.PrefetchScalarGridSpec(num_scalar_pr...  9.59 us
    pallas_call x1, Pallas kernels, attend(): pl.pallas_call(body, grid_spec=pltpu.PrefetchScalarGridSpec(num_scalar_pr...  5.69 us
    pallas_call x1, Pallas kernels, pack(): pl.pallas_call(body, grid_spec=pltpu.PrefetchScalarGridSpec(num_scalar_pr...  4.19 us
  transfers between devices with their start and end apart: 29, of which 16 were waited for; matrix products, arithmetic and copies ran while one was open for 0% of the time, Pallas kernels for 7%

profile of v4, /device:TPU:0, one launch (start us, length us, event | category | flops | bytes accessed | tf_op | source)
XLA Modules:
  0.0 142.7 jit_solution(1261849816202525739)
XLA Ops:
  0.0 2.1 %cut_weight.1.refs_14_ = bf16[1024,640]{1,0:T(8,128)(2,1)} custom-call(s32[1]{0:T(128)} %bitcast.8.place_ref, bf16[1024,5120]{1,0:T(8,128)(2,1)} %w_ref.1), custom_call_target="tpu_custom_call" | custom-call | bytes 2621440 | tf_op jit(solution)/shard_map/cut_weight/pallas_call | solution.py:78
  2.1 5.0 %collective-permute-start.14 = (bf16[1024,640]{1,0:T(8,128)(2,1)}, bf16[1024,640]{1,0:T(8,128)(2,1)S(1)}, u32[]{:S(2)}, u32[]{:S(2)}) collective-permute-start(bf16[1024,640]{1,0:T(8,128)(2,1)} %cut_weight.1.refs_14_), channel_id=1, source_target_pairs={{0,1},{1,2},{2,3},{4,5},{5,6},{6,7},{8,9},{9,10},{10,11},{12,13},{... | collective-permute-start | bytes 3932168 | tf_op jit(solution)/shard_map/ppermute | solution.py:166
  7.1 1.3 collective-permute-start.15
  9.1 4.2 %pack.1 = (bf16[3,160,512]{2,1,0:T(8,128)(2,1)}, bf16[3,160,512]{2,1,0:T(8,128)(2,1)}, bf16[3,160,512]{2,1,0:T(8,128)(2,1)}, bf16[3,160,512]{2,1,0:T(8,128)(2,1)...) custom-call(s32[1]{0:T(128)} %bitcast.8.place_ref, ...), custom_call_target="tpu_custom_call" | custom-call | bytes 7864320 | tf_op jit(solution)/shard_map/pack/pallas_call | solution.py:135
  13.3 2.5 %collective-permute-start.9 = (bf16[3,160,512]{2,1,0:T(8,128)(2,1)}, bf16[3,160,512]{2,1,0:T(8,128)(2,1)S(1)}, u32[]{:S(2)}, u32[]{:S(2)}) collective-permute-start(bf16[3,160,512]{2,1,0:T(8,128)(2,1)} %get-tuple-element.64), channel_id=1, source_target_pairs={{0,24},{4,28},{8,16},{12,20},{16,8},{20,12},{24,0},{28,4},{1,25},{... | collective-permute-start | bytes 1474568 | tf_op jit(solution)/shard_map/ppermute | solution.py:48
  15.8 0.5 collective-permute-start.12
  16.3 0.5 collective-permute-start.13
  16.8 11.8 %collective-permute-done.9.refs_6_ = bf16[3,160,512]{2,1,0:T(8,128)(2,1)S(1)} collective-permute-done((bf16[3,160,512]{2,1,0:T(8,128)(2,1)}, bf16[3,160,512]{2,1,0:T(8,128)(2,1)S(1)}, u32[]{:S(2)}, u32[]{:S(2)}) %collective-permute-start.9) | collective-permute-done | bytes 491552 | tf_op jit(solution)/shard_map/ppermute | solution.py:48
  28.6 10.6 %collective-permute-done.12.refs_2_ = bf16[3,160,512]{2,1,0:T(8,128)(2,1)S(1)} collective-permute-done((bf16[3,160,512]{2,1,0:T(8,128)(2,1)}, bf16[3,160,512]{2,1,0:T(8,128)(2,1)S(1)}, u32[]{:S(2)}, u32[]{:S(2)}) %collective-permute-start.12) | collective-permute-done | bytes 491552 | tf_op jit(solution)/shard_map/ppermute | solution.py:48
  39.2 0.2 collective-permute-done.15.refs_13_
  39.5 1.8 %collective-permute-start.19 = (bf16[1024,640]{1,0:T(8,128)(2,1)S(1)}, bf16[1024,640]{1,0:T(8,128)(2,1)}, u32[]{:S(2)}, u32[]{:S(2)}) collective-permute-start(bf16[1024,640]{1,0:T(8,128)(2,1)S(1)} %collective-permute-done.14.refs_15_), channel_id=1, source_target_pairs={{1,2},{2,3},{5,6},{6,7},{9,10},{10,11},{13,14},{14,15},{17,18},{18... | collective-permute-start | bytes 3932168 | tf_op jit(solution)/shard_map/ppermute | solution.py:166
  41.2 1.3 collective-permute-start.20
  42.5 4.9 %collective-permute-done.10.refs_7_ = bf16[3,160,512]{2,1,0:T(8,128)(2,1)S(1)} collective-permute-done((bf16[3,160,512]{2,1,0:T(8,128)(2,1)}, bf16[3,160,512]{2,1,0:T(8,128)(2,1)S(1)}, u32[]{:S(2)}, u32[]{:S(2)}) %collective-permute-start.10) | collective-permute-done | bytes 491552 | tf_op jit(solution)/shard_map/ppermute | solution.py:48
  47.4 0.6 collective-permute-start.11
  48.0 1.1 collective-permute-start.16
  49.1 1.6 %collective-permute-start.17 = (bf16[3,160,512]{2,1,0:T(8,128)(2,1)}, bf16[3,160,512]{2,1,0:T(8,128)(2,1)S(1)}, u32[]{:S(2)}, u32[]{:S(2)}) collective-permute-start(bf16[3,160,512]{2,1,0:T(8,128)(2,1)} %get-tuple-element.77), channel_id=1, source_target_pairs={{0,20},{4,16},{8,28},{12,24},{16,4},{20,0},{24,12},{28,8},{1,21},{... | collective-permute-start | bytes 1474568 | tf_op jit(solution)/shard_map/ppermute | solution.py:48
  50.8 10.8 %collective-permute-done.16.refs_3_ = bf16[3,160,512]{2,1,0:T(8,128)(2,1)S(1)} collective-permute-done((bf16[3,160,512]{2,1,0:T(8,128)(2,1)}, bf16[3,160,512]{2,1,0:T(8,128)(2,1)S(1)}, u32[]{:S(2)}, u32[]{:S(2)}) %collective-permute-start.16) | collective-permute-done | bytes 491552 | tf_op jit(solution)/shard_map/ppermute | solution.py:48
  61.6 0.6 collective-permute-done.17.refs_5_
  62.2 5.7 %attend.1 = (bf16[768,512]{1,0:T(8,128)(2,1)S(1)}, bf16[512,512]{1,0:T(8,128)(2,1)}, s32[8]{0:T(128)S(1)}, s32[1]{0:T(128)}) custom-call(s32[1]{0:T(128)} %bitcast.8.place_ref, bf16[3,160,512]{2,1,0:T(8,128)(2,1)} %get-tuple-element.63.refs_0_, bf16[3,160,512]{2,1,0:T(8,128)(2,1)S(1)} %collective-permute-done.11.refs_1_, ...), custom_call_target="tpu_custom_call" | custom-call | flops 134217728 | bytes 655360 | tf_op jit(solution)/shard_map/attend/pallas_call | solution.py:275
  67.9 0.9 collective-permute-start.18
  68.8 0.5 collective-permute-start.21
  69.4 1.5 %collective-permute-start.23 = (bf16[768,512]{1,0:T(8,128)(2,1)S(1)}, bf16[768,512]{1,0:T(8,128)(2,1)S(1)}, u32[]{:S(2)}, u32[]{:S(2)}) collective-permute-start(bf16[768,512]{1,0:T(8,128)(2,1)S(1)} %get-tuple-element.88.refs_0_), channel_id=1, source_target_pairs={{0,16},{4,20},{8,24},{12,28},{16,0},{20,4},{24,8},{28,12},{1,17},{... | collective-permute-start | bytes 2359304 | tf_op jit(solution)/shard_map/ppermute | solution.py:48
  70.9 6.0 %collective-permute-done.20.refs_12_ = bf16[1024,640]{1,0:T(8,128)(2,1)} collective-permute-done((bf16[1024,640]{1,0:T(8,128)(2,1)S(1)}, bf16[1024,640]{1,0:T(8,128)(2,1)}, u32[]{:S(2)}, u32[]{:S(2)}) %collective-permute-start.20) | collective-permute-done | bytes 1310752 | tf_op jit(solution)/shard_map/ppermute | solution.py:166
  76.9 1.3 collective-permute-start.29
  78.1 1.8 %collective-permute-start.30 = (bf16[1024,640]{1,0:T(8,128)(2,1)}, bf16[1024,640]{1,0:T(8,128)(2,1)}, u32[]{:S(2)}, u32[]{:S(2)}) collective-permute-start(bf16[1024,640]{1,0:T(8,128)(2,1)} %collective-permute-done.19.refs_16_), channel_id=1, source_target_pairs={{2,3},{6,7},{10,11},{14,15},{18,19},{22,23},{26,27},{30,31}} | collective-permute-start | bytes 3932168 | tf_op jit(solution)/shard_map/ppermute | solution.py:166
  79.9 8.4 %collective-permute-done.21.refs_2_ = bf16[768,512]{1,0:T(8,128)(2,1)S(1)} collective-permute-done((bf16[768,512]{1,0:T(8,128)(2,1)S(1)}, bf16[768,512]{1,0:T(8,128)(2,1)S(1)}, u32[]{:S(2)}, u32[]{:S(2)}) %collective-permute-start.21) | collective-permute-done | bytes 786464 | tf_op jit(solution)/shard_map/ppermute | solution.py:48
  88.4 1.6 %collective-permute-start.25 = (bf16[384,512]{1,0:T(8,128)(2,1)S(1)}, bf16[384,512]{1,0:T(8,128)(2,1)S(1)}, u32[]{:S(2)}, u32[]{:S(2)}) collective-permute-start(bf16[384,512]{1,0:T(8,128)(2,1)S(1)} %slice.16), channel_id=1, source_target_pairs={{0,16},{4,20},{8,24},{12,28},{16,0},{20,4},{24,8},{28,12},{1,17},{... | collective-permute-start | bytes 1179656 | tf_op jit(solution)/shard_map/ppermute | solution.py:48
  90.0 0.6 collective-permute-start.26
  90.6 8.2 %collective-permute-done.25.refs_6_ = bf16[384,512]{1,0:T(8,128)(2,1)S(1)} collective-permute-done((bf16[384,512]{1,0:T(8,128)(2,1)S(1)}, bf16[384,512]{1,0:T(8,128)(2,1)S(1)}, u32[]{:S(2)}, u32[]{:S(2)}) %collective-permute-start.25) | collective-permute-done | bytes 393248 | tf_op jit(solution)/shard_map/ppermute | solution.py:48
  98.8 2.9 %collective-permute-done.26.refs_7_ = bf16[384,512]{1,0:T(8,128)(2,1)} collective-permute-done((bf16[384,512]{1,0:T(8,128)(2,1)S(1)}, bf16[384,512]{1,0:T(8,128)(2,1)}, u32[]{:S(2)}, u32[]{:S(2)}) %collective-permute-start.26) | collective-permute-done | bytes 393248 | tf_op jit(solution)/shard_map/ppermute | solution.py:48
  101.7 0.6 collective-permute-start.28
  102.3 0.3 copy-done.8
  103.2 0.4 collective-permute-done.27.refs_8_
  103.6 0.8 collective-permute-done.28.refs_9_
  104.3 4.3 %collective-permute-done.29.refs_11_ = bf16[1024,640]{1,0:T(8,128)(2,1)} collective-permute-done((bf16[1024,640]{1,0:T(8,128)(2,1)}, bf16[1024,640]{1,0:T(8,128)(2,1)}, u32[]{:S(2)}, u32[]{:S(2)}) %collective-permute-start.29) | collective-permute-done | bytes 1310752 | tf_op jit(solution)/shard_map/ppermute | solution.py:166
  108.7 0.0 copy-start.1
  108.7 9.6 %project.1 = (bf16[160,640]{1,0:T(8,128)(2,1)}, bf16[160,640]{1,0:T(8,128)(2,1)}, bf16[160,640]{1,0:T(8,128)(2,1)}, bf16[160,640]{1,0:T(8,128)(2,1)}, bf16[160,6...) custom-call(s32[1]{0:T(128)} %bitcast.8.place_ref, ...), custom_call_target="tpu_custom_call" | custom-call | flops 3355443200 | bytes 5242880 | tf_op jit(solution)/shard_map/project/pallas_call | solution.py:419
  118.3 0.1 collective-permute-start.31
  118.4 1.6 %collective-permute-start.32 = (bf16[160,640]{1,0:T(8,128)(2,1)}, bf16[160,640]{1,0:T(8,128)(2,1)S(1)}, u32[]{:S(2)}, u32[]{:S(2)}) collective-permute-start(bf16[160,640]{1,0:T(8,128)(2,1)} %get-tuple-element.109), channel_id=1, source_target_pairs={{0,8},{4,12},{8,0},{12,4},{16,24},{20,28},{24,16},{28,20},{1,9},{5... | collective-permute-start | bytes 614408 | tf_op jit(solution)/shard_map/ppermute | solution.py:48
  119.9 0.3 collective-permute-start.33
  120.2 1.7 %collective-permute-start.34 = (bf16[160,640]{1,0:T(8,128)(2,1)}, bf16[160,640]{1,0:T(8,128)(2,1)S(1)}, u32[]{:S(2)}, u32[]{:S(2)}) collective-permute-start(bf16[160,640]{1,0:T(8,128)(2,1)} %get-tuple-element.111), channel_id=1, source_target_pairs={{0,16},{4,20},{8,24},{12,28},{16,0},{20,4},{24,8},{28,12},{1,17},{... | collective-permute-start | bytes 614408 | tf_op jit(solution)/shard_map/ppermute | solution.py:48
  121.9 0.0 collective-permute-start.35
  122.0 2.6 %collective-permute-start.36 = (bf16[160,640]{1,0:T(8,128)(2,1)}, bf16[160,640]{1,0:T(8,128)(2,1)S(1)}, u32[]{:S(2)}, u32[]{:S(2)}) collective-permute-start(bf16[160,640]{1,0:T(8,128)(2,1)} %get-tuple-element.113), channel_id=1, source_target_pairs={{0,24},{4,28},{8,16},{12,20},{16,8},{20,12},{24,0},{28,4},{1,25},{... | collective-permute-start | bytes 614408 | tf_op jit(solution)/shard_map/ppermute | solution.py:48
  124.6 2.0 %collective-permute-done.32.refs_2_ = bf16[160,640]{1,0:T(8,128)(2,1)S(1)} collective-permute-done((bf16[160,640]{1,0:T(8,128)(2,1)}, bf16[160,640]{1,0:T(8,128)(2,1)S(1)}, u32[]{:S(2)}, u32[]{:S(2)}) %collective-permute-start.32) | collective-permute-done | bytes 204832 | tf_op jit(solution)/shard_map/ppermute | solution.py:48
  126.5 1.4 %collective-permute-start.37 = (bf16[160,640]{1,0:T(8,128)(2,1)}, bf16[160,640]{1,0:T(8,128)(2,1)S(1)}, u32[]{:S(2)}, u32[]{:S(2)}) collective-permute-start(bf16[160,640]{1,0:T(8,128)(2,1)} %get-tuple-element.114), channel_id=1, source_target_pairs={{0,28},{4,24},{8,20},{12,16},{16,12},{20,8},{24,4},{28,0},{1,29},{... | collective-permute-start | bytes 614408 | tf_op jit(solution)/shard_map/ppermute | solution.py:48
  128.0 2.1 %collective-permute-done.33.refs_3_ = bf16[160,640]{1,0:T(8,128)(2,1)S(1)} collective-permute-done((bf16[160,640]{1,0:T(8,128)(2,1)}, bf16[160,640]{1,0:T(8,128)(2,1)S(1)}, u32[]{:S(2)}, u32[]{:S(2)}) %collective-permute-start.33) | collective-permute-done | bytes 204832 | tf_op jit(solution)/shard_map/ppermute | solution.py:48
  130.0 10.2 %collective-permute-done.35.refs_5_ = bf16[160,640]{1,0:T(8,128)(2,1)S(1)} collective-permute-done((bf16[160,640]{1,0:T(8,128)(2,1)}, bf16[160,640]{1,0:T(8,128)(2,1)S(1)}, u32[]{:S(2)}, u32[]{:S(2)}) %collective-permute-start.35) | collective-permute-done | bytes 204832 | tf_op jit(solution)/shard_map/ppermute | solution.py:48
  140.3 2.4 %assemble.1 = bf16[160,5120]{1,0:T(8,128)(2,1)} custom-call(s32[1]{0:T(128)} %bitcast.8.place_ref, s32[1,1]{1,0:T(1,128)S(6)} %copy.16.blocks_ref, s32[1,160]{1,0:T(1,128)S(1)} %copy-done.1, bf16[160,640]{1,0:T(8,128)(2,1)} %get-tuple-element.107.refs_0_, bf16[160,640]{1,0:T(8,128)(2,1)S(1)} %collective-permute-done.31.refs_1_, ...), custom_call_target="tpu_custom_call" | custom-call | bytes 3276800 | tf_op jit(solution)/shard_map/assemble/pallas_call | solution.py:463
  (39 shorter events, 0.2 us)
Async XLA Ops:
  2.1 37.1 %collective-permute-start.14 = (bf16[1024,640]{1,0:T(8,128)(2,1)}, bf16[1024,640]{1,0:T(8,128)(2,1)S(1)}, u32[]{:S(2)}, u32[]{:S(2)}) collective-permute-start(bf16[1024,640]{1,0:T(8,128)(2,1)} %cut_weight.1.refs_14_), channel_id=1, source_target_pairs={{0,1},{1,2},{2,3},{4,5},{5,6},{6,7},{8,9},{9,10},{10,11},{12,13},{... | collective-permute-start | bytes 3932168 | tf_op jit(solution)/shard_map/ppermute | solution.py:166
  7.1 32.3 %collective-permute-start.15 = (bf16[1024,640]{1,0:T(8,128)(2,1)}, bf16[1024,640]{1,0:T(8,128)(2,1)S(1)}, u32[]{:S(2)}, u32[]{:S(2)}) collective-permute-start(bf16[1024,640]{1,0:T(8,128)(2,1)} %cut_weight.1.refs_14_), channel_id=1, source_target_pairs={{1,0},{2,1},{3,2},{5,4},{6,5},{7,6},{9,8},{10,9},{11,10},{13,12},{... | collective-permute-start | bytes 3932168 | tf_op jit(solution)/shard_map/ppermute | solution.py:166
  13.3 15.4 %collective-permute-start.9 = (bf16[3,160,512]{2,1,0:T(8,128)(2,1)}, bf16[3,160,512]{2,1,0:T(8,128)(2,1)S(1)}, u32[]{:S(2)}, u32[]{:S(2)}) collective-permute-start(bf16[3,160,512]{2,1,0:T(8,128)(2,1)} %get-tuple-element.64), channel_id=1, source_target_pairs={{0,24},{4,28},{8,16},{12,20},{16,8},{20,12},{24,0},{28,4},{1,25},{... | collective-permute-start | bytes 1474568 | tf_op jit(solution)/shard_map/ppermute | solution.py:48
  15.8 23.4 %collective-permute-start.12 = (bf16[3,160,512]{2,1,0:T(8,128)(2,1)}, bf16[3,160,512]{2,1,0:T(8,128)(2,1)S(1)}, u32[]{:S(2)}, u32[]{:S(2)}) collective-permute-start(bf16[3,160,512]{2,1,0:T(8,128)(2,1)} %get-tuple-element.68), channel_id=1, source_target_pairs={{0,8},{4,12},{8,0},{12,4},{16,24},{20,28},{24,16},{28,20},{1,9},{5... | collective-permute-start | bytes 1474568 | tf_op jit(solution)/shard_map/ppermute | solution.py:48
  16.3 22.9 %collective-permute-start.13 = (bf16[3,160,512]{2,1,0:T(8,128)(2,1)}, bf16[3,160,512]{2,1,0:T(8,128)(2,1)S(1)}, u32[]{:S(2)}, u32[]{:S(2)}) collective-permute-start(bf16[3,160,512]{2,1,0:T(8,128)(2,1)} %get-tuple-element.70), channel_id=1, source_target_pairs={{0,16},{4,20},{8,24},{12,28},{16,0},{20,4},{24,8},{28,12},{1,17},{... | collective-permute-start | bytes 1474568 | tf_op jit(solution)/shard_map/ppermute | solution.py:48
  28.6 18.8 %collective-permute-start.10 = (bf16[3,160,512]{2,1,0:T(8,128)(2,1)}, bf16[3,160,512]{2,1,0:T(8,128)(2,1)S(1)}, u32[]{:S(2)}, u32[]{:S(2)}) collective-permute-start(bf16[3,160,512]{2,1,0:T(8,128)(2,1)} %get-tuple-element.66), channel_id=1, source_target_pairs={{0,28},{4,24},{8,20},{12,16},{16,12},{20,8},{24,4},{28,0},{1,29},{... | collective-permute-start | bytes 1474568 | tf_op jit(solution)/shard_map/ppermute | solution.py:48
  39.2 62.5 %copy-start.5 = (bf16[1024,640]{1,0:T(8,128)(2,1)}, bf16[1024,640]{1,0:T(8,128)(2,1)S(1)}, u32[]{:S(2)}) copy-start(bf16[1024,640]{1,0:T(8,128)(2,1)S(1)} %collective-permute-done.14.refs_15_) | copy-start | bytes 3932164
  39.5 62.8 %copy-start.6 = (bf16[1024,640]{1,0:T(8,128)(2,1)}, bf16[1024,640]{1,0:T(8,128)(2,1)S(1)}, u32[]{:S(2)}) copy-start(bf16[1024,640]{1,0:T(8,128)(2,1)S(1)} %collective-permute-done.15.refs_13_) | copy-start | bytes 3932164
  39.5 31.4 %collective-permute-start.19 = (bf16[1024,640]{1,0:T(8,128)(2,1)S(1)}, bf16[1024,640]{1,0:T(8,128)(2,1)}, u32[]{:S(2)}, u32[]{:S(2)}) collective-permute-start(bf16[1024,640]{1,0:T(8,128)(2,1)S(1)} %collective-permute-done.14.refs_15_), channel_id=1, source_target_pairs={{1,2},{2,3},{5,6},{6,7},{9,10},{10,11},{13,14},{14,15},{17,18},{18... | collective-permute-start | bytes 3932168 | tf_op jit(solution)/shard_map/ppermute | solution.py:166
  41.2 35.6 %collective-permute-start.20 = (bf16[1024,640]{1,0:T(8,128)(2,1)S(1)}, bf16[1024,640]{1,0:T(8,128)(2,1)}, u32[]{:S(2)}, u32[]{:S(2)}) collective-permute-start(bf16[1024,640]{1,0:T(8,128)(2,1)S(1)} %collective-permute-done.15.refs_13_), channel_id=1, source_target_pairs={{1,0},{2,1},{5,4},{6,5},{9,8},{10,9},{13,12},{14,13},{17,16},{18,1... | collective-permute-start | bytes 3932168 | tf_op jit(solution)/shard_map/ppermute | solution.py:166
  47.4 3.4 %collective-permute-start.11 = (bf16[3,160,512]{2,1,0:T(8,128)(2,1)}, bf16[3,160,512]{2,1,0:T(8,128)(2,1)S(1)}, u32[]{:S(2)}, u32[]{:S(2)}) collective-permute-start(bf16[3,160,512]{2,1,0:T(8,128)(2,1)} %get-tuple-element.72), channel_id=1, source_target_pairs={{0,4},{4,0},{8,12},{12,8},{16,20},{20,16},{24,28},{28,24},{1,5},{5... | collective-permute-start | bytes 1474568 | tf_op jit(solution)/shard_map/ppermute | solution.py:48
  48.0 13.5 %collective-permute-start.16 = (bf16[3,160,512]{2,1,0:T(8,128)(2,1)}, bf16[3,160,512]{2,1,0:T(8,128)(2,1)S(1)}, u32[]{:S(2)}, u32[]{:S(2)}) collective-permute-start(bf16[3,160,512]{2,1,0:T(8,128)(2,1)} %get-tuple-element.75), channel_id=1, source_target_pairs={{0,12},{4,8},{8,4},{12,0},{16,28},{20,24},{24,20},{28,16},{1,13},{... | collective-permute-start | bytes 1474568 | tf_op jit(solution)/shard_map/ppermute | solution.py:48
  49.1 13.1 %collective-permute-start.17 = (bf16[3,160,512]{2,1,0:T(8,128)(2,1)}, bf16[3,160,512]{2,1,0:T(8,128)(2,1)S(1)}, u32[]{:S(2)}, u32[]{:S(2)}) collective-permute-start(bf16[3,160,512]{2,1,0:T(8,128)(2,1)} %get-tuple-element.77), channel_id=1, source_target_pairs={{0,20},{4,16},{8,28},{12,24},{16,4},{20,0},{24,12},{28,8},{1,21},{... | collective-permute-start | bytes 1474568 | tf_op jit(solution)/shard_map/ppermute | solution.py:48
  67.9 22.1 %copy-start.2 = (s32[8]{0:T(128)}, s32[8]{0:T(128)S(1)}, u32[]{:S(2)}) copy-start(s32[8]{0:T(128)S(1)} %get-tuple-element.80.counts_ref) | copy-start | bytes 100
  67.9 40.7 %copy-start = (bf16[768,512]{1,0:T(8,128)(2,1)}, bf16[768,512]{1,0:T(8,128)(2,1)S(1)}, u32[]{:S(2)}) copy-start(bf16[768,512]{1,0:T(8,128)(2,1)S(1)} %get-tuple-element.88.refs_0_) | copy-start | bytes 2359300
  67.9 3.0 %collective-permute-start.18 = (bf16[768,512]{1,0:T(8,128)(2,1)S(1)}, bf16[768,512]{1,0:T(8,128)(2,1)S(1)}, u32[]{:S(2)}, u32[]{:S(2)}) collective-permute-start(bf16[768,512]{1,0:T(8,128)(2,1)S(1)} %get-tuple-element.88.refs_0_), channel_id=1, source_target_pairs={{0,4},{4,0},{8,12},{12,8},{16,20},{20,16},{24,28},{28,24},{1,5},{5... | collective-permute-start | bytes 2359304 | tf_op jit(solution)/shard_map/ppermute | solution.py:48
  68.8 19.5 %collective-permute-start.21 = (bf16[768,512]{1,0:T(8,128)(2,1)S(1)}, bf16[768,512]{1,0:T(8,128)(2,1)S(1)}, u32[]{:S(2)}, u32[]{:S(2)}) collective-permute-start(bf16[768,512]{1,0:T(8,128)(2,1)S(1)} %get-tuple-element.88.refs_0_), channel_id=1, source_target_pairs={{0,8},{4,12},{8,0},{12,4},{16,24},{20,28},{24,16},{28,20},{1,9},{5... | collective-permute-start | bytes 2359304 | tf_op jit(solution)/shard_map/ppermute | solution.py:48
  69.4 20.6 %collective-permute-start.23 = (bf16[768,512]{1,0:T(8,128)(2,1)S(1)}, bf16[768,512]{1,0:T(8,128)(2,1)S(1)}, u32[]{:S(2)}, u32[]{:S(2)}) collective-permute-start(bf16[768,512]{1,0:T(8,128)(2,1)S(1)} %get-tuple-element.88.refs_0_), channel_id=1, source_target_pairs={{0,16},{4,20},{8,24},{12,28},{16,0},{20,4},{24,8},{28,12},{1,17},{... | collective-permute-start | bytes 2359304 | tf_op jit(solution)/shard_map/ppermute | solution.py:48
  70.9 37.7 %copy-start.7 = (bf16[768,512]{1,0:T(8,128)(2,1)}, bf16[768,512]{1,0:T(8,128)(2,1)S(1)}, u32[]{:S(2)}) copy-start(bf16[768,512]{1,0:T(8,128)(2,1)S(1)} %collective-permute-done.18.refs_1_) | copy-start | bytes 2359300
  76.9 31.8 %collective-permute-start.29 = (bf16[1024,640]{1,0:T(8,128)(2,1)}, bf16[1024,640]{1,0:T(8,128)(2,1)}, u32[]{:S(2)}, u32[]{:S(2)}) collective-permute-start(bf16[1024,640]{1,0:T(8,128)(2,1)} %collective-permute-done.20.refs_12_), channel_id=1, source_target_pairs={{1,0},{5,4},{9,8},{13,12},{17,16},{21,20},{25,24},{29,28}} | collective-permute-start | bytes 3932168 | tf_op jit(solution)/shard_map/ppermute | solution.py:166
  78.1 30.5 %collective-permute-start.30 = (bf16[1024,640]{1,0:T(8,128)(2,1)}, bf16[1024,640]{1,0:T(8,128)(2,1)}, u32[]{:S(2)}, u32[]{:S(2)}) collective-permute-start(bf16[1024,640]{1,0:T(8,128)(2,1)} %collective-permute-done.19.refs_16_), channel_id=1, source_target_pairs={{2,3},{6,7},{10,11},{14,15},{18,19},{22,23},{26,27},{30,31}} | collective-permute-start | bytes 3932168 | tf_op jit(solution)/shard_map/ppermute | solution.py:166
  88.4 20.3 %copy-start.3 = (bf16[768,512]{1,0:T(8,128)(2,1)}, bf16[768,512]{1,0:T(8,128)(2,1)S(1)}, u32[]{:S(2)}) copy-start(bf16[768,512]{1,0:T(8,128)(2,1)S(1)} %collective-permute-done.21.refs_2_) | copy-start | bytes 2359300
  88.4 10.4 %collective-permute-start.25 = (bf16[384,512]{1,0:T(8,128)(2,1)S(1)}, bf16[384,512]{1,0:T(8,128)(2,1)S(1)}, u32[]{:S(2)}, u32[]{:S(2)}) collective-permute-start(bf16[384,512]{1,0:T(8,128)(2,1)S(1)} %slice.16), channel_id=1, source_target_pairs={{0,16},{4,20},{8,24},{12,28},{16,0},{20,4},{24,8},{28,12},{1,17},{... | collective-permute-start | bytes 1179656 | tf_op jit(solution)/shard_map/ppermute | solution.py:48
  90.0 11.7 %collective-permute-start.22 = (bf16[768,512]{1,0:T(8,128)(2,1)S(1)}, bf16[768,512]{1,0:T(8,128)(2,1)S(1)}, u32[]{:S(2)}, u32[]{:S(2)}) collective-permute-start(bf16[768,512]{1,0:T(8,128)(2,1)S(1)} %collective-permute-done.21.refs_2_), channel_id=1, source_target_pairs={{0,4},{4,0},{8,12},{12,8},{16,20},{20,16},{24,28},{28,24},{1,5},{5... | collective-permute-start | bytes 2359304 | tf_op jit(solution)/shard_map/ppermute | solution.py:48
  90.0 18.7 %copy-start.4 = (bf16[768,512]{1,0:T(8,128)(2,1)}, bf16[768,512]{1,0:T(8,128)(2,1)S(1)}, u32[]{:S(2)}) copy-start(bf16[768,512]{1,0:T(8,128)(2,1)S(1)} %collective-permute-done.23.refs_4_) | copy-start | bytes 2359300
  90.0 11.7 %collective-permute-start.26 = (bf16[384,512]{1,0:T(8,128)(2,1)S(1)}, bf16[384,512]{1,0:T(8,128)(2,1)}, u32[]{:S(2)}, u32[]{:S(2)}) collective-permute-start(bf16[384,512]{1,0:T(8,128)(2,1)S(1)} %slice.17), channel_id=1, source_target_pairs={{0,8},{4,12},{8,0},{12,4},{16,24},{20,28},{24,16},{28,20},{1,9},{5... | collective-permute-start | bytes 1179656 | tf_op jit(solution)/shard_map/ppermute | solution.py:48
  98.8 9.9 %copy-start.9 = (bf16[384,512]{1,0:T(8,128)(2,1)}, bf16[384,512]{1,0:T(8,128)(2,1)S(1)}, u32[]{:S(2)}) copy-start(bf16[384,512]{1,0:T(8,128)(2,1)S(1)} %collective-permute-done.25.refs_6_) | copy-start | bytes 1179652
  98.8 4.4 %collective-permute-start.24 = (bf16[768,512]{1,0:T(8,128)(2,1)S(1)}, bf16[768,512]{1,0:T(8,128)(2,1)}, u32[]{:S(2)}, u32[]{:S(2)}) collective-permute-start(bf16[768,512]{1,0:T(8,128)(2,1)S(1)} %collective-permute-done.23.refs_4_), channel_id=1, source_target_pairs={{0,4},{4,0},{8,12},{12,8},{16,20},{20,16},{24,28},{28,24},{1,5},{5... | collective-permute-start | bytes 2359304 | tf_op jit(solution)/shard_map/ppermute | solution.py:48
  101.7 1.9 %collective-permute-start.27 = (bf16[384,512]{1,0:T(8,128)(2,1)S(1)}, bf16[384,512]{1,0:T(8,128)(2,1)}, u32[]{:S(2)}, u32[]{:S(2)}) collective-permute-start(bf16[384,512]{1,0:T(8,128)(2,1)S(1)} %collective-permute-done.25.refs_6_), channel_id=1, source_target_pairs={{0,4},{4,0},{8,12},{12,8},{16,20},{20,16},{24,28},{28,24},{1,5},{5... | collective-permute-start | bytes 1179656 | tf_op jit(solution)/shard_map/ppermute | solution.py:48
  101.7 0.9 copy-start.8
  101.7 2.6 %collective-permute-start.28 = (bf16[384,512]{1,0:T(8,128)(2,1)}, bf16[384,512]{1,0:T(8,128)(2,1)}, u32[]{:S(2)}, u32[]{:S(2)}) collective-permute-start(bf16[384,512]{1,0:T(8,128)(2,1)} %collective-permute-done.26.refs_7_), channel_id=1, source_target_pairs={{0,4},{4,0},{8,12},{12,8},{16,20},{20,16},{24,28},{28,24},{1,5},{5... | collective-permute-start | bytes 1179656 | tf_op jit(solution)/shard_map/ppermute | solution.py:48
  108.7 31.6 %copy-start.1 = (s32[1,160]{1,0:T(1,128)S(1)}, s32[1,160]{1,0:T(1,128)}, u32[]{:S(2)}) copy-start(s32[1,160]{1,0:T(1,128)} %mask_ref.3) | copy-start | bytes 1924
  118.3 3.7 %collective-permute-start.31 = (bf16[160,640]{1,0:T(8,128)(2,1)}, bf16[160,640]{1,0:T(8,128)(2,1)S(1)}, u32[]{:S(2)}, u32[]{:S(2)}) collective-permute-start(bf16[160,640]{1,0:T(8,128)(2,1)} %get-tuple-element.108), channel_id=1, source_target_pairs={{0,4},{4,0},{8,12},{12,8},{16,20},{20,16},{24,28},{28,24},{1,5},{5... | collective-permute-start | bytes 614408 | tf_op jit(solution)/shard_map/ppermute | solution.py:48
  118.4 8.2 %collective-permute-start.32 = (bf16[160,640]{1,0:T(8,128)(2,1)}, bf16[160,640]{1,0:T(8,128)(2,1)S(1)}, u32[]{:S(2)}, u32[]{:S(2)}) collective-permute-start(bf16[160,640]{1,0:T(8,128)(2,1)} %get-tuple-element.109), channel_id=1, source_target_pairs={{0,8},{4,12},{8,0},{12,4},{16,24},{20,28},{24,16},{28,20},{1,9},{5... | collective-permute-start | bytes 614408 | tf_op jit(solution)/shard_map/ppermute | solution.py:48
  119.9 10.1 %collective-permute-start.33 = (bf16[160,640]{1,0:T(8,128)(2,1)}, bf16[160,640]{1,0:T(8,128)(2,1)S(1)}, u32[]{:S(2)}, u32[]{:S(2)}) collective-permute-start(bf16[160,640]{1,0:T(8,128)(2,1)} %get-tuple-element.110), channel_id=1, source_target_pairs={{0,12},{4,8},{8,4},{12,0},{16,28},{20,24},{24,20},{28,16},{1,13},{... | collective-permute-start | bytes 614408 | tf_op jit(solution)/shard_map/ppermute | solution.py:48
  120.2 9.8 %collective-permute-start.34 = (bf16[160,640]{1,0:T(8,128)(2,1)}, bf16[160,640]{1,0:T(8,128)(2,1)S(1)}, u32[]{:S(2)}, u32[]{:S(2)}) collective-permute-start(bf16[160,640]{1,0:T(8,128)(2,1)} %get-tuple-element.111), channel_id=1, source_target_pairs={{0,16},{4,20},{8,24},{12,28},{16,0},{20,4},{24,8},{28,12},{1,17},{... | collective-permute-start | bytes 614408 | tf_op jit(solution)/shard_map/ppermute | solution.py:48
  121.9 18.3 %collective-permute-start.35 = (bf16[160,640]{1,0:T(8,128)(2,1)}, bf16[160,640]{1,0:T(8,128)(2,1)S(1)}, u32[]{:S(2)}, u32[]{:S(2)}) collective-permute-start(bf16[160,640]{1,0:T(8,128)(2,1)} %get-tuple-element.112), channel_id=1, source_target_pairs={{0,20},{4,16},{8,28},{12,24},{16,4},{20,0},{24,12},{28,8},{1,21},{... | collective-permute-start | bytes 614408 | tf_op jit(solution)/shard_map/ppermute | solution.py:48
  122.0 18.3 %collective-permute-start.36 = (bf16[160,640]{1,0:T(8,128)(2,1)}, bf16[160,640]{1,0:T(8,128)(2,1)S(1)}, u32[]{:S(2)}, u32[]{:S(2)}) collective-permute-start(bf16[160,640]{1,0:T(8,128)(2,1)} %get-tuple-element.113), channel_id=1, source_target_pairs={{0,24},{4,28},{8,16},{12,20},{16,8},{20,12},{24,0},{28,4},{1,25},{... | collective-permute-start | bytes 614408 | tf_op jit(solution)/shard_map/ppermute | solution.py:48
  126.5 13.7 %collective-permute-start.37 = (bf16[160,640]{1,0:T(8,128)(2,1)}, bf16[160,640]{1,0:T(8,128)(2,1)S(1)}, u32[]{:S(2)}, u32[]{:S(2)}) collective-permute-start(bf16[160,640]{1,0:T(8,128)(2,1)} %get-tuple-element.114), channel_id=1, source_target_pairs={{0,28},{4,24},{8,20},{12,16},{16,12},{20,8},{24,4},{28,0},{1,29},{... | collective-permute-start | bytes 614408 | tf_op jit(solution)/shard_map/ppermute | solution.py:48
